TPU v7x, 32 devices: a whole 2x2x4 slice. The times are simulated.
32 devices in a mesh: groups: 2 (over x), hst: 2 (over core), local: 8 (over z, y).
Axes of the slice: x: 2, y: 2, z: 4, core: 2. Of those that a mesh axis runs over, the one named last changes fastest.
Arguments:
- tokens: bfloat16 [4096, 7168], P(('groups', 'hst', 'local')), parts along dimension 0, may hold values from -6 to 6
- expert_ids: int32 [4096, 8], P(('groups', 'hst', 'local')), parts along dimension 0, may hold values from 0 to 255, as said below
- route_weights: float32 [4096, 8], P(('groups', 'hst', 'local')), parts along dimension 0, may hold values from 0.1 to 1
- gate_weight: bfloat16 [7168, 2048], P(None, ('hst', 'local')), may hold values from -0.0625 to 0.0625
- up_weight: bfloat16 [7168, 2048], P(None, ('hst', 'local')), may hold values from -0.0625 to 0.0625
- down_weight: bfloat16 [2048, 7168], P(('hst', 'local')), may hold values from -0.1875 to 0.1875
Outputs:
- routed: bfloat16 [4096, 7168], P(('groups', 'hst', 'local')), parts along dimension 0
There are 2 independent parts, one for each index of `groups`. A program takes and returns all parts, laid end to end along the dimension named above; an argument that names none is the same for every part. Nothing has to cross between parts.
Inputs may be any that keep to these rules, and one draw needn't show every extreme that they name: `expert_ids`: each row names 8 different experts. The experts below 2 are the held ones; of the 128 rows of one device at most 6 name any one held expert. One held expert is named by exactly 6 rows of every device, and every other held expert by up to 6 rows.
All inputs are finite; a program needn't handle non-finite values.
Results may differ from a plain program's by a relative error of at most 0.0057.
Values may be sent and summed in bfloat16 or wider, within the bound.
No kernel may reach another device: no remote copies, remote signals or barrier semaphores. Data moves between devices by JAX's collectives and lax.ppermute only.
A program may use at most 64 MiB of HBM per device.

v0:
```python
import jax
import jax.numpy as jnp
from jax import lax
from jax.sharding import PartitionSpec as P

SPLIT = 8
MOST = 6


def route_table(expert_ids, route_weights, experts_win):
    window = jnp.arange(experts_win, dtype=jnp.int32)
    matched = expert_ids[:, :, None] == window[None, None, :]
    is_hit = jnp.any(matched, axis=1).astype(jnp.int32)
    weight = jnp.sum(jnp.where(matched, route_weights[:, :, None], jnp.float32(0.0)), axis=1)
    position = jnp.cumsum(is_hit, axis=0) - 1
    slot_index = jnp.arange(MOST, dtype=jnp.int32)
    select = (is_hit.T[:, None, :] == 1) & (position.T[:, None, :] == slot_index[None, :, None])
    return (select, weight)


def on_device(tokens, expert_ids, route_weights, gate_weight, up_weight, down_weight):
    host_count = lax.axis_size("hst")
    local_count = lax.axis_size("local")
    per_host = local_count // SPLIT
    experts_win = host_count * per_host
    width = tokens.shape[1]
    select, weight = route_table(expert_ids, route_weights, experts_win)
    outgoing = jnp.einsum(
        "wmt,td->wmd", select.astype(jnp.bfloat16), tokens, preferred_element_type=jnp.float32
    ).astype(jnp.bfloat16)
    slot_weight = jnp.einsum(
        "wmt,tw->wm", select.astype(jnp.float32), weight, precision=lax.Precision.HIGHEST
    )
    host_rows = lax.all_to_all(
        outgoing.reshape(host_count, per_host, MOST, width),
        "hst",
        split_axis=0,
        concat_axis=0,
        tiled=True,
    )
    spread = jnp.repeat(jnp.transpose(host_rows, (1, 0, 2, 3)), SPLIT, axis=0)
    row_block = lax.all_to_all(spread, "local", split_axis=0, concat_axis=0, tiled=True)
    in_shape = row_block.shape
    flattened = row_block.reshape(-1, width)
    gate_sum = jnp.dot(flattened, gate_weight, preferred_element_type=jnp.float32)
    up_sum = jnp.dot(flattened, up_weight, preferred_element_type=jnp.float32)
    hidden = (jax.nn.silu(gate_sum) * up_sum).astype(jnp.bfloat16)
    partial_value = jnp.dot(hidden, down_weight, preferred_element_type=jnp.float32).astype(
        jnp.bfloat16
    )
    partial_value = partial_value.reshape(in_shape)
    returned_rows = lax.all_to_all(partial_value, "local", split_axis=0, concat_axis=0, tiled=True)
    summed = jnp.sum(
        returned_rows.reshape(per_host, SPLIT, host_count, MOST, width).astype(jnp.float32), axis=1
    )
    returned_sums = lax.all_to_all(
        jnp.transpose(summed, (1, 0, 2, 3)), "hst", split_axis=0, concat_axis=0, tiled=True
    )
    combined = returned_sums.reshape(experts_win, MOST, width)
    weighted = combined * slot_weight[:, :, None]
    total = jnp.einsum(
        "wmt,wmd->td", select.astype(jnp.float32), weighted, precision=lax.Precision.HIGHEST
    )
    return total.astype(jnp.bfloat16)


def solution(mesh):
    in_specs = (
        P(("groups", "hst", "local"), None),
        P(("groups", "hst", "local"), None),
        P(("groups", "hst", "local"), None),
        P(None, ("hst", "local")),
        P(None, ("hst", "local")),
        P(("hst", "local"), None),
    )
    out_specs = P(("groups", "hst", "local"), None)
    return jax.shard_map(
        on_device, mesh=mesh, in_specs=in_specs, out_specs=out_specs, check_vma=False
    )
```

profile of v0, /device:TPU:0, one launch (start us, length us, event | category | flops | bytes accessed | tf_op | source)
XLA Modules:
  0.0 108.8 jit_solution(17467729604062168068)
XLA Ops:
  0.0 0.0 copy-start
  0.0 0.8 fusion.11
  0.9 0.1 copy.34
  1.0 0.2 reduce_window_sum.11
  1.1 0.1 copy.35
  1.2 1.9 %fusion.1 = bf16[2,1,6,7168]{3,2,1,0:T(8,128)(2,1)S(1)} fusion(bf16[128,7168]{1,0:T(8,128)(2,1)} %param.6, s32[2,128]{1,0:T(2,128)S(1)} %copy.35, pred[2,128]{1,0:T(4,128)(4,1)S(1)} %get-tuple-element.5), kind=kOutput, calls=%fused_computation.4 | convolution fusion | flops 22109184 | bytes 2008320 | tf_op jit(solution)/shard_map/wmt,td->wmd/dot_general | solution.py:28
  3.1 3.9 %all_to_all.20 = bf16[2,1,6,7168]{3,2,1,0:T(8,128)(2,1)S(1)} all-to-all(bf16[2,1,6,7168]{3,2,1,0:T(8,128)(2,1)S(1)} %fusion.1), channel_id=1, replica_groups=mesh['groups'=2,'hst'=2,'local'=8] {'hst'}, dimensions={0} | all-to-all | bytes 344064 | tf_op jit(solution)/shard_map/all_to_all | solution.py:34
  7.0 0.2 copy.37
  7.2 0.7 reshape.28
  7.9 40.8 %all_to_all.21 = bf16[8,2,6,7168]{3,1,2,0:T(2,128)(2,1)S(1)} all-to-all(bf16[8,2,6,7168]{3,1,2,0:T(2,128)(2,1)S(1)} %reshape.28), channel_id=1, replica_groups=mesh['groups'=2,'hst'=2,'local'=8] {'local'}, dimensions={0} | all-to-all | bytes 2752512 | tf_op jit(solution)/shard_map/all_to_all | solution.py:42
  48.7 1.6 %copy.38 = bf16[8,2,6,7168]{3,2,1,0:T(8,128)(2,1)} copy(bf16[8,2,6,7168]{3,1,2,0:T(2,128)(2,1)S(1)} %all_to_all.21) | data formatting | bytes 2752512 | tf_op jit(solution)/shard_map/all_to_all | solution.py:42
  50.2 1.7 %reshape.29 = bf16[96,7168]{1,0:T(8,128)(2,1)S(1)} reshape(bf16[8,2,6,7168]{3,2,1,0:T(8,128)(2,1)} %copy.38) | data formatting | bytes 2752512 | tf_op jit(solution)/shard_map/reshape | solution.py:44
  52.0 2.0 %fusion.24 = f32[96,128]{1,0:T(8,128)S(1)} fusion(bf16[96,7168]{1,0:T(8,128)(2,1)S(1)} %reshape.29, bf16[7168,128]{1,0:T(8,128)(2,1)} %param.9), kind=kOutput, calls=%fused_computation.32 | convolution fusion | flops 176160768 | bytes 3260416 | tf_op jit(solution)/shard_map/dot_general | solution.py:45
  54.0 0.0 copy-done
  54.0 3.6 %convolution_convert_fusion = bf16[96,7168]{1,0:T(8,128)(2,1)} fusion(bf16[128,7168]{1,0:T(8,128)(2,1)S(1)} %copy-done, bf16[96,7168]{1,0:T(8,128)(2,1)S(1)} %reshape.29, bf16[7168,128]{1,0:T(8,128)(2,1)} %param.10, f32[96,128]{1,0:T(8,128)S(1)} %fusion.24), kind=kOutput, calls=%fused_computation.2 | convolution fusion | flops 353083392 | bytes 6471680 | tf_op jit(solution)/shard_map/dot_general | solution.py:48
  57.6 2.6 %reshape.30 = bf16[8,2,6,7168]{3,2,1,0:T(8,128)(2,1)} reshape(bf16[96,7168]{1,0:T(8,128)(2,1)} %convolution_convert_fusion) | data formatting | bytes 2752512 | tf_op jit(solution)/shard_map/reshape | solution.py:51
  60.2 4.0 %copy.39 = bf16[8,2,6,7168]{3,1,2,0:T(2,128)(2,1)} copy(bf16[8,2,6,7168]{3,2,1,0:T(8,128)(2,1)} %reshape.30) | data formatting | bytes 2752512 | tf_op jit(solution)/shard_map/reshape | solution.py:51
  64.1 0.0 copy-start.1
  64.1 0.0 copy-start.2
  64.2 3.7 %all-to-all-start.2 = ((bf16[8,2,6,7168]{3,1,2,0:T(2,128)(2,1)}), bf16[8,2,6,7168]{3,1,2,0:T(2,128)(2,1)S(1)}, u32[]{:S(2)}, u32[]{:S(2)}) async-start(bf16[8,2,6,7168]{3,1,2,0:T(2,128)(2,1)} %copy.39), calls=%async_computation.2 | async-start | bytes 2752512 | tf_op jit(solution)/shard_map/all_to_all | solution.py:52
  67.9 0.0 copy-done.1
  67.9 0.0 copy-done.2
  67.9 0.1 fusion.14
  68.0 0.1 copy.44
  68.1 32.0 %all-to-all-done.2 = bf16[8,2,6,7168]{3,1,2,0:T(2,128)(2,1)S(1)} async-done(((bf16[8,2,6,7168]{3,1,2,0:T(2,128)(2,1)}), bf16[8,2,6,7168]{3,1,2,0:T(2,128)(2,1)S(1)}, u32[]{:S(2)}, u32[]{:S(2)}) %all-to-all-start.2) | async-done | bytes 1376288 | tf_op jit(solution)/shard_map/all_to_all | solution.py:52
  100.1 1.2 %convert_reduce_fusion = f32[2,6,7168]{2,0,1:T(2,128)S(1)} fusion(bf16[8,2,6,7168]{3,1,2,0:T(2,128)(2,1)S(1)} %all-to-all-done.2), kind=kLoop, calls=%fused_computation.5 | loop fusion | flops 1290240 | bytes 1720320 | tf_op jit(solution)/shard_map/reduce_sum | solution.py:53
  101.3 0.4 copy.40
  101.6 4.0 %all_to_all.22 = f32[2,1,6,7168]{3,1,2,0:T(1,128)S(1)} all-to-all(f32[2,1,6,7168]{3,1,2,0:T(1,128)S(1)} %copy.40), channel_id=1, replica_groups=mesh['groups'=2,'hst'=2,'local'=8] {'hst'}, dimensions={0} | all-to-all | bytes 688128 | tf_op jit(solution)/shard_map/all_to_all | solution.py:56
  105.6 0.2 bitcast_multiply_fusion
  105.9 2.9 %fusion = bf16[128,7168]{1,0:T(8,128)(2,1)} fusion(f32[2,6,7168]{2,0,1:T(2,128)S(1)} %bitcast_multiply_fusion, s32[2,128]{1,0:T(2,128)S(1)} %copy.35, pred[2,128]{1,0:T(4,128)(4,1)S(1)} %get-tuple-element.5), kind=kOutput, calls=%fused_computation.1 | convolution fusion | flops 133041152 | bytes 2180352 | tf_op jit(solution)/shard_map/wmt,wmd->td/dot_general | solution.py:61
  (3 shorter events, 0.0 us)
Async XLA Ops:
  0.0 54.0 %copy-start = (bf16[128,7168]{1,0:T(8,128)(2,1)S(1)}, bf16[128,7168]{1,0:T(8,128)(2,1)}, u32[]{:S(2)}) copy-start(bf16[128,7168]{1,0:T(8,128)(2,1)} %param.11) | copy-start | bytes 5505028
  64.1 3.7 %copy-start.1 = (s32[128,8]{0,1:T(8,128)S(1)}, s32[128,8]{0,1:T(8,128)}, u32[]{:S(2)}) copy-start(s32[128,8]{0,1:T(8,128)} %param.7) | copy-start | bytes 12292
  64.1 3.7 %copy-start.2 = (f32[128,8]{0,1:T(8,128)S(1)}, f32[128,8]{0,1:T(8,128)}, u32[]{:S(2)}) copy-start(f32[128,8]{0,1:T(8,128)} %param.8) | copy-start | bytes 12292
  64.2 35.9 %all-to-all-start.2 = ((bf16[8,2,6,7168]{3,1,2,0:T(2,128)(2,1)}), bf16[8,2,6,7168]{3,1,2,0:T(2,128)(2,1)S(1)}, u32[]{:S(2)}, u32[]{:S(2)}) async-start(bf16[8,2,6,7168]{3,1,2,0:T(2,128)(2,1)} %copy.39), calls=%async_computation.2 | async-start | bytes 2752512 | tf_op jit(solution)/shard_map/all_to_all | solution.py:52
where the time goes:
time: 109 us
  blocking collectives  48.7 us (45%)
  waiting for transfers between devices  32 us (29%)
  local copies, waits for them, and re-layouts  11.4 us (10%)
  matrix products  10.5 us (10%)
  starting transfers between devices  3.7 us (3%)
  other arithmetic  2.47 us (2%)
    all_to_all x1, blocking collectives, on_device(): lax.all_to_all(spread, 'local', split_axis=0, concat_axis=0, tiled=True)  40.8 us
    all_to_all x1, waiting for transfers between devices, on_device(): lax.all_to_all(partial_value, 'local', split_axis=0, concat_axis=0, tiled...  32 us
    reshape x2, local copies, waits for them, and re-layouts, on_device(): partial_value = partial_value.reshape(in_shape)  6.57 us
    all_to_all x1, blocking collectives, on_device(): lax.all_to_all(jnp.transpose(summed, (1, 0, 2, 3)), 'hst', split_axis=0,...  3.98 us
    all_to_all x1, blocking collectives, on_device(): lax.all_to_all(outgoing.reshape(host_count, per_host, MOST, width), 'hst'...  3.9 us
    all_to_all x1, starting transfers between devices, on_device(): lax.all_to_all(partial_value, 'local', split_axis=0, concat_axis=0, tiled...  3.7 us
    dot_general x1, matrix products, on_device(): jnp.dot(hidden, down_weight, preferred_element_type=jnp.float32)  3.58 us
    dot_general x1, matrix products, on_device(): jnp.einsum('wmt,wmd->td', select.astype(jnp.float32), weighted, precision...  2.91 us
  transfers between devices with their start and end apart: 1, of which 1 were waited for; matrix products, arithmetic and copies ran while one was open for 0% of the time, Pallas kernels for 0%

commit v1 on v0

v1 whole, which is shorter than its diff:
```python
import jax
import jax.numpy as jnp
from jax import lax
from jax.experimental import pallas as pl
from jax.experimental.pallas import tpu as pltpu
from jax.sharding import PartitionSpec as P

SPLIT = 8
MOST = 6
SEGS = 4
ROWS = SEGS * MOST
BF = jnp.bfloat16
F32 = jnp.float32
VMEM_LIMIT = 48 * 1024 * 1024


def route_table(expert_ids, route_weights, experts_win):
    window = jnp.arange(experts_win, dtype=jnp.int32)
    matched = expert_ids[:, :, None] == window[None, None, :]
    is_hit = jnp.any(matched, axis=1).astype(jnp.int32)
    weight = jnp.sum(jnp.where(matched, route_weights[:, :, None], F32(0.0)), axis=1)
    position = jnp.cumsum(is_hit, axis=0) - 1
    slot_index = jnp.arange(MOST, dtype=jnp.int32)
    select = (is_hit.T[:, None, :] == 1) & (position.T[:, None, :] == slot_index[None, :, None])
    return (select, weight)


def general(tokens, expert_ids, route_weights, gate_weight, up_weight, down_weight):
    host_count = lax.axis_size("hst")
    local_count = lax.axis_size("local")
    per_host = local_count // SPLIT
    experts_win = host_count * per_host
    width = tokens.shape[1]
    select, weight = route_table(expert_ids, route_weights, experts_win)
    outgoing = jnp.einsum(
        "wmt,td->wmd", select.astype(BF), tokens, preferred_element_type=F32
    ).astype(BF)
    slot_weight = jnp.einsum(
        "wmt,tw->wm", select.astype(F32), weight, precision=lax.Precision.HIGHEST
    )
    host_rows = lax.all_to_all(
        outgoing.reshape(host_count, per_host, MOST, width), "hst", 0, 0, tiled=True
    )
    spread = jnp.repeat(jnp.transpose(host_rows, (1, 0, 2, 3)), SPLIT, axis=0)
    row_block = lax.all_to_all(spread, "local", 0, 0, tiled=True)
    in_shape = row_block.shape
    flattened = row_block.reshape(-1, width)
    gate_sum = jnp.dot(flattened, gate_weight, preferred_element_type=F32)
    up_sum = jnp.dot(flattened, up_weight, preferred_element_type=F32)
    hidden = (jax.nn.silu(gate_sum) * up_sum).astype(BF)
    partial_value = jnp.dot(hidden, down_weight, preferred_element_type=F32).astype(BF)
    partial_value = partial_value.reshape(in_shape)
    returned_rows = lax.all_to_all(partial_value, "local", 0, 0, tiled=True)
    summed = jnp.sum(
        returned_rows.reshape(per_host, SPLIT, host_count, MOST, width).astype(F32), axis=1
    )
    returned_sums = lax.all_to_all(
        jnp.transpose(summed, (1, 0, 2, 3)), "hst", 0, 0, tiled=True
    )
    combined = returned_sums.reshape(experts_win, MOST, width)
    weighted = combined * slot_weight[:, :, None]
    total = jnp.einsum(
        "wmt,wmd->td", select.astype(F32), weighted, precision=lax.Precision.HIGHEST
    )
    return total.astype(BF)


def select_rows(core, tokens, ids_t, weights_t):
    count, width = tokens.shape
    seg = width // SEGS
    topk = ids_t.shape[0]

    def kernel(core_ref, ids_ref, weights_ref, tokens_ref, own_ref, twin_ref, slot_ref, scale_ref, acc):
        step = pl.program_id(0)

        @pl.when(step == 0)
        def _():
            core = core_ref[0]
            ids = ids_ref[...]
            row = lax.broadcasted_iota(jnp.int32, (count, count), 0)
            col = lax.broadcasted_iota(jnp.int32, (count, count), 1)
            before = (row < col).astype(BF)
            slot = lax.broadcasted_iota(jnp.int32, (ROWS, count), 0) % MOST
            for part in range(2):
                expert = core if part == 0 else 1 - core
                named = ids == expert
                hit = jnp.max(named.astype(F32), axis=0, keepdims=True)
                weight = jnp.sum(jnp.where(named, weights_ref[...], 0.0), axis=0, keepdims=True)
                wide = jnp.broadcast_to(hit, (16, count)).astype(BF)
                position = jnp.dot(wide, before, preferred_element_type=F32)[0:1]
                chosen = (hit > 0.0) & (position.astype(jnp.int32) == slot)
                table = chosen.astype(F32)
                slot_ref[part] = table
                scale = jnp.sum(table * weight, axis=1, keepdims=True)
                scale_ref[part] = jnp.broadcast_to(scale, (ROWS, 128))

        line = lax.broadcasted_iota(jnp.int32, (ROWS, count), 0) // MOST
        keep = line == step
        table = jnp.concatenate(
            [jnp.where(keep, slot_ref[0], 0.0), jnp.where(keep, slot_ref[1], 0.0)], axis=0
        ).astype(BF)
        rows = jnp.dot(table, tokens_ref[...], preferred_element_type=F32)

        @pl.when(step == 0)
        def _():
            acc[...] = rows

        @pl.when(step > 0)
        def _():
            acc[...] += rows

        @pl.when(step == SEGS - 1)
        def _():
            own_ref[...] = acc[0:ROWS].astype(BF)
            twin_ref[...] = acc[ROWS : 2 * ROWS].astype(BF)

    whole = lambda *shape: pl.BlockSpec(shape, lambda i, *_: (0,) * len(shape))
    return pl.pallas_call(
        kernel,
        grid_spec=pltpu.PrefetchScalarGridSpec(
            num_scalar_prefetch=1,
            grid=(SEGS,),
            in_specs=[
                whole(topk, count),
                whole(topk, count),
                pl.BlockSpec((count, seg), lambda i, *_: (0, i)),
            ],
            out_specs=[
                whole(ROWS, seg),
                whole(ROWS, seg),
                whole(2, ROWS, count),
                whole(2, ROWS, 128),
            ],
            scratch_shapes=[pltpu.VMEM((2 * ROWS, seg), F32)],
        ),
        out_shape=[
            jax.ShapeDtypeStruct((ROWS, seg), BF),
            jax.ShapeDtypeStruct((ROWS, seg), BF),
            jax.ShapeDtypeStruct((2, ROWS, count), F32),
            jax.ShapeDtypeStruct((2, ROWS, 128), F32),
        ],
        compiler_params=pltpu.CompilerParams(vmem_limit_bytes=VMEM_LIMIT),
        name="select_rows",
    )(core, ids_t, weights_t, tokens)


def experts(blocks, gate_weight, up_weight, down_weight):
    seg = blocks[0].shape[1]
    units = gate_weight.shape[1]
    height = SPLIT * ROWS
    tile = 256

    def kernel(*refs):
        block_refs = refs[:SPLIT]
        gate_ref, up_ref, down_ref, far_ref, near_ref, kept_ref = refs[SPLIT:]
        rows = jnp.concatenate([ref[...] for ref in block_refs], axis=0)
        line = lax.broadcasted_iota(jnp.int32, (height, 2 * units), 0) % ROWS // MOST
        total = jnp.zeros((height, 2 * units), F32)
        for s in range(SEGS):
            cut = slice(s * seg, (s + 1) * seg)
            both = jnp.concatenate([gate_ref[cut, :], up_ref[cut, :]], axis=1)
            part = jnp.dot(rows, both, preferred_element_type=F32)
            total = total + jnp.where(line == s, part, 0.0)
        one = lax.broadcasted_iota(jnp.int32, (height, height), 0)
        two = lax.broadcasted_iota(jnp.int32, (height, height), 1)
        same = (one // ROWS == two // ROWS) & (one % MOST == two % MOST)
        spread = jnp.dot(
            same.astype(F32), total, precision=lax.Precision.HIGHEST, preferred_element_type=F32
        )
        gate = spread[:, :units]
        up = spread[:, units:]
        hidden = gate / (1.0 + jnp.exp(-gate)) * up
        wide = jnp.concatenate(
            [jnp.where(line[:, :units] == s, hidden, 0.0) for s in range(SEGS)], axis=1
        ).astype(BF)
        for j in range(seg // tile):
            weights = jnp.concatenate(
                [down_ref[:, s * seg + j * tile : s * seg + (j + 1) * tile] for s in range(SEGS)],
                axis=0,
            )
            out = jnp.dot(wide, weights, preferred_element_type=F32).astype(BF)
            cut = slice(j * tile, (j + 1) * tile)
            far_ref[:, cut] = out[: 2 * ROWS]
            near_ref[:, cut] = out[2 * ROWS : 4 * ROWS]
            kept_ref[:, cut] = out[4 * ROWS :]

    return pl.pallas_call(
        kernel,
        in_specs=[pl.BlockSpec(memory_space=pltpu.VMEM)] * (SPLIT + 3),
        out_specs=[pl.BlockSpec(memory_space=pltpu.VMEM)] * 3,
        out_shape=[
            jax.ShapeDtypeStruct((2 * ROWS, seg), BF),
            jax.ShapeDtypeStruct((2 * ROWS, seg), BF),
            jax.ShapeDtypeStruct((4 * ROWS, seg), BF),
        ],
        compiler_params=pltpu.CompilerParams(vmem_limit_bytes=VMEM_LIMIT),
        cost_estimate=pl.CostEstimate(
            flops=2 * height * seg * SEGS * units * 3,
            bytes_accessed=3 * 2 * units * seg * SEGS,
            transcendentals=0,
        ),
        name="experts",
    )(*blocks, gate_weight, up_weight, down_weight)


def combine(own_terms, twin, slot, scale):
    kept, near, others = own_terms
    seg = twin.shape[1]
    count = slot.shape[2]

    def kernel(kept_ref, near_ref, one_ref, two_ref, three_ref, twin_ref, slot_ref, scale_ref, out_ref, rows):
        step = pl.program_id(0)

        @pl.when(step == 0)
        def _():
            own = kept_ref[0:ROWS].astype(F32) + near_ref[ROWS : 2 * ROWS].astype(F32)
            own = own + one_ref[...].astype(F32)
            own = own + two_ref[...].astype(F32)
            own = own + three_ref[...].astype(F32)
            own = own * scale_ref[0][:, 0:1]
            other = twin_ref[...].astype(F32) * scale_ref[1][:, 0:1]
            both = jnp.concatenate([own, other], axis=0)
            high = both.astype(BF)
            low = (both - high.astype(F32)).astype(BF)
            rows[...] = jnp.concatenate([high, low], axis=0)

        line = lax.broadcasted_iota(jnp.int32, (ROWS, count), 0) // MOST
        keep = line == step
        table = jnp.concatenate(
            [jnp.where(keep, slot_ref[0], 0.0), jnp.where(keep, slot_ref[1], 0.0)], axis=0
        ).astype(BF)
        table = jnp.concatenate([table, table], axis=0)
        out_ref[...] = lax.dot_general(
            table, rows[...], (((0,), (0,)), ((), ())), preferred_element_type=F32
        ).astype(BF)

    whole = lambda *shape: pl.BlockSpec(shape, lambda i: (0,) * len(shape))
    operands = (kept, near, *others, twin, slot, scale)
    return pl.pallas_call(
        kernel,
        grid=(SEGS,),
        in_specs=[whole(*x.shape) for x in operands],
        out_specs=pl.BlockSpec((count, seg), lambda i: (0, i)),
        out_shape=jax.ShapeDtypeStruct((count, seg * SEGS), BF),
        scratch_shapes=[pltpu.VMEM((4 * ROWS, seg), BF)],
        compiler_params=pltpu.CompilerParams(vmem_limit_bytes=VMEM_LIMIT),
        name="combine",
    )(*operands)


def swap(x, mask):
    return lax.ppermute(x, "local", [(i, i ^ mask) for i in range(SPLIT)])


def swap_cores(x):
    return lax.ppermute(x, "hst", [(0, 1), (1, 0)])


def gather(block):
    got = {0: block}
    got[1] = swap(block, 1)
    got[4] = swap(block, 4)
    got[6] = swap(block, 6)
    got[2] = swap(block, 2)
    for k in (2, 4, 6):
        got[k + 1] = swap(got[k], 1)
    return got


def scatter(far, near, kept):
    far = swap(far, 1)
    near = swap(near, 1)
    add = lambda a, b: (a.astype(F32) + b.astype(F32)).astype(BF)
    four = swap(add(kept[2 * ROWS : 3 * ROWS], far[:ROWS]), 4)
    six = swap(add(kept[3 * ROWS :], far[ROWS:]), 6)
    two = swap(add(kept[ROWS : 2 * ROWS], near[:ROWS]), 2)
    return kept, near, (two, four, six)


def single(tokens, expert_ids, route_weights, gate_weight, up_weight, down_weight):
    core = lax.axis_index("hst").astype(jnp.int32).reshape(1)
    own, other, slot, scale = select_rows(core, tokens, expert_ids.T, route_weights.T)
    terms = []
    twin = swap_cores(other)
    for block in (own, twin):
        got = gather(block)
        order = [got[k] for k in (5, 7, 3, 1, 0, 2, 4, 6)]
        far, near, kept = experts(order, gate_weight, up_weight, down_weight)
        terms.append(scatter(far, near, kept))
    kept, near, others = terms[1]
    back = kept[:ROWS].astype(F32) + near[ROWS:].astype(F32)
    for x in others:
        back = back + x.astype(F32)
    back = swap_cores(back.astype(BF))
    return combine(terms[0], back, slot, scale)


def solution(mesh):
    in_specs = (
        P(("groups", "hst", "local"), None),
        P(("groups", "hst", "local"), None),
        P(("groups", "hst", "local"), None),
        P(None, ("hst", "local")),
        P(None, ("hst", "local")),
        P(("hst", "local"), None),
    )
    out_specs = P(("groups", "hst", "local"), None)
    body = single if mesh.shape["local"] == SPLIT and mesh.shape["hst"] == 2 else general
    return jax.shard_map(
        body, mesh=mesh, in_specs=in_specs, out_specs=out_specs, check_vma=False
    )
```

time: 109 us -> 64.2 us (0.59)
  blocking collectives: 48.7 us -> 0 us
  starting transfers between devices: 3.7 us -> 32 us
  waiting for transfers between devices: 32 us -> 16 us
  Pallas kernels: 0 us -> 11.2 us
  matrix products: 10.5 us -> 0 us
  local copies, waits for them, and re-layouts: 11.4 us -> 4.51 us
  other arithmetic: 2.47 us -> 0.2 us
    all_to_all x3 -> x0, blocking collectives: 48.7 us -> none  [the longest x1 40.8 us: on_device(): lax.all_to_all(spread, 'local', split_axis=0, concat_axis=0, tiled=True)]
    ppermute x0 -> x26, starting transfers between devices: none -> 32 us  [the longest x24 31.4 us: swap(): return lax.ppermute(x, 'local', [(i, i ^ mask) for i in range(SPLIT)])]
    all_to_all x1 -> x0, waiting for transfers between devices: 32 us -> none  [on_device(): lax.all_to_all(partial_value, 'local', split_axis=0, concat_axis=0, tiled...]
    ppermute x0 -> x26, waiting for transfers between devices: none -> 16 us  [the longest x24 16 us: swap(): return lax.ppermute(x, 'local', [(i, i ^ mask) for i in range(SPLIT)])]
    pallas_call x0 -> x4, Pallas kernels: none -> 11.2 us  [the longest x2 7.12 us: experts(): pl.pallas_call(kernel, in_specs=[pl.BlockSpec(memory_space=pltpu.VMEM)] *...]
    dot_general x5 -> x0, matrix products: 10.5 us -> none  [the longest x1 3.58 us: on_device(): jnp.dot(hidden, down_weight, preferred_element_type=jnp.float32)]
    reshape x4 -> x0, local copies, waits for them, and re-layouts: 9 us -> none  [the longest x2 6.57 us: on_device(): partial_value = partial_value.reshape(in_shape)]
    unnamed x6 -> x12, local copies, waits for them, and re-layouts: 0.01 us -> 4.51 us
  transfers between devices with their start and end apart: 1 -> 26, of which waited for: 1 -> 7; matrix products, arithmetic and copies ran while one was open for 0% -> 0% of each run, Pallas kernels for 0% -> 11%
where the time goes in v1:
time: 64.2 us; the launch traced here: 64 us
  starting transfers between devices  32 us (50%)
  waiting for transfers between devices  16 us (25%)
  Pallas kernels  11.2 us (17%)
  local copies, waits for them, and re-layouts  4.51 us (7%)
    ppermute x24, starting transfers between devices, swap(): return lax.ppermute(x, 'local', [(i, i ^ mask) for i in range(SPLIT)])  31.4 us
    ppermute x24, waiting for transfers between devices, swap(): return lax.ppermute(x, 'local', [(i, i ^ mask) for i in range(SPLIT)])  16 us
    pallas_call x2, Pallas kernels, experts(): pl.pallas_call(kernel, in_specs=[pl.BlockSpec(memory_space=pltpu.VMEM)] *...  7.12 us
    unnamed x12, local copies, waits for them, and re-layouts  4.51 us
    pallas_call x1, Pallas kernels, combine(): pl.pallas_call(kernel, grid=(SEGS,), in_specs=[whole(*x.shape) for x in o...  2.72 us
    pallas_call x1, Pallas kernels, select_rows(): pl.pallas_call(kernel, grid_spec=pltpu.PrefetchScalarGridSpec(num_scalar_...  1.37 us
  transfers between devices with their start and end apart: 26, of which 7 were waited for; matrix products, arithmetic and copies ran while one was open for 0% of the time, Pallas kernels for 11%

profile of v1, /device:TPU:0, one launch (start us, length us, event | category | flops | bytes accessed | tf_op | source)
XLA Modules:
  0.0 64.0 jit_solution(3141871236855659689)
XLA Ops:
  0.0 1.6 %copy-done.3 = bf16[128,7168]{1,0:T(8,128)(2,1)S(1)} copy-done((bf16[128,7168]{1,0:T(8,128)(2,1)S(1)}, bf16[128,7168]{1,0:T(8,128)(2,1)}, u32[]{:S(2)}) %copy-start.3) | copy-done | bytes 1835032
  1.6 0.7 %copy-done.4 = s32[128,8]{0,1:T(8,128)S(1)} copy-done((s32[128,8]{0,1:T(8,128)S(1)}, s32[128,8]{0,1:T(8,128)}, u32[]{:S(2)}) %copy-start.4) | copy-done | bytes 4120
  2.3 0.7 %copy-done.5 = f32[128,8]{0,1:T(8,128)S(1)} copy-done((f32[128,8]{0,1:T(8,128)S(1)}, f32[128,8]{0,1:T(8,128)}, u32[]{:S(2)}) %copy-start.5) | copy-done | bytes 4120
  3.0 1.4 %select_rows.1 = (bf16[24,1792]{1,0:T(8,128)(2,1)S(1)}, bf16[24,1792]{1,0:T(8,128)(2,1)S(1)}, f32[2,24,128]{2,1,0:T(8,128)S(1)}, f32[2,24,128]{2,1,0:T(8,128)S(1)}) custom-call(s32[1]{0:T(128)} %bitcast.core_ref, s32[8,128]{1,0:T(8,128)S(1)} %bitcast.3, f32[8,128]{1,0:T(8,128)S(1)} %bitcast.4, bf16[128,7168]{1,0:T(8,128)(2,1)S(1)} %copy-done.3), custom_call_target="tpu_custom_call" | custom-call | tf_op jit(solution)/shard_map/select_rows/pallas_call | solution.py:118
  4.4 0.5 collective-permute-start.12
  4.9 2.6 %collective-permute-start.4 = (bf16[24,1792]{1,0:T(8,128)(2,1)S(1)}, bf16[24,1792]{1,0:T(8,128)(2,1)S(1)}, u32[]{:S(2)}, u32[]{:S(2)}) collective-permute-start(bf16[24,1792]{1,0:T(8,128)(2,1)S(1)} %get-tuple-element.15.refs_4_), channel_id=1, source_target_pairs={{0,2},{1,3},{2,0},{3,1},{4,6},{5,7},{6,4},{7,5},{8,10},{9,11},{10,... | collective-permute-start | bytes 258056 | tf_op jit(solution)/shard_map/ppermute | solution.py:252
  7.6 2.5 %collective-permute-start.2 = (bf16[24,1792]{1,0:T(8,128)(2,1)S(1)}, bf16[24,1792]{1,0:T(8,128)(2,1)S(1)}, u32[]{:S(2)}, u32[]{:S(2)}) collective-permute-start(bf16[24,1792]{1,0:T(8,128)(2,1)S(1)} %get-tuple-element.15.refs_4_), channel_id=1, source_target_pairs={{0,6},{1,7},{2,4},{3,5},{4,2},{5,3},{6,0},{7,1},{8,14},{9,15},{10,... | collective-permute-start | bytes 258056 | tf_op jit(solution)/shard_map/ppermute | solution.py:252
  10.0 0.7 %collective-permute-start.17 = (bf16[24,1792]{1,0:T(8,128)(2,1)S(1)}, bf16[24,1792]{1,0:T(8,128)(2,1)S(1)}, u32[]{:S(2)}, u32[]{:S(2)}) collective-permute-start(bf16[24,1792]{1,0:T(8,128)(2,1)S(1)} %collective-permute-done.12.refs_4_), channel_id=1, source_target_pairs={{0,2},{1,3},{2,0},{3,1},{4,6},{5,7},{6,4},{7,5},{8,10},{9,11},{10,... | collective-permute-start | bytes 258056 | tf_op jit(solution)/shard_map/ppermute | solution.py:252
  10.7 0.9 %collective-permute-start.15 = (bf16[24,1792]{1,0:T(8,128)(2,1)S(1)}, bf16[24,1792]{1,0:T(8,128)(2,1)S(1)}, u32[]{:S(2)}, u32[]{:S(2)}) collective-permute-start(bf16[24,1792]{1,0:T(8,128)(2,1)S(1)} %collective-permute-done.12.refs_4_), channel_id=1, source_target_pairs={{0,6},{1,7},{2,4},{3,5},{4,2},{5,3},{6,0},{7,1},{8,14},{9,15},{10,... | collective-permute-start | bytes 258056 | tf_op jit(solution)/shard_map/ppermute | solution.py:252
  11.6 1.9 %collective-permute-start.13 = (bf16[24,1792]{1,0:T(8,128)(2,1)S(1)}, bf16[24,1792]{1,0:T(8,128)(2,1)S(1)}, u32[]{:S(2)}, u32[]{:S(2)}) collective-permute-start(bf16[24,1792]{1,0:T(8,128)(2,1)S(1)} %collective-permute-done.12.refs_4_), channel_id=1, source_target_pairs={{0,4},{1,5},{2,6},{3,7},{4,0},{5,1},{6,2},{7,3},{8,12},{9,13},{10,... | collective-permute-start | bytes 258056 | tf_op jit(solution)/shard_map/ppermute | solution.py:252
  13.5 1.0 %collective-permute-start = (bf16[24,1792]{1,0:T(8,128)(2,1)S(1)}, bf16[24,1792]{1,0:T(8,128)(2,1)S(1)}, u32[]{:S(2)}, u32[]{:S(2)}) collective-permute-start(bf16[24,1792]{1,0:T(8,128)(2,1)S(1)} %get-tuple-element.15.refs_4_), channel_id=1, source_target_pairs={{0,4},{1,5},{2,6},{3,7},{4,0},{5,1},{6,2},{7,3},{8,12},{9,13},{10,... | collective-permute-start | bytes 258056 | tf_op jit(solution)/shard_map/ppermute | solution.py:252
  14.5 0.7 %collective-permute-done.2.refs_7_ = bf16[24,1792]{1,0:T(8,128)(2,1)S(1)} collective-permute-done((bf16[24,1792]{1,0:T(8,128)(2,1)S(1)}, bf16[24,1792]{1,0:T(8,128)(2,1)S(1)}, u32[]{:S(2)}, u32[]{:S(2)}) %collective-permute-start.2) | collective-permute-done | bytes 86048 | tf_op jit(solution)/shard_map/ppermute | solution.py:252
  15.2 1.5 %collective-permute-start.19 = (bf16[24,1792]{1,0:T(8,128)(2,1)S(1)}, bf16[24,1792]{1,0:T(8,128)(2,1)S(1)}, u32[]{:S(2)}, u32[]{:S(2)}) collective-permute-start(bf16[24,1792]{1,0:T(8,128)(2,1)S(1)} %collective-permute-done.12.refs_4_), channel_id=1, source_target_pairs={{0,1},{1,0},{2,3},{3,2},{4,5},{5,4},{6,7},{7,6},{8,9},{9,8},{10,11... | collective-permute-start | bytes 258056 | tf_op jit(solution)/shard_map/ppermute | solution.py:252
  16.7 1.0 %collective-permute-start.18 = (bf16[24,1792]{1,0:T(8,128)(2,1)S(1)}, bf16[24,1792]{1,0:T(8,128)(2,1)S(1)}, u32[]{:S(2)}, u32[]{:S(2)}) collective-permute-start(bf16[24,1792]{1,0:T(8,128)(2,1)S(1)} %collective-permute-done.17.refs_5_), channel_id=1, source_target_pairs={{0,1},{1,0},{2,3},{3,2},{4,5},{5,4},{6,7},{7,6},{8,9},{9,8},{10,11... | collective-permute-start | bytes 258056 | tf_op jit(solution)/shard_map/ppermute | solution.py:252
  17.7 1.3 %collective-permute-done.15.refs_7_ = bf16[24,1792]{1,0:T(8,128)(2,1)S(1)} collective-permute-done((bf16[24,1792]{1,0:T(8,128)(2,1)S(1)}, bf16[24,1792]{1,0:T(8,128)(2,1)S(1)}, u32[]{:S(2)}, u32[]{:S(2)}) %collective-permute-start.15) | collective-permute-done | bytes 86048 | tf_op jit(solution)/shard_map/ppermute | solution.py:252
  19.0 1.5 %collective-permute-start.16 = (bf16[24,1792]{1,0:T(8,128)(2,1)S(1)}, bf16[24,1792]{1,0:T(8,128)(2,1)S(1)}, u32[]{:S(2)}, u32[]{:S(2)}) collective-permute-start(bf16[24,1792]{1,0:T(8,128)(2,1)S(1)} %collective-permute-done.15.refs_7_), channel_id=1, source_target_pairs={{0,1},{1,0},{2,3},{3,2},{4,5},{5,4},{6,7},{7,6},{8,9},{9,8},{10,11... | collective-permute-start | bytes 258056 | tf_op jit(solution)/shard_map/ppermute | solution.py:252
  20.5 3.8 %collective-permute-done.13.refs_6_ = bf16[24,1792]{1,0:T(8,128)(2,1)S(1)} collective-permute-done((bf16[24,1792]{1,0:T(8,128)(2,1)S(1)}, bf16[24,1792]{1,0:T(8,128)(2,1)S(1)}, u32[]{:S(2)}, u32[]{:S(2)}) %collective-permute-start.13) | collective-permute-done | bytes 86048 | tf_op jit(solution)/shard_map/ppermute | solution.py:252
  24.3 1.5 %collective-permute-start.14 = (bf16[24,1792]{1,0:T(8,128)(2,1)S(1)}, bf16[24,1792]{1,0:T(8,128)(2,1)S(1)}, u32[]{:S(2)}, u32[]{:S(2)}) collective-permute-start(bf16[24,1792]{1,0:T(8,128)(2,1)S(1)} %collective-permute-done.13.refs_6_), channel_id=1, source_target_pairs={{0,1},{1,0},{2,3},{3,2},{4,5},{5,4},{6,7},{7,6},{8,9},{9,8},{10,11... | collective-permute-start | bytes 258056 | tf_op jit(solution)/shard_map/ppermute | solution.py:252
  25.9 0.0 collective-permute-done.refs_6_
  25.9 1.5 %collective-permute-start.6 = (bf16[24,1792]{1,0:T(8,128)(2,1)S(1)}, bf16[24,1792]{1,0:T(8,128)(2,1)S(1)}, u32[]{:S(2)}, u32[]{:S(2)}) collective-permute-start(bf16[24,1792]{1,0:T(8,128)(2,1)S(1)} %get-tuple-element.15.refs_4_), channel_id=1, source_target_pairs={{0,1},{1,0},{2,3},{3,2},{4,5},{5,4},{6,7},{7,6},{8,9},{9,8},{10,11... | collective-permute-start | bytes 258056 | tf_op jit(solution)/shard_map/ppermute | solution.py:252
  27.4 0.0 collective-permute-done.19.refs_3_
  27.4 0.5 collective-permute-start.5
  27.9 1.5 %collective-permute-start.3 = (bf16[24,1792]{1,0:T(8,128)(2,1)S(1)}, bf16[24,1792]{1,0:T(8,128)(2,1)S(1)}, u32[]{:S(2)}, u32[]{:S(2)}) collective-permute-start(bf16[24,1792]{1,0:T(8,128)(2,1)S(1)} %collective-permute-done.2.refs_7_), channel_id=1, source_target_pairs={{0,1},{1,0},{2,3},{3,2},{4,5},{5,4},{6,7},{7,6},{8,9},{9,8},{10,11... | collective-permute-start | bytes 258056 | tf_op jit(solution)/shard_map/ppermute | solution.py:252
  29.5 0.0 collective-permute-done.16.refs_1_
  29.5 0.5 collective-permute-start.1
  30.0 0.0 collective-permute-done.14.refs_0_
  30.0 1.5 %copy-done.1 = bf16[7168,128]{1,0:T(8,128)(2,1)S(1)} copy-done((bf16[7168,128]{1,0:T(8,128)(2,1)S(1)}, bf16[7168,128]{1,0:T(8,128)(2,1)}, u32[]{:S(2)}) %copy-start.1) | copy-done | bytes 1835032
  31.5 3.6 %experts.3 = (bf16[48,1792]{1,0:T(8,128)(2,1)S(1)}, bf16[48,1792]{1,0:T(8,128)(2,1)S(1)}, bf16[96,1792]{1,0:T(8,128)(2,1)S(1)}) custom-call(bf16[24,1792]{1,0:T(8,128)(2,1)S(1)} %collective-permute-done.14.refs_0_, bf16[24,1792]{1,0:T(8,128)(2,1)S(1)} %collective-permute-done.16.refs_1_, bf16[24,1792]{1,0:T(8,128)(2,1)S(1)} %collective-permute-done.18.refs_2_, ...), custom_call_target="tpu_custom_call" | custom-call | flops 1056964608 | bytes 5505024 | tf_op jit(solution)/shard_map/experts/pallas_call | solution.py:187
  35.1 1.6 %collective-permute-start.20 = (bf16[48,1792]{1,0:T(8,128)(2,1)S(1)}, bf16[48,1792]{1,0:T(8,128)(2,1)S(1)}, u32[]{:S(2)}, u32[]{:S(2)}) collective-permute-start(bf16[48,1792]{1,0:T(8,128)(2,1)S(1)} %get-tuple-element.21), channel_id=1, source_target_pairs={{0,1},{1,0},{2,3},{3,2},{4,5},{5,4},{6,7},{7,6},{8,9},{9,8},{10,11... | collective-permute-start | bytes 516104 | tf_op jit(solution)/shard_map/ppermute | solution.py:252
  36.7 0.0 collective-permute-done.6.refs_3_
  36.7 0.5 collective-permute-start.22
  37.2 3.5 %experts.2 = (bf16[48,1792]{1,0:T(8,128)(2,1)S(1)}, bf16[48,1792]{1,0:T(8,128)(2,1)S(1)}, bf16[96,1792]{1,0:T(8,128)(2,1)S(1)}) custom-call(bf16[24,1792]{1,0:T(8,128)(2,1)S(1)} %collective-permute-done.1.refs_0_, bf16[24,1792]{1,0:T(8,128)(2,1)S(1)} %collective-permute-done.3.refs_1_, bf16[24,1792]{1,0:T(8,128)(2,1)S(1)} %collective-permute-done.5.refs_2_, ...), custom_call_target="tpu_custom_call" | custom-call | flops 1056964608 | bytes 5505024 | tf_op jit(solution)/shard_map/experts/pallas_call | solution.py:187
  40.7 1.6 %collective-permute-start.7 = (bf16[48,1792]{1,0:T(8,128)(2,1)S(1)}, bf16[48,1792]{1,0:T(8,128)(2,1)S(1)}, u32[]{:S(2)}, u32[]{:S(2)}) collective-permute-start(bf16[48,1792]{1,0:T(8,128)(2,1)S(1)} %get-tuple-element.17), channel_id=1, source_target_pairs={{0,1},{1,0},{2,3},{3,2},{4,5},{5,4},{6,7},{7,6},{8,9},{9,8},{10,11... | collective-permute-start | bytes 516104 | tf_op jit(solution)/shard_map/ppermute | solution.py:252
  42.3 0.5 collective-permute-start.9
  42.8 3.0 %collective-permute-done.22 = bf16[48,1792]{1,0:T(8,128)(2,1)S(1)} collective-permute-done((bf16[48,1792]{1,0:T(8,128)(2,1)S(1)}, bf16[48,1792]{1,0:T(8,128)(2,1)S(1)}, u32[]{:S(2)}, u32[]{:S(2)}) %collective-permute-start.22) | collective-permute-done | bytes 172064 | tf_op jit(solution)/shard_map/ppermute | solution.py:252
  45.8 0.1 add_convert_fusion.2
  45.9 2.1 %collective-permute-start.23 = (bf16[24,1792]{1,0:T(8,128)(2,1)S(1)}, bf16[24,1792]{1,0:T(8,128)(2,1)S(1)}, u32[]{:S(2)}, u32[]{:S(2)}) collective-permute-start(bf16[24,1792]{1,0:T(8,128)(2,1)S(1)} %get-tuple-element.25), channel_id=1, source_target_pairs={{0,4},{1,5},{2,6},{3,7},{4,0},{5,1},{6,2},{7,3},{8,12},{9,13},{10,... | collective-permute-start | bytes 258056 | tf_op jit(solution)/shard_map/ppermute | solution.py:252
  48.0 0.8 %collective-permute-start.24 = (bf16[24,1792]{1,0:T(8,128)(2,1)S(1)}, bf16[24,1792]{1,0:T(8,128)(2,1)S(1)}, u32[]{:S(2)}, u32[]{:S(2)}) collective-permute-start(bf16[24,1792]{1,0:T(8,128)(2,1)S(1)} %get-tuple-element.26), channel_id=1, source_target_pairs={{0,6},{1,7},{2,4},{3,5},{4,2},{5,3},{6,0},{7,1},{8,14},{9,15},{10,... | collective-permute-start | bytes 258056 | tf_op jit(solution)/shard_map/ppermute | solution.py:252
  48.8 0.7 %collective-permute-start.21 = (bf16[24,1792]{1,0:T(8,128)(2,1)S(1)}, bf16[24,1792]{1,0:T(8,128)(2,1)S(1)}, u32[]{:S(2)}, u32[]{:S(2)}) collective-permute-start(bf16[24,1792]{1,0:T(8,128)(2,1)S(1)} %get-tuple-element.29), channel_id=1, source_target_pairs={{0,2},{1,3},{2,0},{3,1},{4,6},{5,7},{6,4},{7,5},{8,10},{9,11},{10,... | collective-permute-start | bytes 258056 | tf_op jit(solution)/shard_map/ppermute | solution.py:252
  49.5 1.8 %collective-permute-done.9 = bf16[48,1792]{1,0:T(8,128)(2,1)S(1)} collective-permute-done((bf16[48,1792]{1,0:T(8,128)(2,1)S(1)}, bf16[48,1792]{1,0:T(8,128)(2,1)S(1)}, u32[]{:S(2)}, u32[]{:S(2)}) %collective-permute-start.9) | collective-permute-done | bytes 172064 | tf_op jit(solution)/shard_map/ppermute | solution.py:252
  51.2 0.1 add_convert_fusion.4
  51.3 2.4 %collective-permute-start.11 = (bf16[24,1792]{1,0:T(8,128)(2,1)S(1)}, bf16[24,1792]{1,0:T(8,128)(2,1)S(1)}, u32[]{:S(2)}, u32[]{:S(2)}) collective-permute-start(bf16[24,1792]{1,0:T(8,128)(2,1)S(1)} %get-tuple-element.27), channel_id=1, source_target_pairs={{0,6},{1,7},{2,4},{3,5},{4,2},{5,3},{6,0},{7,1},{8,14},{9,15},{10,... | collective-permute-start | bytes 258056 | tf_op jit(solution)/shard_map/ppermute | solution.py:252
  53.7 2.1 %collective-permute-start.8 = (bf16[24,1792]{1,0:T(8,128)(2,1)S(1)}, bf16[24,1792]{1,0:T(8,128)(2,1)S(1)}, u32[]{:S(2)}, u32[]{:S(2)}) collective-permute-start(bf16[24,1792]{1,0:T(8,128)(2,1)S(1)} %get-tuple-element.30), channel_id=1, source_target_pairs={{0,2},{1,3},{2,0},{3,1},{4,6},{5,7},{6,4},{7,5},{8,10},{9,11},{10,... | collective-permute-start | bytes 258056 | tf_op jit(solution)/shard_map/ppermute | solution.py:252
  55.8 0.1 add_convert_fusion
  55.8 0.1 collective-permute-start.25
  55.9 2.7 %collective-permute-done.11.three_ref = bf16[24,1792]{1,0:T(8,128)(2,1)S(1)} collective-permute-done((bf16[24,1792]{1,0:T(8,128)(2,1)S(1)}, bf16[24,1792]{1,0:T(8,128)(2,1)S(1)}, u32[]{:S(2)}, u32[]{:S(2)}) %collective-permute-start.11) | collective-permute-done | bytes 86048 | tf_op jit(solution)/shard_map/ppermute | solution.py:252
  58.6 2.6 %collective-permute-done.10.two_ref = bf16[24,1792]{1,0:T(8,128)(2,1)S(1)} collective-permute-done((bf16[24,1792]{1,0:T(8,128)(2,1)S(1)}, bf16[24,1792]{1,0:T(8,128)(2,1)S(1)}, u32[]{:S(2)}, u32[]{:S(2)}) %collective-permute-start.10) | collective-permute-done | bytes 86048 | tf_op jit(solution)/shard_map/ppermute | solution.py:252
  61.3 2.7 %combine.1 = bf16[128,7168]{1,0:T(8,128)(2,1)} custom-call(bf16[96,1792]{1,0:T(8,128)(2,1)S(1)} %get-tuple-element.16.kept_ref, bf16[48,1792]{1,0:T(8,128)(2,1)S(1)} %collective-permute-done.7.near_ref, bf16[24,1792]{1,0:T(8,128)(2,1)S(1)} %collective-permute-done.8.one_ref, bf16[24,1792]{1,0:T(8,128)(2,1)S(1)} %collective-permute-done.10.two_ref, ...), custom_call_target="tpu_custom_call" | custom-call | tf_op jit(solution)/shard_map/combine/pallas_call | solution.py:239
  (23 shorter events, 0.1 us)
Async XLA Ops:
  0.0 30.0 %copy-start = (bf16[7168,128]{1,0:T(8,128)(2,1)S(1)}, bf16[7168,128]{1,0:T(8,128)(2,1)}, u32[]{:S(2)}) copy-start(bf16[7168,128]{1,0:T(8,128)(2,1)} %refs_8_.3) | copy-start | bytes 5505028
  0.0 1.6 %copy-start.3 = (bf16[128,7168]{1,0:T(8,128)(2,1)S(1)}, bf16[128,7168]{1,0:T(8,128)(2,1)}, u32[]{:S(2)}) copy-start(bf16[128,7168]{1,0:T(8,128)(2,1)} %tokens_ref.1) | copy-start | bytes 5505028
  1.6 0.7 %copy-start.4 = (s32[128,8]{0,1:T(8,128)S(1)}, s32[128,8]{0,1:T(8,128)}, u32[]{:S(2)}) copy-start(s32[128,8]{0,1:T(8,128)} %param.7) | copy-start | bytes 12292
  2.3 0.7 %copy-start.5 = (f32[128,8]{0,1:T(8,128)S(1)}, f32[128,8]{0,1:T(8,128)}, u32[]{:S(2)}) copy-start(f32[128,8]{0,1:T(8,128)} %param.8) | copy-start | bytes 12292
  4.4 5.6 %collective-permute-start.12 = (bf16[24,1792]{1,0:T(8,128)(2,1)S(1)}, bf16[24,1792]{1,0:T(8,128)(2,1)S(1)}, u32[]{:S(2)}, u32[]{:S(2)}) collective-permute-start(bf16[24,1792]{1,0:T(8,128)(2,1)S(1)} %get-tuple-element.19), channel_id=1, source_target_pairs={{0,8},{8,0},{1,9},{9,1},{2,10},{10,2},{3,11},{11,3},{4,12},{12,4},... | collective-permute-start | bytes 258056 | tf_op jit(solution)/shard_map/ppermute | solution.py:256
  4.9 8.6 %collective-permute-start.4 = (bf16[24,1792]{1,0:T(8,128)(2,1)S(1)}, bf16[24,1792]{1,0:T(8,128)(2,1)S(1)}, u32[]{:S(2)}, u32[]{:S(2)}) collective-permute-start(bf16[24,1792]{1,0:T(8,128)(2,1)S(1)} %get-tuple-element.15.refs_4_), channel_id=1, source_target_pairs={{0,2},{1,3},{2,0},{3,1},{4,6},{5,7},{6,4},{7,5},{8,10},{9,11},{10,... | collective-permute-start | bytes 258056 | tf_op jit(solution)/shard_map/ppermute | solution.py:252
  7.6 7.6 %collective-permute-start.2 = (bf16[24,1792]{1,0:T(8,128)(2,1)S(1)}, bf16[24,1792]{1,0:T(8,128)(2,1)S(1)}, u32[]{:S(2)}, u32[]{:S(2)}) collective-permute-start(bf16[24,1792]{1,0:T(8,128)(2,1)S(1)} %get-tuple-element.15.refs_4_), channel_id=1, source_target_pairs={{0,6},{1,7},{2,4},{3,5},{4,2},{5,3},{6,0},{7,1},{8,14},{9,15},{10,... | collective-permute-start | bytes 258056 | tf_op jit(solution)/shard_map/ppermute | solution.py:252
  10.0 6.7 %collective-permute-start.17 = (bf16[24,1792]{1,0:T(8,128)(2,1)S(1)}, bf16[24,1792]{1,0:T(8,128)(2,1)S(1)}, u32[]{:S(2)}, u32[]{:S(2)}) collective-permute-start(bf16[24,1792]{1,0:T(8,128)(2,1)S(1)} %collective-permute-done.12.refs_4_), channel_id=1, source_target_pairs={{0,2},{1,3},{2,0},{3,1},{4,6},{5,7},{6,4},{7,5},{8,10},{9,11},{10,... | collective-permute-start | bytes 258056 | tf_op jit(solution)/shard_map/ppermute | solution.py:252
  10.7 8.3 %collective-permute-start.15 = (bf16[24,1792]{1,0:T(8,128)(2,1)S(1)}, bf16[24,1792]{1,0:T(8,128)(2,1)S(1)}, u32[]{:S(2)}, u32[]{:S(2)}) collective-permute-start(bf16[24,1792]{1,0:T(8,128)(2,1)S(1)} %collective-permute-done.12.refs_4_), channel_id=1, source_target_pairs={{0,6},{1,7},{2,4},{3,5},{4,2},{5,3},{6,0},{7,1},{8,14},{9,15},{10,... | collective-permute-start | bytes 258056 | tf_op jit(solution)/shard_map/ppermute | solution.py:252
  11.6 12.7 %collective-permute-start.13 = (bf16[24,1792]{1,0:T(8,128)(2,1)S(1)}, bf16[24,1792]{1,0:T(8,128)(2,1)S(1)}, u32[]{:S(2)}, u32[]{:S(2)}) collective-permute-start(bf16[24,1792]{1,0:T(8,128)(2,1)S(1)} %collective-permute-done.12.refs_4_), channel_id=1, source_target_pairs={{0,4},{1,5},{2,6},{3,7},{4,0},{5,1},{6,2},{7,3},{8,12},{9,13},{10,... | collective-permute-start | bytes 258056 | tf_op jit(solution)/shard_map/ppermute | solution.py:252
  13.5 12.4 %collective-permute-start = (bf16[24,1792]{1,0:T(8,128)(2,1)S(1)}, bf16[24,1792]{1,0:T(8,128)(2,1)S(1)}, u32[]{:S(2)}, u32[]{:S(2)}) collective-permute-start(bf16[24,1792]{1,0:T(8,128)(2,1)S(1)} %get-tuple-element.15.refs_4_), channel_id=1, source_target_pairs={{0,4},{1,5},{2,6},{3,7},{4,0},{5,1},{6,2},{7,3},{8,12},{9,13},{10,... | collective-permute-start | bytes 258056 | tf_op jit(solution)/shard_map/ppermute | solution.py:252
  15.2 12.2 %collective-permute-start.19 = (bf16[24,1792]{1,0:T(8,128)(2,1)S(1)}, bf16[24,1792]{1,0:T(8,128)(2,1)S(1)}, u32[]{:S(2)}, u32[]{:S(2)}) collective-permute-start(bf16[24,1792]{1,0:T(8,128)(2,1)S(1)} %collective-permute-done.12.refs_4_), channel_id=1, source_target_pairs={{0,1},{1,0},{2,3},{3,2},{4,5},{5,4},{6,7},{7,6},{8,9},{9,8},{10,11... | collective-permute-start | bytes 258056 | tf_op jit(solution)/shard_map/ppermute | solution.py:252
  16.7 11.2 %collective-permute-start.18 = (bf16[24,1792]{1,0:T(8,128)(2,1)S(1)}, bf16[24,1792]{1,0:T(8,128)(2,1)S(1)}, u32[]{:S(2)}, u32[]{:S(2)}) collective-permute-start(bf16[24,1792]{1,0:T(8,128)(2,1)S(1)} %collective-permute-done.17.refs_5_), channel_id=1, source_target_pairs={{0,1},{1,0},{2,3},{3,2},{4,5},{5,4},{6,7},{7,6},{8,9},{9,8},{10,11... | collective-permute-start | bytes 258056 | tf_op jit(solution)/shard_map/ppermute | solution.py:252
  19.0 10.5 %collective-permute-start.16 = (bf16[24,1792]{1,0:T(8,128)(2,1)S(1)}, bf16[24,1792]{1,0:T(8,128)(2,1)S(1)}, u32[]{:S(2)}, u32[]{:S(2)}) collective-permute-start(bf16[24,1792]{1,0:T(8,128)(2,1)S(1)} %collective-permute-done.15.refs_7_), channel_id=1, source_target_pairs={{0,1},{1,0},{2,3},{3,2},{4,5},{5,4},{6,7},{7,6},{8,9},{9,8},{10,11... | collective-permute-start | bytes 258056 | tf_op jit(solution)/shard_map/ppermute | solution.py:252
  24.3 5.6 %collective-permute-start.14 = (bf16[24,1792]{1,0:T(8,128)(2,1)S(1)}, bf16[24,1792]{1,0:T(8,128)(2,1)S(1)}, u32[]{:S(2)}, u32[]{:S(2)}) collective-permute-start(bf16[24,1792]{1,0:T(8,128)(2,1)S(1)} %collective-permute-done.13.refs_6_), channel_id=1, source_target_pairs={{0,1},{1,0},{2,3},{3,2},{4,5},{5,4},{6,7},{7,6},{8,9},{9,8},{10,11... | collective-permute-start | bytes 258056 | tf_op jit(solution)/shard_map/ppermute | solution.py:252
  25.9 10.8 %collective-permute-start.6 = (bf16[24,1792]{1,0:T(8,128)(2,1)S(1)}, bf16[24,1792]{1,0:T(8,128)(2,1)S(1)}, u32[]{:S(2)}, u32[]{:S(2)}) collective-permute-start(bf16[24,1792]{1,0:T(8,128)(2,1)S(1)} %get-tuple-element.15.refs_4_), channel_id=1, source_target_pairs={{0,1},{1,0},{2,3},{3,2},{4,5},{5,4},{6,7},{7,6},{8,9},{9,8},{10,11... | collective-permute-start | bytes 258056 | tf_op jit(solution)/shard_map/ppermute | solution.py:252
  27.4 9.8 %collective-permute-start.5 = (bf16[24,1792]{1,0:T(8,128)(2,1)S(1)}, bf16[24,1792]{1,0:T(8,128)(2,1)S(1)}, u32[]{:S(2)}, u32[]{:S(2)}) collective-permute-start(bf16[24,1792]{1,0:T(8,128)(2,1)S(1)} %collective-permute-done.4.refs_5_), channel_id=1, source_target_pairs={{0,1},{1,0},{2,3},{3,2},{4,5},{5,4},{6,7},{7,6},{8,9},{9,8},{10,11... | collective-permute-start | bytes 258056 | tf_op jit(solution)/shard_map/ppermute | solution.py:252
  27.9 9.3 %collective-permute-start.3 = (bf16[24,1792]{1,0:T(8,128)(2,1)S(1)}, bf16[24,1792]{1,0:T(8,128)(2,1)S(1)}, u32[]{:S(2)}, u32[]{:S(2)}) collective-permute-start(bf16[24,1792]{1,0:T(8,128)(2,1)S(1)} %collective-permute-done.2.refs_7_), channel_id=1, source_target_pairs={{0,1},{1,0},{2,3},{3,2},{4,5},{5,4},{6,7},{7,6},{8,9},{9,8},{10,11... | collective-permute-start | bytes 258056 | tf_op jit(solution)/shard_map/ppermute | solution.py:252
  29.5 7.8 %collective-permute-start.1 = (bf16[24,1792]{1,0:T(8,128)(2,1)S(1)}, bf16[24,1792]{1,0:T(8,128)(2,1)S(1)}, u32[]{:S(2)}, u32[]{:S(2)}) collective-permute-start(bf16[24,1792]{1,0:T(8,128)(2,1)S(1)} %collective-permute-done.refs_6_), channel_id=1, source_target_pairs={{0,1},{1,0},{2,3},{3,2},{4,5},{5,4},{6,7},{7,6},{8,9},{9,8},{10,11... | collective-permute-start | bytes 258056 | tf_op jit(solution)/shard_map/ppermute | solution.py:252
  30.0 1.5 %copy-start.1 = (bf16[7168,128]{1,0:T(8,128)(2,1)S(1)}, bf16[7168,128]{1,0:T(8,128)(2,1)}, u32[]{:S(2)}) copy-start(bf16[7168,128]{1,0:T(8,128)(2,1)} %refs_9_.3) | copy-start | bytes 5505028
  31.5 5.7 %copy-start.2 = (bf16[7168,128]{1,0:T(8,128)(2,1)S(1)}, bf16[7168,128]{1,0:T(8,128)(2,1)}, u32[]{:S(2)}) copy-start(bf16[7168,128]{1,0:T(8,128)(2,1)} %refs_9_.3) | copy-start | bytes 5505028
  35.1 7.7 %collective-permute-start.20 = (bf16[48,1792]{1,0:T(8,128)(2,1)S(1)}, bf16[48,1792]{1,0:T(8,128)(2,1)S(1)}, u32[]{:S(2)}, u32[]{:S(2)}) collective-permute-start(bf16[48,1792]{1,0:T(8,128)(2,1)S(1)} %get-tuple-element.21), channel_id=1, source_target_pairs={{0,1},{1,0},{2,3},{3,2},{4,5},{5,4},{6,7},{7,6},{8,9},{9,8},{10,11... | collective-permute-start | bytes 516104 | tf_op jit(solution)/shard_map/ppermute | solution.py:252
  36.7 9.1 %collective-permute-start.22 = (bf16[48,1792]{1,0:T(8,128)(2,1)S(1)}, bf16[48,1792]{1,0:T(8,128)(2,1)S(1)}, u32[]{:S(2)}, u32[]{:S(2)}) collective-permute-start(bf16[48,1792]{1,0:T(8,128)(2,1)S(1)} %get-tuple-element.22), channel_id=1, source_target_pairs={{0,1},{1,0},{2,3},{3,2},{4,5},{5,4},{6,7},{7,6},{8,9},{9,8},{10,11... | collective-permute-start | bytes 516104 | tf_op jit(solution)/shard_map/ppermute | solution.py:252
  40.7 8.7 %collective-permute-start.7 = (bf16[48,1792]{1,0:T(8,128)(2,1)S(1)}, bf16[48,1792]{1,0:T(8,128)(2,1)S(1)}, u32[]{:S(2)}, u32[]{:S(2)}) collective-permute-start(bf16[48,1792]{1,0:T(8,128)(2,1)S(1)} %get-tuple-element.17), channel_id=1, source_target_pairs={{0,1},{1,0},{2,3},{3,2},{4,5},{5,4},{6,7},{7,6},{8,9},{9,8},{10,11... | collective-permute-start | bytes 516104 | tf_op jit(solution)/shard_map/ppermute | solution.py:252
  42.3 8.9 %collective-permute-start.9 = (bf16[48,1792]{1,0:T(8,128)(2,1)S(1)}, bf16[48,1792]{1,0:T(8,128)(2,1)S(1)}, u32[]{:S(2)}, u32[]{:S(2)}) collective-permute-start(bf16[48,1792]{1,0:T(8,128)(2,1)S(1)} %get-tuple-element.18), channel_id=1, source_target_pairs={{0,1},{1,0},{2,3},{3,2},{4,5},{5,4},{6,7},{7,6},{8,9},{9,8},{10,11... | collective-permute-start | bytes 516104 | tf_op jit(solution)/shard_map/ppermute | solution.py:252
  45.9 7.8 %collective-permute-start.23 = (bf16[24,1792]{1,0:T(8,128)(2,1)S(1)}, bf16[24,1792]{1,0:T(8,128)(2,1)S(1)}, u32[]{:S(2)}, u32[]{:S(2)}) collective-permute-start(bf16[24,1792]{1,0:T(8,128)(2,1)S(1)} %get-tuple-element.25), channel_id=1, source_target_pairs={{0,4},{1,5},{2,6},{3,7},{4,0},{5,1},{6,2},{7,3},{8,12},{9,13},{10,... | collective-permute-start | bytes 258056 | tf_op jit(solution)/shard_map/ppermute | solution.py:252
  48.0 7.8 %collective-permute-start.24 = (bf16[24,1792]{1,0:T(8,128)(2,1)S(1)}, bf16[24,1792]{1,0:T(8,128)(2,1)S(1)}, u32[]{:S(2)}, u32[]{:S(2)}) collective-permute-start(bf16[24,1792]{1,0:T(8,128)(2,1)S(1)} %get-tuple-element.26), channel_id=1, source_target_pairs={{0,6},{1,7},{2,4},{3,5},{4,2},{5,3},{6,0},{7,1},{8,14},{9,15},{10,... | collective-permute-start | bytes 258056 | tf_op jit(solution)/shard_map/ppermute | solution.py:252
  48.8 7.0 %collective-permute-start.21 = (bf16[24,1792]{1,0:T(8,128)(2,1)S(1)}, bf16[24,1792]{1,0:T(8,128)(2,1)S(1)}, u32[]{:S(2)}, u32[]{:S(2)}) collective-permute-start(bf16[24,1792]{1,0:T(8,128)(2,1)S(1)} %get-tuple-element.29), channel_id=1, source_target_pairs={{0,2},{1,3},{2,0},{3,1},{4,6},{5,7},{6,4},{7,5},{8,10},{9,11},{10,... | collective-permute-start | bytes 258056 | tf_op jit(solution)/shard_map/ppermute | solution.py:252
  51.3 7.3 %collective-permute-start.11 = (bf16[24,1792]{1,0:T(8,128)(2,1)S(1)}, bf16[24,1792]{1,0:T(8,128)(2,1)S(1)}, u32[]{:S(2)}, u32[]{:S(2)}) collective-permute-start(bf16[24,1792]{1,0:T(8,128)(2,1)S(1)} %get-tuple-element.27), channel_id=1, source_target_pairs={{0,6},{1,7},{2,4},{3,5},{4,2},{5,3},{6,0},{7,1},{8,14},{9,15},{10,... | collective-permute-start | bytes 258056 | tf_op jit(solution)/shard_map/ppermute | solution.py:252
  53.7 7.6 %collective-permute-start.10 = (bf16[24,1792]{1,0:T(8,128)(2,1)S(1)}, bf16[24,1792]{1,0:T(8,128)(2,1)S(1)}, u32[]{:S(2)}, u32[]{:S(2)}) collective-permute-start(bf16[24,1792]{1,0:T(8,128)(2,1)S(1)} %get-tuple-element.28), channel_id=1, source_target_pairs={{0,4},{1,5},{2,6},{3,7},{4,0},{5,1},{6,2},{7,3},{8,12},{9,13},{10,... | collective-permute-start | bytes 258056 | tf_op jit(solution)/shard_map/ppermute | solution.py:252
  53.7 7.6 %collective-permute-start.8 = (bf16[24,1792]{1,0:T(8,128)(2,1)S(1)}, bf16[24,1792]{1,0:T(8,128)(2,1)S(1)}, u32[]{:S(2)}, u32[]{:S(2)}) collective-permute-start(bf16[24,1792]{1,0:T(8,128)(2,1)S(1)} %get-tuple-element.30), channel_id=1, source_target_pairs={{0,2},{1,3},{2,0},{3,1},{4,6},{5,7},{6,4},{7,5},{8,10},{9,11},{10,... | collective-permute-start | bytes 258056 | tf_op jit(solution)/shard_map/ppermute | solution.py:252
  55.8 5.5 %collective-permute-start.25 = (bf16[24,1792]{1,0:T(8,128)(2,1)S(1)}, bf16[24,1792]{1,0:T(8,128)(2,1)S(1)}, u32[]{:S(2)}, u32[]{:S(2)}) collective-permute-start(bf16[24,1792]{1,0:T(8,128)(2,1)S(1)} %add_convert_fusion), channel_id=1, source_target_pairs={{0,8},{8,0},{1,9},{9,1},{2,10},{10,2},{3,11},{11,3},{4,12},{12,4},... | collective-permute-start | bytes 258056 | tf_op jit(solution)/shard_map/ppermute | solution.py:256

commit v2 on v0

v2 whole, which is shorter than its diff:
```python
import jax
import jax.numpy as jnp
from jax import lax
from jax.experimental import pallas as pl
from jax.experimental.pallas import tpu as pltpu
from jax.sharding import PartitionSpec as P

SPLIT = 8
MOST = 6
SEGS = 4
ROWS = SEGS * MOST
BF = jnp.bfloat16
F32 = jnp.float32
MIB = 1024 * 1024


def route_table(expert_ids, route_weights, experts_win):
    window = jnp.arange(experts_win, dtype=jnp.int32)
    matched = expert_ids[:, :, None] == window[None, None, :]
    is_hit = jnp.any(matched, axis=1).astype(jnp.int32)
    weight = jnp.sum(jnp.where(matched, route_weights[:, :, None], F32(0.0)), axis=1)
    position = jnp.cumsum(is_hit, axis=0) - 1
    slot_index = jnp.arange(MOST, dtype=jnp.int32)
    select = (is_hit.T[:, None, :] == 1) & (position.T[:, None, :] == slot_index[None, :, None])
    return (select, weight)


def general(tokens, expert_ids, route_weights, gate_weight, up_weight, down_weight):
    host_count = lax.axis_size("hst")
    local_count = lax.axis_size("local")
    per_host = local_count // SPLIT
    experts_win = host_count * per_host
    width = tokens.shape[1]
    select, weight = route_table(expert_ids, route_weights, experts_win)
    outgoing = jnp.einsum(
        "wmt,td->wmd", select.astype(BF), tokens, preferred_element_type=F32
    ).astype(BF)
    slot_weight = jnp.einsum(
        "wmt,tw->wm", select.astype(F32), weight, precision=lax.Precision.HIGHEST
    )
    host_rows = lax.all_to_all(
        outgoing.reshape(host_count, per_host, MOST, width), "hst", 0, 0, tiled=True
    )
    spread = jnp.repeat(jnp.transpose(host_rows, (1, 0, 2, 3)), SPLIT, axis=0)
    row_block = lax.all_to_all(spread, "local", 0, 0, tiled=True)
    in_shape = row_block.shape
    flattened = row_block.reshape(-1, width)
    gate_sum = jnp.dot(flattened, gate_weight, preferred_element_type=F32)
    up_sum = jnp.dot(flattened, up_weight, preferred_element_type=F32)
    hidden = (jax.nn.silu(gate_sum) * up_sum).astype(BF)
    partial_value = jnp.dot(hidden, down_weight, preferred_element_type=F32).astype(BF)
    partial_value = partial_value.reshape(in_shape)
    returned_rows = lax.all_to_all(partial_value, "local", 0, 0, tiled=True)
    summed = jnp.sum(
        returned_rows.reshape(per_host, SPLIT, host_count, MOST, width).astype(F32), axis=1
    )
    returned_sums = lax.all_to_all(
        jnp.transpose(summed, (1, 0, 2, 3)), "hst", 0, 0, tiled=True
    )
    combined = returned_sums.reshape(experts_win, MOST, width)
    weighted = combined * slot_weight[:, :, None]
    total = jnp.einsum(
        "wmt,wmd->td", select.astype(F32), weighted, precision=lax.Precision.HIGHEST
    )
    return total.astype(BF)


def in_hbm(x):
    return pltpu.with_memory_space_constraint(x, pltpu.HBM)


def join(*arrays):
    many = len(arrays)

    def kernel(*refs):
        pass

    return pl.pallas_call(
        kernel,
        in_specs=[pl.BlockSpec(memory_space=pltpu.VMEM)] * many,
        out_specs=[pl.BlockSpec(memory_space=pltpu.VMEM)] * many,
        out_shape=[jax.ShapeDtypeStruct(x.shape, x.dtype) for x in arrays],
        input_output_aliases={i: i for i in range(many)},
        compiler_params=pltpu.CompilerParams(vmem_limit_bytes=8 * MIB),
        name="join",
    )(*arrays)


def load_weights(gate_weight, up_weight, down_weight):
    width, units = gate_weight.shape
    seg = width // SEGS

    def kernel(gate_hbm, up_hbm, down_hbm, both_ref, down_ref, sems):
        copies = [
            pltpu.make_async_copy(gate_hbm, both_ref.at[:, pl.ds(0, units)], sems.at[0]),
            pltpu.make_async_copy(up_hbm, both_ref.at[:, pl.ds(units, units)], sems.at[1]),
        ]
        for s in range(SEGS):
            copies.append(
                pltpu.make_async_copy(
                    down_hbm.at[:, pl.ds(s * seg, seg)],
                    down_ref.at[pl.ds(s * units, units), :],
                    sems.at[2 + s],
                )
            )
        for copy in copies:
            copy.start()
        for copy in copies:
            copy.wait()

    return pl.pallas_call(
        kernel,
        in_specs=[pl.BlockSpec(memory_space=pltpu.HBM)] * 3,
        out_specs=[pl.BlockSpec(memory_space=pltpu.VMEM)] * 2,
        out_shape=[
            jax.ShapeDtypeStruct((width, 2 * units), BF),
            jax.ShapeDtypeStruct((SEGS * units, seg), BF),
        ],
        scratch_shapes=[pltpu.SemaphoreType.DMA((2 + SEGS,))],
        compiler_params=pltpu.CompilerParams(vmem_limit_bytes=12 * MIB),
        name="load_weights",
    )(*[in_hbm(x) for x in (gate_weight, up_weight, down_weight)])


def select_rows(core, tokens, ids_t, weights_t):
    count, width = tokens.shape
    seg = width // SEGS
    topk = ids_t.shape[0]

    def kernel(
        core_ref, ids_hbm, weights_hbm, tokens_hbm,
        own_ref, twin_ref, slot_ref, scale_ref,
        ids_ref, weights_ref, tokens_ref, small_sem, sems,
    ):
        first = pltpu.make_async_copy(ids_hbm, ids_ref, small_sem.at[0])
        second = pltpu.make_async_copy(weights_hbm, weights_ref, small_sem.at[1])
        first.start()
        second.start()
        copies = [
            pltpu.make_async_copy(
                tokens_hbm.at[:, pl.ds(s * seg, seg)], tokens_ref.at[s], sems.at[s]
            )
            for s in range(SEGS)
        ]
        for copy in copies:
            copy.start()
        core = core_ref[0]
        row = lax.broadcasted_iota(jnp.int32, (count, count), 0)
        col = lax.broadcasted_iota(jnp.int32, (count, count), 1)
        before = (row < col).astype(BF)
        slot = lax.broadcasted_iota(jnp.int32, (ROWS, count), 0) % MOST
        line = lax.broadcasted_iota(jnp.int32, (2 * ROWS, count), 0) % ROWS // MOST
        first.wait()
        second.wait()
        ids = ids_ref[...]
        tables = []
        for part in range(2):
            expert = core if part == 0 else 1 - core
            named = ids == expert
            hit = jnp.max(named.astype(F32), axis=0, keepdims=True)
            weight = jnp.sum(jnp.where(named, weights_ref[...], 0.0), axis=0, keepdims=True)
            wide = jnp.broadcast_to(hit, (16, count)).astype(BF)
            position = jnp.dot(wide, before, preferred_element_type=F32)[0:1]
            table = ((hit > 0.0) & (position.astype(jnp.int32) == slot)).astype(F32)
            slot_ref[part] = table
            scale = jnp.sum(table * weight, axis=1, keepdims=True)
            scale_ref[part] = jnp.broadcast_to(scale, (ROWS, 128))
            tables.append(table)
        table = jnp.concatenate(tables, axis=0)
        rows = jnp.zeros((2 * ROWS, seg), F32)
        for s in range(SEGS):
            copies[s].wait()
            chosen = jnp.where(line == s, table, 0.0).astype(BF)
            rows = rows + jnp.dot(chosen, tokens_ref[s], preferred_element_type=F32)
        own_ref[...] = rows[:ROWS].astype(BF)
        twin_ref[...] = rows[ROWS:].astype(BF)

    return pl.pallas_call(
        kernel,
        in_specs=[pl.BlockSpec(memory_space=pltpu.SMEM)] + [pl.BlockSpec(memory_space=pltpu.HBM)] * 3,
        out_specs=[pl.BlockSpec(memory_space=pltpu.VMEM)] * 4,
        out_shape=[
            jax.ShapeDtypeStruct((ROWS, seg), BF),
            jax.ShapeDtypeStruct((ROWS, seg), BF),
            jax.ShapeDtypeStruct((2, ROWS, count), F32),
            jax.ShapeDtypeStruct((2, ROWS, 128), F32),
        ],
        scratch_shapes=[
            pltpu.VMEM((topk, count), jnp.int32),
            pltpu.VMEM((topk, count), F32),
            pltpu.VMEM((SEGS, count, seg), BF),
            pltpu.SemaphoreType.DMA((2,)),
            pltpu.SemaphoreType.DMA((SEGS,)),
        ],
        compiler_params=pltpu.CompilerParams(vmem_limit_bytes=12 * MIB),
        name="select_rows",
    )(core, *[in_hbm(x) for x in (ids_t, weights_t, tokens)])


def experts(blocks, both_weight, down_weight):
    many = len(blocks)
    tall, seg = blocks[0].shape
    units = both_weight.shape[1] // 2
    height = many * tall
    tile = 256

    def kernel(*refs):
        block_refs = refs[:many]
        both_ref, down_ref = refs[many : many + 2]
        out_refs = refs[many + 2 :]
        rows = jnp.concatenate([ref[...] for ref in block_refs], axis=0)
        line = lax.broadcasted_iota(jnp.int32, (height, 2 * units), 0) % ROWS // MOST
        total = jnp.zeros((height, 2 * units), F32)
        for s in range(SEGS):
            cut = slice(s * seg, (s + 1) * seg)
            part = jnp.dot(rows, both_ref[cut, :], preferred_element_type=F32)
            total = total + jnp.where(line == s, part, 0.0)
        one = lax.broadcasted_iota(jnp.int32, (tall, tall), 0)
        two = lax.broadcasted_iota(jnp.int32, (tall, tall), 1)
        same = ((one // ROWS == two // ROWS) & (one % MOST == two % MOST)).astype(F32)
        spread = jnp.concatenate(
            [
                jnp.dot(
                    same,
                    total[b * tall : (b + 1) * tall],
                    precision=lax.Precision.HIGHEST,
                    preferred_element_type=F32,
                )
                for b in range(many)
            ],
            axis=0,
        )
        gate = spread[:, :units]
        up = spread[:, units:]
        hidden = gate / (1.0 + jnp.exp(-gate)) * up
        wide = jnp.concatenate(
            [jnp.where(line[:, :units] == s, hidden, 0.0) for s in range(SEGS)], axis=1
        ).astype(BF)
        for j in range(seg // tile):
            cut = slice(j * tile, (j + 1) * tile)
            out = jnp.dot(wide, down_ref[:, cut], preferred_element_type=F32).astype(BF)
            for b in range(many):
                out_refs[b][:, cut] = out[b * tall : (b + 1) * tall]

    return pl.pallas_call(
        kernel,
        in_specs=[pl.BlockSpec(memory_space=pltpu.VMEM)] * (many + 2),
        out_specs=[pl.BlockSpec(memory_space=pltpu.VMEM)] * many,
        out_shape=[jax.ShapeDtypeStruct((tall, seg), BF)] * many,
        compiler_params=pltpu.CompilerParams(vmem_limit_bytes=24 * MIB),
        cost_estimate=pl.CostEstimate(
            flops=2 * height * seg * SEGS * units * 3,
            bytes_accessed=3 * 2 * units * seg * SEGS,
            transcendentals=0,
        ),
        name="experts",
    )(*blocks, both_weight, down_weight)


def combine(own_terms, twin, slot, scale):
    seg = twin.shape[1]
    count = slot.shape[2]
    terms = len(own_terms)

    def kernel(*refs):
        term_refs = refs[:terms]
        twin_ref, slot_ref, scale_ref, out_ref, stage, sems = refs[terms:]
        own = term_refs[0][0:ROWS].astype(F32)
        for ref in term_refs[1:]:
            own = own + ref[0:ROWS].astype(F32)
        own = own * scale_ref[0][:, 0:1]
        other = twin_ref[...].astype(F32) * scale_ref[1][:, 0:1]
        both = jnp.concatenate([own, other], axis=0)
        high = both.astype(BF)
        low = (both - high.astype(F32)).astype(BF)
        rows = jnp.concatenate([high, low], axis=0)
        table = jnp.concatenate([slot_ref[0], slot_ref[1]], axis=0)
        table = jnp.concatenate([table, table], axis=0).T
        line = lax.broadcasted_iota(jnp.int32, (count, 4 * ROWS), 1) % ROWS // MOST
        copies = []
        for s in range(SEGS):
            chosen = jnp.where(line == s, table, 0.0).astype(BF)
            stage[s] = jnp.dot(chosen, rows, preferred_element_type=F32).astype(BF)
            copy = pltpu.make_async_copy(
                stage.at[s], out_ref.at[:, pl.ds(s * seg, seg)], sems.at[s]
            )
            copy.start()
            copies.append(copy)
        for copy in copies:
            copy.wait()

    return pl.pallas_call(
        kernel,
        in_specs=[pl.BlockSpec(memory_space=pltpu.VMEM)] * (terms + 3),
        out_specs=pl.BlockSpec(memory_space=pltpu.HBM),
        out_shape=jax.ShapeDtypeStruct((count, seg * SEGS), BF),
        scratch_shapes=[
            pltpu.VMEM((SEGS, count, seg), BF),
            pltpu.SemaphoreType.DMA((SEGS,)),
        ],
        compiler_params=pltpu.CompilerParams(vmem_limit_bytes=16 * MIB),
        name="combine",
    )(*own_terms, twin, slot, scale)


def swap(x, mask):
    return lax.ppermute(x, "local", [(i, i ^ mask) for i in range(SPLIT)])


def swap_cores(x):
    return lax.ppermute(x, "hst", [(0, 1), (1, 0)])


def add(*terms):
    return sum(x.astype(F32) for x in terms).astype(BF)


def single(tokens, expert_ids, route_weights, gate_weight, up_weight, down_weight):
    core = lax.axis_index("hst").astype(jnp.int32).reshape(1)
    own, other, slot, scale = select_rows(core, tokens, expert_ids.T, route_weights.T)
    block = jnp.concatenate([own, swap_cores(other)], axis=0)
    loaded = load_weights(gate_weight, up_weight, down_weight)
    six, two, one, *loaded = join(swap(block, 6), swap(block, 2), swap(block, 1), *loaded)
    four, seven = join(swap(six, 2), swap(six, 1))
    five, three = swap(four, 1), swap(one, 2)
    part7, part6 = experts([seven, six], *loaded)
    part0, part1, part2 = experts([block, one, two], *loaded)
    part5, part4, part3 = experts([five, four, three], *loaded)
    half = add(part5, swap(part7, 2))
    far = swap(add(part4, swap(part6, 2), swap(half, 1)), 4)
    near = swap(add(part2, swap(part3, 1)), 2)
    terms = (part0, swap(part1, 1), near, far)
    back = sum(x[ROWS:].astype(F32) for x in terms)
    back = swap_cores(back.astype(BF))
    return combine(terms, back, slot, scale)


def solution(mesh):
    in_specs = (
        P(("groups", "hst", "local"), None),
        P(("groups", "hst", "local"), None),
        P(("groups", "hst", "local"), None),
        P(None, ("hst", "local")),
        P(None, ("hst", "local")),
        P(("hst", "local"), None),
    )
    out_specs = P(("groups", "hst", "local"), None)
    body = single if mesh.shape["local"] == SPLIT and mesh.shape["hst"] == 2 else general
    return jax.shard_map(
        body, mesh=mesh, in_specs=in_specs, out_specs=out_specs, check_vma=False
    )
```

time: 109 us -> 53 us (0.49)
  blocking collectives: 48.7 us -> 0 us
  starting transfers between devices: 3.7 us -> 18.5 us
  local copies, waits for them, and re-layouts: 11.4 us -> 0.01 us
  matrix products: 10.5 us -> 0 us
  Pallas kernels: 0 us -> 10.3 us
  waiting for transfers between devices: 32 us -> 23.7 us
  other arithmetic: 2.47 us -> 0.2 us
    all_to_all x3 -> x0, blocking collectives: 48.7 us -> none  [the longest x1 40.8 us: on_device(): lax.all_to_all(spread, 'local', split_axis=0, concat_axis=0, tiled=True)]
    all_to_all x1 -> x0, waiting for transfers between devices: 32 us -> none  [on_device(): lax.all_to_all(partial_value, 'local', split_axis=0, concat_axis=0, tiled...]
    ppermute x0 -> x16, waiting for transfers between devices: none -> 23.7 us  [the longest x14 21.5 us: swap(): return lax.ppermute(x, 'local', [(i, i ^ mask) for i in range(SPLIT)])]
    ppermute x0 -> x16, starting transfers between devices: none -> 18.5 us  [the longest x14 18 us: swap(): return lax.ppermute(x, 'local', [(i, i ^ mask) for i in range(SPLIT)])]
    dot_general x5 -> x0, matrix products: 10.5 us -> none  [the longest x1 3.58 us: on_device(): jnp.dot(hidden, down_weight, preferred_element_type=jnp.float32)]
    pallas_call x0 -> x8, Pallas kernels: none -> 10.3 us  [the longest x3 4.21 us: experts(): pl.pallas_call(kernel, in_specs=[pl.BlockSpec(memory_space=pltpu.VMEM)] *...]
    reshape x4 -> x0, local copies, waits for them, and re-layouts: 9 us -> none  [the longest x2 6.57 us: on_device(): partial_value = partial_value.reshape(in_shape)]
    all_to_all x1 -> x0, starting transfers between devices: 3.7 us -> none  [on_device(): lax.all_to_all(partial_value, 'local', split_axis=0, concat_axis=0, tiled...]
  transfers between devices with their start and end apart: 1 -> 16, of which waited for: 1 -> 10; matrix products, arithmetic and copies ran while one was open for 0% -> 0% of each run, Pallas kernels for 0% -> 13%
where the time goes in v2:
time: 53 us; the launch traced here: 52.9 us
  waiting for transfers between devices  23.7 us (45%)
  starting transfers between devices  18.5 us (35%)
  Pallas kernels  10.3 us (19%)
    ppermute x14, waiting for transfers between devices, swap(): return lax.ppermute(x, 'local', [(i, i ^ mask) for i in range(SPLIT)])  21.5 us
    ppermute x14, starting transfers between devices, swap(): return lax.ppermute(x, 'local', [(i, i ^ mask) for i in range(SPLIT)])  18 us
    pallas_call x3, Pallas kernels, experts(): pl.pallas_call(kernel, in_specs=[pl.BlockSpec(memory_space=pltpu.VMEM)] *...  4.21 us
    pallas_call x1, Pallas kernels, load_weights(): pl.pallas_call(kernel, in_specs=[pl.BlockSpec(memory_space=pltpu.HBM)] *...  2.59 us
    ppermute x2, waiting for transfers between devices, swap_cores(): return lax.ppermute(x, 'hst', [(0, 1), (1, 0)])  2.19 us
    pallas_call x1, Pallas kernels, select_rows(): pl.pallas_call(kernel, in_specs=[pl.BlockSpec(memory_space=pltpu.SMEM)] +...  1.89 us
    pallas_call x1, Pallas kernels, combine(): pl.pallas_call(kernel, in_specs=[pl.BlockSpec(memory_space=pltpu.VMEM)] *...  1.63 us
  transfers between devices with their start and end apart: 16, of which 10 were waited for; matrix products, arithmetic and copies ran while one was open for 0% of the time, Pallas kernels for 13%

profile of v2, /device:TPU:0, one launch (start us, length us, event | category | flops | bytes accessed | tf_op | source)
XLA Modules:
  0.0 52.9 jit_solution(14466501914051868773)
XLA Ops:
  0.0 1.9 %select_rows.1 = (bf16[24,1792]{1,0:T(8,128)(2,1)S(1)}, bf16[24,1792]{1,0:T(8,128)(2,1)S(1)}, f32[2,24,128]{2,1,0:T(8,128)S(1)}, f32[2,24,128]{2,1,0:T(8,128)S(1)}) custom-call(s32[1]{0:T(128)} %bitcast.core_ref, s32[8,128]{1,0:T(8,128)} %bitcast.3, f32[8,128]{1,0:T(8,128)} %bitcast.4, bf16[128,7168]{1,0:T(8,128)(2,1)} %tokens_hbm.1), custom_call_target="tpu_custom_call" | custom-call | tf_op jit(solution)/shard_map/select_rows/pallas_call | solution.py:178
  1.9 0.5 collective-permute-start
  2.4 0.9 %collective-permute-done = bf16[24,1792]{1,0:T(8,128)(2,1)S(1)} collective-permute-done((bf16[24,1792]{1,0:T(8,128)(2,1)S(1)}, bf16[24,1792]{1,0:T(8,128)(2,1)S(1)}, u32[]{:S(2)}, u32[]{:S(2)}) %collective-permute-start) | collective-permute-done | bytes 86048 | tf_op jit(solution)/shard_map/ppermute | solution.py:311
  3.4 2.9 %collective-permute-start.3 = (bf16[48,1792]{1,0:T(8,128)(2,1)S(1)}, bf16[48,1792]{1,0:T(8,128)(2,1)S(1)}, u32[]{:S(2)}, u32[]{:S(2)}) collective-permute-start(bf16[48,1792]{1,0:T(8,128)(2,1)S(1)} %constant_dynamic-update-slice_fusion.refs_0_), channel_id=1, source_target_pairs={{0,1},{1,0},{2,3},{3,2},{4,5},{5,4},{6,7},{7,6},{8,9},{9,8},{10,11... | collective-permute-start | bytes 516104 | tf_op jit(solution)/shard_map/ppermute | solution.py:307
  6.3 1.6 %collective-permute-start.2 = (bf16[48,1792]{1,0:T(8,128)(2,1)S(1)}, bf16[48,1792]{1,0:T(8,128)(2,1)S(1)}, u32[]{:S(2)}, u32[]{:S(2)}) collective-permute-start(bf16[48,1792]{1,0:T(8,128)(2,1)S(1)} %constant_dynamic-update-slice_fusion.refs_0_), channel_id=1, source_target_pairs={{0,2},{1,3},{2,0},{3,1},{4,6},{5,7},{6,4},{7,5},{8,10},{9,11},{10,... | collective-permute-start | bytes 516104 | tf_op jit(solution)/shard_map/ppermute | solution.py:307
  7.9 2.5 %collective-permute-start.1 = (bf16[48,1792]{1,0:T(8,128)(2,1)S(1)}, bf16[48,1792]{1,0:T(8,128)(2,1)S(1)}, u32[]{:S(2)}, u32[]{:S(2)}) collective-permute-start(bf16[48,1792]{1,0:T(8,128)(2,1)S(1)} %constant_dynamic-update-slice_fusion.refs_0_), channel_id=1, source_target_pairs={{0,6},{1,7},{2,4},{3,5},{4,2},{5,3},{6,0},{7,1},{8,14},{9,15},{10,... | collective-permute-start | bytes 516104 | tf_op jit(solution)/shard_map/ppermute | solution.py:307
  10.3 2.6 %load_weights.1 = (bf16[7168,256]{1,0:T(8,128)(2,1)S(1)}, bf16[512,1792]{1,0:T(8,128)(2,1)S(1)}) custom-call(bf16[7168,128]{1,0:T(8,128)(2,1)} %gate_hbm.1, bf16[7168,128]{1,0:T(8,128)(2,1)} %up_hbm.1, bf16[128,7168]{1,0:T(8,128)(2,1)} %down_hbm.1), custom_call_target="tpu_custom_call" | custom-call | tf_op jit(solution)/shard_map/load_weights/pallas_call | solution.py:111
  12.9 0.0 collective-permute-done.3.refs_2_
  12.9 0.0 collective-permute-done.2.refs_1_
  12.9 5.2 %collective-permute-done.1.refs_0_ = bf16[48,1792]{1,0:T(8,128)(2,1)S(1)} collective-permute-done((bf16[48,1792]{1,0:T(8,128)(2,1)S(1)}, bf16[48,1792]{1,0:T(8,128)(2,1)S(1)}, u32[]{:S(2)}, u32[]{:S(2)}) %collective-permute-start.1) | collective-permute-done | bytes 172064 | tf_op jit(solution)/shard_map/ppermute | solution.py:307
  18.2 0.5 collective-permute-start.6
  18.7 0.6 %collective-permute-start.5 = (bf16[48,1792]{1,0:T(8,128)(2,1)S(1)}, bf16[48,1792]{1,0:T(8,128)(2,1)S(1)}, u32[]{:S(2)}, u32[]{:S(2)}) collective-permute-start(bf16[48,1792]{1,0:T(8,128)(2,1)S(1)} %get-tuple-element.37.refs_1_), channel_id=1, source_target_pairs={{0,2},{1,3},{2,0},{3,1},{4,6},{5,7},{6,4},{7,5},{8,10},{9,11},{10,... | collective-permute-start | bytes 516104 | tf_op jit(solution)/shard_map/ppermute | solution.py:307
  19.3 1.5 %collective-permute-start.8 = (bf16[48,1792]{1,0:T(8,128)(2,1)S(1)}, bf16[48,1792]{1,0:T(8,128)(2,1)S(1)}, u32[]{:S(2)}, u32[]{:S(2)}) collective-permute-start(bf16[48,1792]{1,0:T(8,128)(2,1)S(1)} %get-tuple-element.30.refs_1_), channel_id=1, source_target_pairs={{0,2},{1,3},{2,0},{3,1},{4,6},{5,7},{6,4},{7,5},{8,10},{9,11},{10,... | collective-permute-start | bytes 516104 | tf_op jit(solution)/shard_map/ppermute | solution.py:307
  20.7 2.9 %collective-permute-done.6.refs_1_ = bf16[48,1792]{1,0:T(8,128)(2,1)S(1)} collective-permute-done((bf16[48,1792]{1,0:T(8,128)(2,1)S(1)}, bf16[48,1792]{1,0:T(8,128)(2,1)S(1)}, u32[]{:S(2)}, u32[]{:S(2)}) %collective-permute-start.6) | collective-permute-done | bytes 172064 | tf_op jit(solution)/shard_map/ppermute | solution.py:307
  23.6 1.8 %collective-permute-done.5.refs_0_ = bf16[48,1792]{1,0:T(8,128)(2,1)S(1)} collective-permute-done((bf16[48,1792]{1,0:T(8,128)(2,1)S(1)}, bf16[48,1792]{1,0:T(8,128)(2,1)S(1)}, u32[]{:S(2)}, u32[]{:S(2)}) %collective-permute-start.5) | collective-permute-done | bytes 172064 | tf_op jit(solution)/shard_map/ppermute | solution.py:307
  25.4 1.5 %collective-permute-start.7 = (bf16[48,1792]{1,0:T(8,128)(2,1)S(1)}, bf16[48,1792]{1,0:T(8,128)(2,1)S(1)}, u32[]{:S(2)}, u32[]{:S(2)}) collective-permute-start(bf16[48,1792]{1,0:T(8,128)(2,1)S(1)} %get-tuple-element.38.refs_1_), channel_id=1, source_target_pairs={{0,1},{1,0},{2,3},{3,2},{4,5},{5,4},{6,7},{7,6},{8,9},{9,8},{10,11... | collective-permute-start | bytes 516104 | tf_op jit(solution)/shard_map/ppermute | solution.py:307
  26.9 1.4 %experts.5 = (bf16[48,1792]{1,0:T(8,128)(2,1)S(1)}, bf16[48,1792]{1,0:T(8,128)(2,1)S(1)}) custom-call(bf16[48,1792]{1,0:T(8,128)(2,1)S(1)} %get-tuple-element.41.refs_0_, bf16[48,1792]{1,0:T(8,128)(2,1)S(1)} %get-tuple-element.37.refs_1_, bf16[7168,256]{1,0:T(8,128)(2,1)S(1)} %get-tuple-element.32.refs_3_.refs_2_, ...), custom_call_target="tpu_custom_call" | custom-call | flops 528482304 | bytes 5505024 | tf_op jit(solution)/shard_map/experts/pallas_call | solution.py:245
  28.3 0.4 collective-permute-start.12
  28.7 1.4 %experts.3 = (bf16[48,1792]{1,0:T(8,128)(2,1)S(1)}, bf16[48,1792]{1,0:T(8,128)(2,1)S(1)}, bf16[48,1792]{1,0:T(8,128)(2,1)S(1)}) custom-call(bf16[48,1792]{1,0:T(8,128)(2,1)S(1)} %constant_dynamic-update-slice_fusion.refs_0_, bf16[48,1792]{1,0:T(8,128)(2,1)S(1)} %get-tuple-element.30.refs_1_, bf16[48,1792]{1,0:T(8,128)(2,1)S(1)} %get-tuple-element.31.refs_2_, ...), custom_call_target="tpu_custom_call" | custom-call | flops 792723456 | bytes 5505024 | tf_op jit(solution)/shard_map/experts/pallas_call | solution.py:245
  30.1 0.6 %collective-permute-start.4 = (bf16[48,1792]{1,0:T(8,128)(2,1)S(1)}, bf16[48,1792]{1,0:T(8,128)(2,1)S(1)}, u32[]{:S(2)}, u32[]{:S(2)}) collective-permute-start(bf16[48,1792]{1,0:T(8,128)(2,1)S(1)} %get-tuple-element.35), channel_id=1, source_target_pairs={{0,1},{1,0},{2,3},{3,2},{4,5},{5,4},{6,7},{7,6},{8,9},{9,8},{10,11... | collective-permute-start | bytes 516104 | tf_op jit(solution)/shard_map/ppermute | solution.py:307
  30.7 1.7 %collective-permute-start.11 = (bf16[48,1792]{1,0:T(8,128)(2,1)S(1)}, bf16[48,1792]{1,0:T(8,128)(2,1)S(1)}, u32[]{:S(2)}, u32[]{:S(2)}) collective-permute-start(bf16[48,1792]{1,0:T(8,128)(2,1)S(1)} %get-tuple-element.42), channel_id=1, source_target_pairs={{0,2},{1,3},{2,0},{3,1},{4,6},{5,7},{6,4},{7,5},{8,10},{9,11},{10,... | collective-permute-start | bytes 516104 | tf_op jit(solution)/shard_map/ppermute | solution.py:307
  32.4 0.0 collective-permute-done.8.refs_2_
  32.4 0.2 collective-permute-done.7.refs_0_
  32.6 1.4 %experts.4 = (bf16[48,1792]{1,0:T(8,128)(2,1)S(1)}, bf16[48,1792]{1,0:T(8,128)(2,1)S(1)}, bf16[48,1792]{1,0:T(8,128)(2,1)S(1)}) custom-call(bf16[48,1792]{1,0:T(8,128)(2,1)S(1)} %collective-permute-done.7.refs_0_, bf16[48,1792]{1,0:T(8,128)(2,1)S(1)} %get-tuple-element.38.refs_1_, bf16[48,1792]{1,0:T(8,128)(2,1)S(1)} %collective-permute-done.8.refs_2_, ...), custom_call_target="tpu_custom_call" | custom-call | flops 792723456 | bytes 5505024 | tf_op jit(solution)/shard_map/experts/pallas_call | solution.py:245
  34.0 1.4 %collective-permute-start.9 = (bf16[48,1792]{1,0:T(8,128)(2,1)S(1)}, bf16[48,1792]{1,0:T(8,128)(2,1)S(1)}, u32[]{:S(2)}, u32[]{:S(2)}) collective-permute-start(bf16[48,1792]{1,0:T(8,128)(2,1)S(1)} %get-tuple-element.39), channel_id=1, source_target_pairs={{0,1},{1,0},{2,3},{3,2},{4,5},{5,4},{6,7},{7,6},{8,9},{9,8},{10,11... | collective-permute-start | bytes 516104 | tf_op jit(solution)/shard_map/ppermute | solution.py:307
  35.4 0.0 collective-permute-done.12
  35.5 0.7 %collective-permute-start.13 = (bf16[48,1792]{1,0:T(8,128)(2,1)S(1)}, bf16[48,1792]{1,0:T(8,128)(2,1)S(1)}, u32[]{:S(2)}, u32[]{:S(2)}) collective-permute-start(bf16[48,1792]{1,0:T(8,128)(2,1)S(1)} %add_convert_fusion.1), channel_id=1, source_target_pairs={{0,1},{1,0},{2,3},{3,2},{4,5},{5,4},{6,7},{7,6},{8,9},{9,8},{10,11... | collective-permute-start | bytes 516104 | tf_op jit(solution)/shard_map/ppermute | solution.py:307
  36.2 3.5 %collective-permute-done.9 = bf16[48,1792]{1,0:T(8,128)(2,1)S(1)} collective-permute-done((bf16[48,1792]{1,0:T(8,128)(2,1)S(1)}, bf16[48,1792]{1,0:T(8,128)(2,1)S(1)}, u32[]{:S(2)}, u32[]{:S(2)}) %collective-permute-start.9) | collective-permute-done | bytes 172064 | tf_op jit(solution)/shard_map/ppermute | solution.py:307
  39.7 0.7 %collective-permute-start.10 = (bf16[48,1792]{1,0:T(8,128)(2,1)S(1)}, bf16[48,1792]{1,0:T(8,128)(2,1)S(1)}, u32[]{:S(2)}, u32[]{:S(2)}) collective-permute-start(bf16[48,1792]{1,0:T(8,128)(2,1)S(1)} %add_convert_fusion.2), channel_id=1, source_target_pairs={{0,2},{1,3},{2,0},{3,1},{4,6},{5,7},{6,4},{7,5},{8,10},{9,11},{10,... | collective-permute-start | bytes 516104 | tf_op jit(solution)/shard_map/ppermute | solution.py:307
  40.4 0.0 collective-permute-done.11
  40.4 1.1 %collective-permute-done.13 = bf16[48,1792]{1,0:T(8,128)(2,1)S(1)} collective-permute-done((bf16[48,1792]{1,0:T(8,128)(2,1)S(1)}, bf16[48,1792]{1,0:T(8,128)(2,1)S(1)}, u32[]{:S(2)}, u32[]{:S(2)}) %collective-permute-start.13) | collective-permute-done | bytes 172064 | tf_op jit(solution)/shard_map/ppermute | solution.py:307
  41.5 0.1 add_convert_fusion
  41.6 1.4 %collective-permute-start.14 = (bf16[48,1792]{1,0:T(8,128)(2,1)S(1)}, bf16[48,1792]{1,0:T(8,128)(2,1)S(1)}, u32[]{:S(2)}, u32[]{:S(2)}) collective-permute-start(bf16[48,1792]{1,0:T(8,128)(2,1)S(1)} %add_convert_fusion), channel_id=1, source_target_pairs={{0,4},{1,5},{2,6},{3,7},{4,0},{5,1},{6,2},{7,3},{8,12},{9,13},{10,... | collective-permute-start | bytes 516104 | tf_op jit(solution)/shard_map/ppermute | solution.py:307
  43.0 0.0 collective-permute-done.4.refs_1_
  43.0 3.6 %collective-permute-done.10.refs_2_ = bf16[48,1792]{1,0:T(8,128)(2,1)S(1)} collective-permute-done((bf16[48,1792]{1,0:T(8,128)(2,1)S(1)}, bf16[48,1792]{1,0:T(8,128)(2,1)S(1)}, u32[]{:S(2)}, u32[]{:S(2)}) %collective-permute-start.10) | collective-permute-done | bytes 172064 | tf_op jit(solution)/shard_map/ppermute | solution.py:307
  46.6 3.2 %collective-permute-done.14.refs_3_ = bf16[48,1792]{1,0:T(8,128)(2,1)S(1)} collective-permute-done((bf16[48,1792]{1,0:T(8,128)(2,1)S(1)}, bf16[48,1792]{1,0:T(8,128)(2,1)S(1)}, u32[]{:S(2)}, u32[]{:S(2)}) %collective-permute-start.14) | collective-permute-done | bytes 172064 | tf_op jit(solution)/shard_map/ppermute | solution.py:307
  49.9 0.1 collective-permute-start.15
  50.0 1.3 %collective-permute-done.15.refs_4_ = bf16[24,1792]{1,0:T(8,128)(2,1)S(1)} collective-permute-done((bf16[24,1792]{1,0:T(8,128)(2,1)S(1)}, bf16[24,1792]{1,0:T(8,128)(2,1)S(1)}, u32[]{:S(2)}, u32[]{:S(2)}) %collective-permute-start.15) | collective-permute-done | bytes 86048 | tf_op jit(solution)/shard_map/ppermute | solution.py:311
  51.2 1.6 %combine.1 = bf16[128,7168]{1,0:T(8,128)(2,1)} custom-call(bf16[48,1792]{1,0:T(8,128)(2,1)S(1)} %get-tuple-element.34.refs_0_, bf16[48,1792]{1,0:T(8,128)(2,1)S(1)} %collective-permute-done.4.refs_1_, bf16[48,1792]{1,0:T(8,128)(2,1)S(1)} %collective-permute-done.10.refs_2_, bf16[48,1792]{1,0:T(8,128)(2,1)S(1)} %collective-permute-done.14.refs_3_, ...), custom_call_target="tpu_custom_call" | custom-call | tf_op jit(solution)/shard_map/combine/pallas_call | solution.py:292
  (7 shorter events, 0.1 us)
Async XLA Ops:
  1.9 1.4 %collective-permute-start = (bf16[24,1792]{1,0:T(8,128)(2,1)S(1)}, bf16[24,1792]{1,0:T(8,128)(2,1)S(1)}, u32[]{:S(2)}, u32[]{:S(2)}) collective-permute-start(bf16[24,1792]{1,0:T(8,128)(2,1)S(1)} %get-tuple-element.27), channel_id=1, source_target_pairs={{0,8},{8,0},{1,9},{9,1},{2,10},{10,2},{3,11},{11,3},{4,12},{12,4},... | collective-permute-start | bytes 258056 | tf_op jit(solution)/shard_map/ppermute | solution.py:311
  3.4 9.6 %collective-permute-start.3 = (bf16[48,1792]{1,0:T(8,128)(2,1)S(1)}, bf16[48,1792]{1,0:T(8,128)(2,1)S(1)}, u32[]{:S(2)}, u32[]{:S(2)}) collective-permute-start(bf16[48,1792]{1,0:T(8,128)(2,1)S(1)} %constant_dynamic-update-slice_fusion.refs_0_), channel_id=1, source_target_pairs={{0,1},{1,0},{2,3},{3,2},{4,5},{5,4},{6,7},{7,6},{8,9},{9,8},{10,11... | collective-permute-start | bytes 516104 | tf_op jit(solution)/shard_map/ppermute | solution.py:307
  6.3 6.7 %collective-permute-start.2 = (bf16[48,1792]{1,0:T(8,128)(2,1)S(1)}, bf16[48,1792]{1,0:T(8,128)(2,1)S(1)}, u32[]{:S(2)}, u32[]{:S(2)}) collective-permute-start(bf16[48,1792]{1,0:T(8,128)(2,1)S(1)} %constant_dynamic-update-slice_fusion.refs_0_), channel_id=1, source_target_pairs={{0,2},{1,3},{2,0},{3,1},{4,6},{5,7},{6,4},{7,5},{8,10},{9,11},{10,... | collective-permute-start | bytes 516104 | tf_op jit(solution)/shard_map/ppermute | solution.py:307
  7.9 10.3 %collective-permute-start.1 = (bf16[48,1792]{1,0:T(8,128)(2,1)S(1)}, bf16[48,1792]{1,0:T(8,128)(2,1)S(1)}, u32[]{:S(2)}, u32[]{:S(2)}) collective-permute-start(bf16[48,1792]{1,0:T(8,128)(2,1)S(1)} %constant_dynamic-update-slice_fusion.refs_0_), channel_id=1, source_target_pairs={{0,6},{1,7},{2,4},{3,5},{4,2},{5,3},{6,0},{7,1},{8,14},{9,15},{10,... | collective-permute-start | bytes 516104 | tf_op jit(solution)/shard_map/ppermute | solution.py:307
  18.2 5.4 %collective-permute-start.6 = (bf16[48,1792]{1,0:T(8,128)(2,1)S(1)}, bf16[48,1792]{1,0:T(8,128)(2,1)S(1)}, u32[]{:S(2)}, u32[]{:S(2)}) collective-permute-start(bf16[48,1792]{1,0:T(8,128)(2,1)S(1)} %get-tuple-element.37.refs_1_), channel_id=1, source_target_pairs={{0,1},{1,0},{2,3},{3,2},{4,5},{5,4},{6,7},{7,6},{8,9},{9,8},{10,11... | collective-permute-start | bytes 516104 | tf_op jit(solution)/shard_map/ppermute | solution.py:307
  18.7 6.7 %collective-permute-start.5 = (bf16[48,1792]{1,0:T(8,128)(2,1)S(1)}, bf16[48,1792]{1,0:T(8,128)(2,1)S(1)}, u32[]{:S(2)}, u32[]{:S(2)}) collective-permute-start(bf16[48,1792]{1,0:T(8,128)(2,1)S(1)} %get-tuple-element.37.refs_1_), channel_id=1, source_target_pairs={{0,2},{1,3},{2,0},{3,1},{4,6},{5,7},{6,4},{7,5},{8,10},{9,11},{10,... | collective-permute-start | bytes 516104 | tf_op jit(solution)/shard_map/ppermute | solution.py:307
  19.3 13.1 %collective-permute-start.8 = (bf16[48,1792]{1,0:T(8,128)(2,1)S(1)}, bf16[48,1792]{1,0:T(8,128)(2,1)S(1)}, u32[]{:S(2)}, u32[]{:S(2)}) collective-permute-start(bf16[48,1792]{1,0:T(8,128)(2,1)S(1)} %get-tuple-element.30.refs_1_), channel_id=1, source_target_pairs={{0,2},{1,3},{2,0},{3,1},{4,6},{5,7},{6,4},{7,5},{8,10},{9,11},{10,... | collective-permute-start | bytes 516104 | tf_op jit(solution)/shard_map/ppermute | solution.py:307
  25.4 7.2 %collective-permute-start.7 = (bf16[48,1792]{1,0:T(8,128)(2,1)S(1)}, bf16[48,1792]{1,0:T(8,128)(2,1)S(1)}, u32[]{:S(2)}, u32[]{:S(2)}) collective-permute-start(bf16[48,1792]{1,0:T(8,128)(2,1)S(1)} %get-tuple-element.38.refs_1_), channel_id=1, source_target_pairs={{0,1},{1,0},{2,3},{3,2},{4,5},{5,4},{6,7},{7,6},{8,9},{9,8},{10,11... | collective-permute-start | bytes 516104 | tf_op jit(solution)/shard_map/ppermute | solution.py:307
  28.3 7.1 %collective-permute-start.12 = (bf16[48,1792]{1,0:T(8,128)(2,1)S(1)}, bf16[48,1792]{1,0:T(8,128)(2,1)S(1)}, u32[]{:S(2)}, u32[]{:S(2)}) collective-permute-start(bf16[48,1792]{1,0:T(8,128)(2,1)S(1)} %get-tuple-element.44), channel_id=1, source_target_pairs={{0,2},{1,3},{2,0},{3,1},{4,6},{5,7},{6,4},{7,5},{8,10},{9,11},{10,... | collective-permute-start | bytes 516104 | tf_op jit(solution)/shard_map/ppermute | solution.py:307
  30.1 12.9 %collective-permute-start.4 = (bf16[48,1792]{1,0:T(8,128)(2,1)S(1)}, bf16[48,1792]{1,0:T(8,128)(2,1)S(1)}, u32[]{:S(2)}, u32[]{:S(2)}) collective-permute-start(bf16[48,1792]{1,0:T(8,128)(2,1)S(1)} %get-tuple-element.35), channel_id=1, source_target_pairs={{0,1},{1,0},{2,3},{3,2},{4,5},{5,4},{6,7},{7,6},{8,9},{9,8},{10,11... | collective-permute-start | bytes 516104 | tf_op jit(solution)/shard_map/ppermute | solution.py:307
  30.7 9.8 %collective-permute-start.11 = (bf16[48,1792]{1,0:T(8,128)(2,1)S(1)}, bf16[48,1792]{1,0:T(8,128)(2,1)S(1)}, u32[]{:S(2)}, u32[]{:S(2)}) collective-permute-start(bf16[48,1792]{1,0:T(8,128)(2,1)S(1)} %get-tuple-element.42), channel_id=1, source_target_pairs={{0,2},{1,3},{2,0},{3,1},{4,6},{5,7},{6,4},{7,5},{8,10},{9,11},{10,... | collective-permute-start | bytes 516104 | tf_op jit(solution)/shard_map/ppermute | solution.py:307
  34.0 5.7 %collective-permute-start.9 = (bf16[48,1792]{1,0:T(8,128)(2,1)S(1)}, bf16[48,1792]{1,0:T(8,128)(2,1)S(1)}, u32[]{:S(2)}, u32[]{:S(2)}) collective-permute-start(bf16[48,1792]{1,0:T(8,128)(2,1)S(1)} %get-tuple-element.39), channel_id=1, source_target_pairs={{0,1},{1,0},{2,3},{3,2},{4,5},{5,4},{6,7},{7,6},{8,9},{9,8},{10,11... | collective-permute-start | bytes 516104 | tf_op jit(solution)/shard_map/ppermute | solution.py:307
  35.5 6.1 %collective-permute-start.13 = (bf16[48,1792]{1,0:T(8,128)(2,1)S(1)}, bf16[48,1792]{1,0:T(8,128)(2,1)S(1)}, u32[]{:S(2)}, u32[]{:S(2)}) collective-permute-start(bf16[48,1792]{1,0:T(8,128)(2,1)S(1)} %add_convert_fusion.1), channel_id=1, source_target_pairs={{0,1},{1,0},{2,3},{3,2},{4,5},{5,4},{6,7},{7,6},{8,9},{9,8},{10,11... | collective-permute-start | bytes 516104 | tf_op jit(solution)/shard_map/ppermute | solution.py:307
  39.7 6.9 %collective-permute-start.10 = (bf16[48,1792]{1,0:T(8,128)(2,1)S(1)}, bf16[48,1792]{1,0:T(8,128)(2,1)S(1)}, u32[]{:S(2)}, u32[]{:S(2)}) collective-permute-start(bf16[48,1792]{1,0:T(8,128)(2,1)S(1)} %add_convert_fusion.2), channel_id=1, source_target_pairs={{0,2},{1,3},{2,0},{3,1},{4,6},{5,7},{6,4},{7,5},{8,10},{9,11},{10,... | collective-permute-start | bytes 516104 | tf_op jit(solution)/shard_map/ppermute | solution.py:307
  41.6 8.2 %collective-permute-start.14 = (bf16[48,1792]{1,0:T(8,128)(2,1)S(1)}, bf16[48,1792]{1,0:T(8,128)(2,1)S(1)}, u32[]{:S(2)}, u32[]{:S(2)}) collective-permute-start(bf16[48,1792]{1,0:T(8,128)(2,1)S(1)} %add_convert_fusion), channel_id=1, source_target_pairs={{0,4},{1,5},{2,6},{3,7},{4,0},{5,1},{6,2},{7,3},{8,12},{9,13},{10,... | collective-permute-start | bytes 516104 | tf_op jit(solution)/shard_map/ppermute | solution.py:307
  49.9 1.3 %collective-permute-start.15 = (bf16[24,1792]{1,0:T(8,128)(2,1)S(1)}, bf16[24,1792]{1,0:T(8,128)(2,1)S(1)}, u32[]{:S(2)}, u32[]{:S(2)}) collective-permute-start(bf16[24,1792]{1,0:T(8,128)(2,1)S(1)} %add_convert_fusion.3), channel_id=1, source_target_pairs={{0,8},{8,0},{1,9},{9,1},{2,10},{10,2},{3,11},{11,3},{4,12},{12,4},... | collective-permute-start | bytes 258056 | tf_op jit(solution)/shard_map/ppermute | solution.py:311

commit v3 on v2

--- a/solution.py
+++ b/solution.py
@@ -12,6 +12,7 @@
 BF = jnp.bfloat16
 F32 = jnp.float32
 MIB = 1024 * 1024
+LATE = 8 * MIB
 
 
 def route_table(expert_ids, route_weights, experts_win):
@@ -69,7 +70,7 @@
     return pltpu.with_memory_space_constraint(x, pltpu.HBM)
 
 
-def join(*arrays):
+def join(*arrays, cost=0):
     many = len(arrays)
 
     def kernel(*refs):
@@ -82,6 +83,7 @@
         out_shape=[jax.ShapeDtypeStruct(x.shape, x.dtype) for x in arrays],
         input_output_aliases={i: i for i in range(many)},
         compiler_params=pltpu.CompilerParams(vmem_limit_bytes=8 * MIB),
+        cost_estimate=pl.CostEstimate(flops=0, bytes_accessed=cost, transcendentals=0),
         name="join",
     )(*arrays)
 
@@ -320,14 +322,18 @@
     own, other, slot, scale = select_rows(core, tokens, expert_ids.T, route_weights.T)
     block = jnp.concatenate([own, swap_cores(other)], axis=0)
     loaded = load_weights(gate_weight, up_weight, down_weight)
-    six, two, one, *loaded = join(swap(block, 6), swap(block, 2), swap(block, 1), *loaded)
+    (six,) = join(swap(block, 6), cost=LATE)
+    six, one, two, *loaded = join(six, swap(block, 1), swap(block, 2), *loaded)
     four, seven = join(swap(six, 2), swap(six, 1))
-    five, three = swap(four, 1), swap(one, 2)
+    five = swap(four, 1)
+    (three,) = join(swap(one, 2), cost=3 * LATE)
     part7, part6 = experts([seven, six], *loaded)
-    part0, part1, part2 = experts([block, one, two], *loaded)
-    part5, part4, part3 = experts([five, four, three], *loaded)
-    half = add(part5, swap(part7, 2))
-    far = swap(add(part4, swap(part6, 2), swap(half, 1)), 4)
+    part0, part1, part2, part3 = experts([block, one, two, three], *loaded)
+    part5, part4 = experts([five, four], *loaded)
+    half = swap(add(part5, swap(part7, 2)), 1)
+    half, part1 = join(half, part1)
+    (other6,) = join(swap(part6, 2), cost=3 * LATE)
+    (far,) = join(swap(add(part4, other6, half), 4), cost=2 * LATE)
     near = swap(add(part2, swap(part3, 1)), 2)
     terms = (part0, swap(part1, 1), near, far)
     back = sum(x[ROWS:].astype(F32) for x in terms)

time: 53 us -> 51.5 us (0.972)
  waiting for transfers between devices: 23.7 us -> 21.4 us
  starting transfers between devices: 18.5 us -> 19.1 us
    ppermute x14, waiting for transfers between devices: 21.5 us -> 19.2 us  [swap(): return lax.ppermute(x, 'local', [(i, i ^ mask) for i in range(SPLIT)])]
  transfers between devices with their start and end apart: 16 -> 16, of which waited for: 10 -> 11; matrix products, arithmetic and copies ran while one was open for 0% -> 0% of each run, Pallas kernels for 13% -> 14%
where the time goes in v3:
time: 51.5 us; the launch traced here: 51.4 us
  waiting for transfers between devices  21.4 us (42%)
  starting transfers between devices  19.1 us (37%)
  Pallas kernels  10.6 us (21%)
    ppermute x14, waiting for transfers between devices, swap(): return lax.ppermute(x, 'local', [(i, i ^ mask) for i in range(SPLIT)])  19.2 us
    ppermute x14, starting transfers between devices, swap(): return lax.ppermute(x, 'local', [(i, i ^ mask) for i in range(SPLIT)])  18.5 us
    pallas_call x3, Pallas kernels, experts(): pl.pallas_call(kernel, in_specs=[pl.BlockSpec(memory_space=pltpu.VMEM)] *...  4.52 us
    pallas_call x1, Pallas kernels, load_weights(): pl.pallas_call(kernel, in_specs=[pl.BlockSpec(memory_space=pltpu.HBM)] *...  2.59 us
    ppermute x2, waiting for transfers between devices, swap_cores(): return lax.ppermute(x, 'hst', [(0, 1), (1, 0)])  2.19 us
    pallas_call x1, Pallas kernels, select_rows(): pl.pallas_call(kernel, in_specs=[pl.BlockSpec(memory_space=pltpu.SMEM)] +...  1.89 us
    pallas_call x1, Pallas kernels, combine(): pl.pallas_call(kernel, in_specs=[pl.BlockSpec(memory_space=pltpu.VMEM)] *...  1.62 us
  transfers between devices with their start and end apart: 16, of which 11 were waited for; matrix products, arithmetic and copies ran while one was open for 0% of the time, Pallas kernels for 14%

profile of v3, /device:TPU:0, one launch (start us, length us, event | category | flops | bytes accessed | tf_op | source)
XLA Modules:
  0.0 51.4 jit_solution(5677237483446634825)
XLA Ops:
  0.0 1.9 %select_rows.1 = (bf16[24,1792]{1,0:T(8,128)(2,1)S(1)}, bf16[24,1792]{1,0:T(8,128)(2,1)S(1)}, f32[2,24,128]{2,1,0:T(8,128)S(1)}, f32[2,24,128]{2,1,0:T(8,128)S(1)}) custom-call(s32[1]{0:T(128)} %bitcast.core_ref, s32[8,128]{1,0:T(8,128)} %bitcast.3, f32[8,128]{1,0:T(8,128)} %bitcast.4, bf16[128,7168]{1,0:T(8,128)(2,1)} %tokens_hbm.1), custom_call_target="tpu_custom_call" | custom-call | tf_op jit(solution)/shard_map/select_rows/pallas_call | solution.py:180
  1.9 0.5 %collective-permute-start = (bf16[24,1792]{1,0:T(8,128)(2,1)S(1)}, bf16[24,1792]{1,0:T(8,128)(2,1)S(1)}, u32[]{:S(2)}, u32[]{:S(2)}) collective-permute-start(bf16[24,1792]{1,0:T(8,128)(2,1)S(1)} %get-tuple-element.29), channel_id=1, source_target_pairs={{0,8},{8,0},{1,9},{9,1},{2,10},{10,2},{3,11},{11,3},{4,12},{12,4},... | collective-permute-start | bytes 258056 | tf_op jit(solution)/shard_map/ppermute | solution.py:313
  2.4 0.9 %collective-permute-done = bf16[24,1792]{1,0:T(8,128)(2,1)S(1)} collective-permute-done((bf16[24,1792]{1,0:T(8,128)(2,1)S(1)}, bf16[24,1792]{1,0:T(8,128)(2,1)S(1)}, u32[]{:S(2)}, u32[]{:S(2)}) %collective-permute-start) | collective-permute-done | bytes 86048 | tf_op jit(solution)/shard_map/ppermute | solution.py:313
  3.4 5.0 %collective-permute-start.1 = (bf16[48,1792]{1,0:T(8,128)(2,1)S(1)}, bf16[48,1792]{1,0:T(8,128)(2,1)S(1)}, u32[]{:S(2)}, u32[]{:S(2)}) collective-permute-start(bf16[48,1792]{1,0:T(8,128)(2,1)S(1)} %constant_dynamic-update-slice_fusion.refs_0_), channel_id=1, source_target_pairs={{0,6},{1,7},{2,4},{3,5},{4,2},{5,3},{6,0},{7,1},{8,14},{9,15},{10,... | collective-permute-start | bytes 516104 | tf_op jit(solution)/shard_map/ppermute | solution.py:309
  8.4 0.0 collective-permute-start.3
  8.4 1.5 %collective-permute-start.2 = (bf16[48,1792]{1,0:T(8,128)(2,1)S(1)}, bf16[48,1792]{1,0:T(8,128)(2,1)S(1)}, u32[]{:S(2)}, u32[]{:S(2)}) collective-permute-start(bf16[48,1792]{1,0:T(8,128)(2,1)S(1)} %constant_dynamic-update-slice_fusion.refs_0_), channel_id=1, source_target_pairs={{0,1},{1,0},{2,3},{3,2},{4,5},{5,4},{6,7},{7,6},{8,9},{9,8},{10,11... | collective-permute-start | bytes 516104 | tf_op jit(solution)/shard_map/ppermute | solution.py:309
  9.9 2.6 %load_weights.1 = (bf16[7168,256]{1,0:T(8,128)(2,1)S(1)}, bf16[512,1792]{1,0:T(8,128)(2,1)S(1)}) custom-call(bf16[7168,128]{1,0:T(8,128)(2,1)} %gate_hbm.1, bf16[7168,128]{1,0:T(8,128)(2,1)} %up_hbm.1, bf16[128,7168]{1,0:T(8,128)(2,1)} %down_hbm.1), custom_call_target="tpu_custom_call" | custom-call | tf_op jit(solution)/shard_map/load_weights/pallas_call | solution.py:113
  12.5 1.1 %collective-permute-done.1.refs_0_ = bf16[48,1792]{1,0:T(8,128)(2,1)S(1)} collective-permute-done((bf16[48,1792]{1,0:T(8,128)(2,1)S(1)}, bf16[48,1792]{1,0:T(8,128)(2,1)S(1)}, u32[]{:S(2)}, u32[]{:S(2)}) %collective-permute-start.1) | collective-permute-done | bytes 172064 | tf_op jit(solution)/shard_map/ppermute | solution.py:309
  13.6 3.2 %collective-permute-done.3.refs_2_ = bf16[48,1792]{1,0:T(8,128)(2,1)S(1)} collective-permute-done((bf16[48,1792]{1,0:T(8,128)(2,1)S(1)}, bf16[48,1792]{1,0:T(8,128)(2,1)S(1)}, u32[]{:S(2)}, u32[]{:S(2)}) %collective-permute-start.3) | collective-permute-done | bytes 172064 | tf_op jit(solution)/shard_map/ppermute | solution.py:309
  16.8 0.0 collective-permute-done.2.refs_1_
  16.8 1.5 %collective-permute-start.6 = (bf16[48,1792]{1,0:T(8,128)(2,1)S(1)}, bf16[48,1792]{1,0:T(8,128)(2,1)S(1)}, u32[]{:S(2)}, u32[]{:S(2)}) collective-permute-start(bf16[48,1792]{1,0:T(8,128)(2,1)S(1)} %get-tuple-element.37.refs_1_), channel_id=1, source_target_pairs={{0,1},{1,0},{2,3},{3,2},{4,5},{5,4},{6,7},{7,6},{8,9},{9,8},{10,11... | collective-permute-start | bytes 516104 | tf_op jit(solution)/shard_map/ppermute | solution.py:309
  18.3 1.7 %collective-permute-start.5 = (bf16[48,1792]{1,0:T(8,128)(2,1)S(1)}, bf16[48,1792]{1,0:T(8,128)(2,1)S(1)}, u32[]{:S(2)}, u32[]{:S(2)}) collective-permute-start(bf16[48,1792]{1,0:T(8,128)(2,1)S(1)} %get-tuple-element.37.refs_1_), channel_id=1, source_target_pairs={{0,2},{1,3},{2,0},{3,1},{4,6},{5,7},{6,4},{7,5},{8,10},{9,11},{10,... | collective-permute-start | bytes 516104 | tf_op jit(solution)/shard_map/ppermute | solution.py:309
  20.0 0.4 collective-permute-start.4
  20.4 2.7 %collective-permute-done.6.refs_1_ = bf16[48,1792]{1,0:T(8,128)(2,1)S(1)} collective-permute-done((bf16[48,1792]{1,0:T(8,128)(2,1)S(1)}, bf16[48,1792]{1,0:T(8,128)(2,1)S(1)}, u32[]{:S(2)}, u32[]{:S(2)}) %collective-permute-start.6) | collective-permute-done | bytes 172064 | tf_op jit(solution)/shard_map/ppermute | solution.py:309
  23.1 2.5 %collective-permute-done.5.refs_0_ = bf16[48,1792]{1,0:T(8,128)(2,1)S(1)} collective-permute-done((bf16[48,1792]{1,0:T(8,128)(2,1)S(1)}, bf16[48,1792]{1,0:T(8,128)(2,1)S(1)}, u32[]{:S(2)}, u32[]{:S(2)}) %collective-permute-start.5) | collective-permute-done | bytes 172064 | tf_op jit(solution)/shard_map/ppermute | solution.py:309
  25.6 0.5 collective-permute-start.7
  26.1 1.4 %experts.5 = (bf16[48,1792]{1,0:T(8,128)(2,1)S(1)}, bf16[48,1792]{1,0:T(8,128)(2,1)S(1)}) custom-call(bf16[48,1792]{1,0:T(8,128)(2,1)S(1)} %get-tuple-element.40.refs_0_, bf16[48,1792]{1,0:T(8,128)(2,1)S(1)} %get-tuple-element.37.refs_1_, bf16[7168,256]{1,0:T(8,128)(2,1)S(1)} %get-tuple-element.34.refs_4_.refs_2_, ...), custom_call_target="tpu_custom_call" | custom-call | flops 528482304 | bytes 5505024 | tf_op jit(solution)/shard_map/experts/pallas_call | solution.py:247
  27.5 1.5 %collective-permute-start.8 = (bf16[48,1792]{1,0:T(8,128)(2,1)S(1)}, bf16[48,1792]{1,0:T(8,128)(2,1)S(1)}, u32[]{:S(2)}, u32[]{:S(2)}) collective-permute-start(bf16[48,1792]{1,0:T(8,128)(2,1)S(1)} %get-tuple-element.41), channel_id=1, source_target_pairs={{0,2},{1,3},{2,0},{3,1},{4,6},{5,7},{6,4},{7,5},{8,10},{9,11},{10,... | collective-permute-start | bytes 516104 | tf_op jit(solution)/shard_map/ppermute | solution.py:309
  29.1 0.0 collective-permute-done.4.refs_0_
  29.1 1.7 %experts.3 = (bf16[48,1792]{1,0:T(8,128)(2,1)S(1)}, bf16[48,1792]{1,0:T(8,128)(2,1)S(1)}, bf16[48,1792]{1,0:T(8,128)(2,1)S(1)}, bf16[48,1792]{1,0:T(8,128)(2,1)S(1)}) custom-call(bf16[48,1792]{1,0:T(8,128)(2,1)S(1)} %constant_dynamic-update-slice_fusion.refs_0_, bf16[48,1792]{1,0:T(8,128)(2,1)S(1)} %get-tuple-element.32.refs_1_, ...), custom_call_target="tpu_custom_call" | custom-call | flops 1056964608 | bytes 5505024 | tf_op jit(solution)/shard_map/experts/pallas_call | solution.py:247
  30.8 1.6 %collective-permute-start.11 = (bf16[48,1792]{1,0:T(8,128)(2,1)S(1)}, bf16[48,1792]{1,0:T(8,128)(2,1)S(1)}, u32[]{:S(2)}, u32[]{:S(2)}) collective-permute-start(bf16[48,1792]{1,0:T(8,128)(2,1)S(1)} %get-tuple-element.45), channel_id=1, source_target_pairs={{0,1},{1,0},{2,3},{3,2},{4,5},{5,4},{6,7},{7,6},{8,9},{9,8},{10,11... | collective-permute-start | bytes 516104 | tf_op jit(solution)/shard_map/ppermute | solution.py:309
  32.4 0.5 %collective-permute-start.13 = (bf16[48,1792]{1,0:T(8,128)(2,1)S(1)}, bf16[48,1792]{1,0:T(8,128)(2,1)S(1)}, u32[]{:S(2)}, u32[]{:S(2)}) collective-permute-start(bf16[48,1792]{1,0:T(8,128)(2,1)S(1)} %get-tuple-element.47), channel_id=1, source_target_pairs={{0,2},{1,3},{2,0},{3,1},{4,6},{5,7},{6,4},{7,5},{8,10},{9,11},{10,... | collective-permute-start | bytes 516104 | tf_op jit(solution)/shard_map/ppermute | solution.py:309
  32.9 0.0 collective-permute-done.7.refs_0_
  32.9 1.4 %experts.4 = (bf16[48,1792]{1,0:T(8,128)(2,1)S(1)}, bf16[48,1792]{1,0:T(8,128)(2,1)S(1)}) custom-call(bf16[48,1792]{1,0:T(8,128)(2,1)S(1)} %collective-permute-done.7.refs_0_, bf16[48,1792]{1,0:T(8,128)(2,1)S(1)} %get-tuple-element.38.refs_1_, bf16[7168,256]{1,0:T(8,128)(2,1)S(1)} %get-tuple-element.34.refs_4_.refs_2_, ...), custom_call_target="tpu_custom_call" | custom-call | flops 528482304 | bytes 5505024 | tf_op jit(solution)/shard_map/experts/pallas_call | solution.py:247
  34.3 0.2 collective-permute-done.8
  34.6 1.6 %collective-permute-start.9 = (bf16[48,1792]{1,0:T(8,128)(2,1)S(1)}, bf16[48,1792]{1,0:T(8,128)(2,1)S(1)}, u32[]{:S(2)}, u32[]{:S(2)}) collective-permute-start(bf16[48,1792]{1,0:T(8,128)(2,1)S(1)} %add_convert_fusion.2), channel_id=1, source_target_pairs={{0,1},{1,0},{2,3},{3,2},{4,5},{5,4},{6,7},{7,6},{8,9},{9,8},{10,11... | collective-permute-start | bytes 516104 | tf_op jit(solution)/shard_map/ppermute | solution.py:309
  36.2 1.0 %collective-permute-done.11 = bf16[48,1792]{1,0:T(8,128)(2,1)S(1)} collective-permute-done((bf16[48,1792]{1,0:T(8,128)(2,1)S(1)}, bf16[48,1792]{1,0:T(8,128)(2,1)S(1)}, u32[]{:S(2)}, u32[]{:S(2)}) %collective-permute-start.11) | collective-permute-done | bytes 172064 | tf_op jit(solution)/shard_map/ppermute | solution.py:309
  37.2 0.6 %collective-permute-done.13.refs_0_ = bf16[48,1792]{1,0:T(8,128)(2,1)S(1)} collective-permute-done((bf16[48,1792]{1,0:T(8,128)(2,1)S(1)}, bf16[48,1792]{1,0:T(8,128)(2,1)S(1)}, u32[]{:S(2)}, u32[]{:S(2)}) %collective-permute-start.13) | collective-permute-done | bytes 172064 | tf_op jit(solution)/shard_map/ppermute | solution.py:309
  37.8 2.2 %collective-permute-done.9.refs_0_ = bf16[48,1792]{1,0:T(8,128)(2,1)S(1)} collective-permute-done((bf16[48,1792]{1,0:T(8,128)(2,1)S(1)}, bf16[48,1792]{1,0:T(8,128)(2,1)S(1)}, u32[]{:S(2)}, u32[]{:S(2)}) %collective-permute-start.9) | collective-permute-done | bytes 172064 | tf_op jit(solution)/shard_map/ppermute | solution.py:309
  40.0 0.1 add_convert_fusion
  40.1 0.4 collective-permute-start.14
  40.5 1.6 %collective-permute-start.12 = (bf16[48,1792]{1,0:T(8,128)(2,1)S(1)}, bf16[48,1792]{1,0:T(8,128)(2,1)S(1)}, u32[]{:S(2)}, u32[]{:S(2)}) collective-permute-start(bf16[48,1792]{1,0:T(8,128)(2,1)S(1)} %add_convert_fusion.1), channel_id=1, source_target_pairs={{0,2},{1,3},{2,0},{3,1},{4,6},{5,7},{6,4},{7,5},{8,10},{9,11},{10,... | collective-permute-start | bytes 516104 | tf_op jit(solution)/shard_map/ppermute | solution.py:309
  42.1 0.7 %collective-permute-start.10 = (bf16[48,1792]{1,0:T(8,128)(2,1)S(1)}, bf16[48,1792]{1,0:T(8,128)(2,1)S(1)}, u32[]{:S(2)}, u32[]{:S(2)}) collective-permute-start(bf16[48,1792]{1,0:T(8,128)(2,1)S(1)} %get-tuple-element.43), channel_id=1, source_target_pairs={{0,1},{1,0},{2,3},{3,2},{4,5},{5,4},{6,7},{7,6},{8,9},{9,8},{10,11... | collective-permute-start | bytes 516104 | tf_op jit(solution)/shard_map/ppermute | solution.py:309
  42.7 5.6 %collective-permute-done.14.refs_0_ = bf16[48,1792]{1,0:T(8,128)(2,1)S(1)} collective-permute-done((bf16[48,1792]{1,0:T(8,128)(2,1)S(1)}, bf16[48,1792]{1,0:T(8,128)(2,1)S(1)}, u32[]{:S(2)}, u32[]{:S(2)}) %collective-permute-start.14) | collective-permute-done | bytes 172064 | tf_op jit(solution)/shard_map/ppermute | solution.py:309
  48.4 0.0 collective-permute-done.12.refs_2_
  48.4 0.0 collective-permute-done.10.refs_1_
  48.4 0.1 collective-permute-start.15
  48.5 1.3 %collective-permute-done.15.refs_4_ = bf16[24,1792]{1,0:T(8,128)(2,1)S(1)} collective-permute-done((bf16[24,1792]{1,0:T(8,128)(2,1)S(1)}, bf16[24,1792]{1,0:T(8,128)(2,1)S(1)}, u32[]{:S(2)}, u32[]{:S(2)}) %collective-permute-start.15) | collective-permute-done | bytes 86048 | tf_op jit(solution)/shard_map/ppermute | solution.py:313
  49.8 1.6 %combine.1 = bf16[128,7168]{1,0:T(8,128)(2,1)} custom-call(bf16[48,1792]{1,0:T(8,128)(2,1)S(1)} %get-tuple-element.36.refs_0_, bf16[48,1792]{1,0:T(8,128)(2,1)S(1)} %collective-permute-done.10.refs_1_, bf16[48,1792]{1,0:T(8,128)(2,1)S(1)} %collective-permute-done.12.refs_2_, bf16[48,1792]{1,0:T(8,128)(2,1)S(1)} %join.13.refs_3_, ...), custom_call_target="tpu_custom_call" | custom-call | tf_op jit(solution)/shard_map/combine/pallas_call | solution.py:294
  (12 shorter events, 0.2 us)
Async XLA Ops:
  1.9 1.4 %collective-permute-start = (bf16[24,1792]{1,0:T(8,128)(2,1)S(1)}, bf16[24,1792]{1,0:T(8,128)(2,1)S(1)}, u32[]{:S(2)}, u32[]{:S(2)}) collective-permute-start(bf16[24,1792]{1,0:T(8,128)(2,1)S(1)} %get-tuple-element.29), channel_id=1, source_target_pairs={{0,8},{8,0},{1,9},{9,1},{2,10},{10,2},{3,11},{11,3},{4,12},{12,4},... | collective-permute-start | bytes 258056 | tf_op jit(solution)/shard_map/ppermute | solution.py:313
  3.4 10.2 %collective-permute-start.1 = (bf16[48,1792]{1,0:T(8,128)(2,1)S(1)}, bf16[48,1792]{1,0:T(8,128)(2,1)S(1)}, u32[]{:S(2)}, u32[]{:S(2)}) collective-permute-start(bf16[48,1792]{1,0:T(8,128)(2,1)S(1)} %constant_dynamic-update-slice_fusion.refs_0_), channel_id=1, source_target_pairs={{0,6},{1,7},{2,4},{3,5},{4,2},{5,3},{6,0},{7,1},{8,14},{9,15},{10,... | collective-permute-start | bytes 516104 | tf_op jit(solution)/shard_map/ppermute | solution.py:309
  8.4 8.4 %collective-permute-start.3 = (bf16[48,1792]{1,0:T(8,128)(2,1)S(1)}, bf16[48,1792]{1,0:T(8,128)(2,1)S(1)}, u32[]{:S(2)}, u32[]{:S(2)}) collective-permute-start(bf16[48,1792]{1,0:T(8,128)(2,1)S(1)} %constant_dynamic-update-slice_fusion.refs_0_), channel_id=1, source_target_pairs={{0,2},{1,3},{2,0},{3,1},{4,6},{5,7},{6,4},{7,5},{8,10},{9,11},{10,... | collective-permute-start | bytes 516104 | tf_op jit(solution)/shard_map/ppermute | solution.py:309
  8.4 8.4 %collective-permute-start.2 = (bf16[48,1792]{1,0:T(8,128)(2,1)S(1)}, bf16[48,1792]{1,0:T(8,128)(2,1)S(1)}, u32[]{:S(2)}, u32[]{:S(2)}) collective-permute-start(bf16[48,1792]{1,0:T(8,128)(2,1)S(1)} %constant_dynamic-update-slice_fusion.refs_0_), channel_id=1, source_target_pairs={{0,1},{1,0},{2,3},{3,2},{4,5},{5,4},{6,7},{7,6},{8,9},{9,8},{10,11... | collective-permute-start | bytes 516104 | tf_op jit(solution)/shard_map/ppermute | solution.py:309
  16.8 6.3 %collective-permute-start.6 = (bf16[48,1792]{1,0:T(8,128)(2,1)S(1)}, bf16[48,1792]{1,0:T(8,128)(2,1)S(1)}, u32[]{:S(2)}, u32[]{:S(2)}) collective-permute-start(bf16[48,1792]{1,0:T(8,128)(2,1)S(1)} %get-tuple-element.37.refs_1_), channel_id=1, source_target_pairs={{0,1},{1,0},{2,3},{3,2},{4,5},{5,4},{6,7},{7,6},{8,9},{9,8},{10,11... | collective-permute-start | bytes 516104 | tf_op jit(solution)/shard_map/ppermute | solution.py:309
  18.3 7.3 %collective-permute-start.5 = (bf16[48,1792]{1,0:T(8,128)(2,1)S(1)}, bf16[48,1792]{1,0:T(8,128)(2,1)S(1)}, u32[]{:S(2)}, u32[]{:S(2)}) collective-permute-start(bf16[48,1792]{1,0:T(8,128)(2,1)S(1)} %get-tuple-element.37.refs_1_), channel_id=1, source_target_pairs={{0,2},{1,3},{2,0},{3,1},{4,6},{5,7},{6,4},{7,5},{8,10},{9,11},{10,... | collective-permute-start | bytes 516104 | tf_op jit(solution)/shard_map/ppermute | solution.py:309
  20.0 9.1 %collective-permute-start.4 = (bf16[48,1792]{1,0:T(8,128)(2,1)S(1)}, bf16[48,1792]{1,0:T(8,128)(2,1)S(1)}, u32[]{:S(2)}, u32[]{:S(2)}) collective-permute-start(bf16[48,1792]{1,0:T(8,128)(2,1)S(1)} %get-tuple-element.32.refs_1_), channel_id=1, source_target_pairs={{0,2},{1,3},{2,0},{3,1},{4,6},{5,7},{6,4},{7,5},{8,10},{9,11},{10,... | collective-permute-start | bytes 516104 | tf_op jit(solution)/shard_map/ppermute | solution.py:309
  25.6 7.3 %collective-permute-start.7 = (bf16[48,1792]{1,0:T(8,128)(2,1)S(1)}, bf16[48,1792]{1,0:T(8,128)(2,1)S(1)}, u32[]{:S(2)}, u32[]{:S(2)}) collective-permute-start(bf16[48,1792]{1,0:T(8,128)(2,1)S(1)} %get-tuple-element.38.refs_1_), channel_id=1, source_target_pairs={{0,1},{1,0},{2,3},{3,2},{4,5},{5,4},{6,7},{7,6},{8,9},{9,8},{10,11... | collective-permute-start | bytes 516104 | tf_op jit(solution)/shard_map/ppermute | solution.py:309
  27.5 7.0 %collective-permute-start.8 = (bf16[48,1792]{1,0:T(8,128)(2,1)S(1)}, bf16[48,1792]{1,0:T(8,128)(2,1)S(1)}, u32[]{:S(2)}, u32[]{:S(2)}) collective-permute-start(bf16[48,1792]{1,0:T(8,128)(2,1)S(1)} %get-tuple-element.41), channel_id=1, source_target_pairs={{0,2},{1,3},{2,0},{3,1},{4,6},{5,7},{6,4},{7,5},{8,10},{9,11},{10,... | collective-permute-start | bytes 516104 | tf_op jit(solution)/shard_map/ppermute | solution.py:309
  30.8 6.4 %collective-permute-start.11 = (bf16[48,1792]{1,0:T(8,128)(2,1)S(1)}, bf16[48,1792]{1,0:T(8,128)(2,1)S(1)}, u32[]{:S(2)}, u32[]{:S(2)}) collective-permute-start(bf16[48,1792]{1,0:T(8,128)(2,1)S(1)} %get-tuple-element.45), channel_id=1, source_target_pairs={{0,1},{1,0},{2,3},{3,2},{4,5},{5,4},{6,7},{7,6},{8,9},{9,8},{10,11... | collective-permute-start | bytes 516104 | tf_op jit(solution)/shard_map/ppermute | solution.py:309
  32.4 5.4 %collective-permute-start.13 = (bf16[48,1792]{1,0:T(8,128)(2,1)S(1)}, bf16[48,1792]{1,0:T(8,128)(2,1)S(1)}, u32[]{:S(2)}, u32[]{:S(2)}) collective-permute-start(bf16[48,1792]{1,0:T(8,128)(2,1)S(1)} %get-tuple-element.47), channel_id=1, source_target_pairs={{0,2},{1,3},{2,0},{3,1},{4,6},{5,7},{6,4},{7,5},{8,10},{9,11},{10,... | collective-permute-start | bytes 516104 | tf_op jit(solution)/shard_map/ppermute | solution.py:309
  34.6 5.5 %collective-permute-start.9 = (bf16[48,1792]{1,0:T(8,128)(2,1)S(1)}, bf16[48,1792]{1,0:T(8,128)(2,1)S(1)}, u32[]{:S(2)}, u32[]{:S(2)}) collective-permute-start(bf16[48,1792]{1,0:T(8,128)(2,1)S(1)} %add_convert_fusion.2), channel_id=1, source_target_pairs={{0,1},{1,0},{2,3},{3,2},{4,5},{5,4},{6,7},{7,6},{8,9},{9,8},{10,11... | collective-permute-start | bytes 516104 | tf_op jit(solution)/shard_map/ppermute | solution.py:309
  40.1 8.3 %collective-permute-start.14 = (bf16[48,1792]{1,0:T(8,128)(2,1)S(1)}, bf16[48,1792]{1,0:T(8,128)(2,1)S(1)}, u32[]{:S(2)}, u32[]{:S(2)}) collective-permute-start(bf16[48,1792]{1,0:T(8,128)(2,1)S(1)} %add_convert_fusion), channel_id=1, source_target_pairs={{0,4},{1,5},{2,6},{3,7},{4,0},{5,1},{6,2},{7,3},{8,12},{9,13},{10,... | collective-permute-start | bytes 516104 | tf_op jit(solution)/shard_map/ppermute | solution.py:309
  40.5 7.9 %collective-permute-start.12 = (bf16[48,1792]{1,0:T(8,128)(2,1)S(1)}, bf16[48,1792]{1,0:T(8,128)(2,1)S(1)}, u32[]{:S(2)}, u32[]{:S(2)}) collective-permute-start(bf16[48,1792]{1,0:T(8,128)(2,1)S(1)} %add_convert_fusion.1), channel_id=1, source_target_pairs={{0,2},{1,3},{2,0},{3,1},{4,6},{5,7},{6,4},{7,5},{8,10},{9,11},{10,... | collective-permute-start | bytes 516104 | tf_op jit(solution)/shard_map/ppermute | solution.py:309
  42.1 6.3 %collective-permute-start.10 = (bf16[48,1792]{1,0:T(8,128)(2,1)S(1)}, bf16[48,1792]{1,0:T(8,128)(2,1)S(1)}, u32[]{:S(2)}, u32[]{:S(2)}) collective-permute-start(bf16[48,1792]{1,0:T(8,128)(2,1)S(1)} %get-tuple-element.43), channel_id=1, source_target_pairs={{0,1},{1,0},{2,3},{3,2},{4,5},{5,4},{6,7},{7,6},{8,9},{9,8},{10,11... | collective-permute-start | bytes 516104 | tf_op jit(solution)/shard_map/ppermute | solution.py:309
  48.4 1.3 %collective-permute-start.15 = (bf16[24,1792]{1,0:T(8,128)(2,1)S(1)}, bf16[24,1792]{1,0:T(8,128)(2,1)S(1)}, u32[]{:S(2)}, u32[]{:S(2)}) collective-permute-start(bf16[24,1792]{1,0:T(8,128)(2,1)S(1)} %add_convert_fusion.3), channel_id=1, source_target_pairs={{0,8},{8,0},{1,9},{9,1},{2,10},{10,2},{3,11},{11,3},{4,12},{12,4},... | collective-permute-start | bytes 258056 | tf_op jit(solution)/shard_map/ppermute | solution.py:313

commit v4 on v3

--- a/solution.py
+++ b/solution.py
@@ -217,20 +217,13 @@
             cut = slice(s * seg, (s + 1) * seg)
             part = jnp.dot(rows, both_ref[cut, :], preferred_element_type=F32)
             total = total + jnp.where(line == s, part, 0.0)
-        one = lax.broadcasted_iota(jnp.int32, (tall, tall), 0)
-        two = lax.broadcasted_iota(jnp.int32, (tall, tall), 1)
-        same = ((one // ROWS == two // ROWS) & (one % MOST == two % MOST)).astype(F32)
-        spread = jnp.concatenate(
-            [
-                jnp.dot(
-                    same,
-                    total[b * tall : (b + 1) * tall],
-                    precision=lax.Precision.HIGHEST,
-                    preferred_element_type=F32,
-                )
-                for b in range(many)
-            ],
-            axis=0,
+        high = total.astype(BF)
+        low = (total - high.astype(F32)).astype(BF)
+        one = lax.broadcasted_iota(jnp.int32, (height, 2 * height), 0)
+        two = lax.broadcasted_iota(jnp.int32, (height, 2 * height), 1) % height
+        same = ((one // ROWS == two // ROWS) & (one % MOST == two % MOST)).astype(BF)
+        spread = jnp.dot(
+            same, jnp.concatenate([high, low], axis=0), preferred_element_type=F32
         )
         gate = spread[:, :units]
         up = spread[:, units:]
@@ -322,14 +315,15 @@
     own, other, slot, scale = select_rows(core, tokens, expert_ids.T, route_weights.T)
     block = jnp.concatenate([own, swap_cores(other)], axis=0)
     loaded = load_weights(gate_weight, up_weight, down_weight)
-    (six,) = join(swap(block, 6), cost=LATE)
+    (six,) = join(swap(block, 6), cost=1 * LATE)
     six, one, two, *loaded = join(six, swap(block, 1), swap(block, 2), *loaded)
-    four, seven = join(swap(six, 2), swap(six, 1))
+    (four,) = join(swap(six, 2), cost=1 * LATE)
+    four, seven = join(four, swap(six, 1))
     five = swap(four, 1)
     (three,) = join(swap(one, 2), cost=3 * LATE)
-    part7, part6 = experts([seven, six], *loaded)
+    part7, part6, part4 = experts([seven, six, four], *loaded)
     part0, part1, part2, part3 = experts([block, one, two, three], *loaded)
-    part5, part4 = experts([five, four], *loaded)
+    (part5,) = experts([five], *loaded)
     half = swap(add(part5, swap(part7, 2)), 1)
     half, part1 = join(half, part1)
     (other6,) = join(swap(part6, 2), cost=3 * LATE)

time: 51.5 us -> 50.2 us (0.975)
  waiting for transfers between devices: 21.4 us -> 20 us
    ppermute x14, waiting for transfers between devices: 19.2 us -> 17.8 us  [swap(): return lax.ppermute(x, 'local', [(i, i ^ mask) for i in range(SPLIT)])]
  transfers between devices with their start and end apart: 16 -> 16, of which waited for: 11 -> 10; matrix products, arithmetic and copies ran while one was open for 0% -> 0% of each run, Pallas kernels for 14% -> 14%
where the time goes in v4:
time: 50.2 us; the launch traced here: 50.1 us
  waiting for transfers between devices  20 us (40%)
  starting transfers between devices  19.3 us (38%)
  Pallas kernels  10.5 us (21%)
    ppermute x14, starting transfers between devices, swap(): return lax.ppermute(x, 'local', [(i, i ^ mask) for i in range(SPLIT)])  18.7 us
    ppermute x14, waiting for transfers between devices, swap(): return lax.ppermute(x, 'local', [(i, i ^ mask) for i in range(SPLIT)])  17.8 us
    pallas_call x3, Pallas kernels, experts(): pl.pallas_call(kernel, in_specs=[pl.BlockSpec(memory_space=pltpu.VMEM)] *...  4.35 us
    pallas_call x1, Pallas kernels, load_weights(): pl.pallas_call(kernel, in_specs=[pl.BlockSpec(memory_space=pltpu.HBM)] *...  2.59 us
    ppermute x2, waiting for transfers between devices, swap_cores(): return lax.ppermute(x, 'hst', [(0, 1), (1, 0)])  2.19 us
    pallas_call x1, Pallas kernels, select_rows(): pl.pallas_call(kernel, in_specs=[pl.BlockSpec(memory_space=pltpu.SMEM)] +...  1.89 us
    pallas_call x1, Pallas kernels, combine(): pl.pallas_call(kernel, in_specs=[pl.BlockSpec(memory_space=pltpu.VMEM)] *...  1.62 us
  transfers between devices with their start and end apart: 16, of which 10 were waited for; matrix products, arithmetic and copies ran while one was open for 0% of the time, Pallas kernels for 14%

profile of v4, /device:TPU:0, one launch (start us, length us, event | category | flops | bytes accessed | tf_op | source)
XLA Modules:
  0.0 50.1 jit_solution(16348563301839952321)
XLA Ops:
  0.0 1.9 %select_rows.1 = (bf16[24,1792]{1,0:T(8,128)(2,1)S(1)}, bf16[24,1792]{1,0:T(8,128)(2,1)S(1)}, f32[2,24,128]{2,1,0:T(8,128)S(1)}, f32[2,24,128]{2,1,0:T(8,128)S(1)}) custom-call(s32[1]{0:T(128)} %bitcast.core_ref, s32[8,128]{1,0:T(8,128)} %bitcast.3, f32[8,128]{1,0:T(8,128)} %bitcast.4, bf16[128,7168]{1,0:T(8,128)(2,1)} %tokens_hbm.1), custom_call_target="tpu_custom_call" | custom-call | tf_op jit(solution)/shard_map/select_rows/pallas_call | solution.py:180
  1.9 0.5 %collective-permute-start = (bf16[24,1792]{1,0:T(8,128)(2,1)S(1)}, bf16[24,1792]{1,0:T(8,128)(2,1)S(1)}, u32[]{:S(2)}, u32[]{:S(2)}) collective-permute-start(bf16[24,1792]{1,0:T(8,128)(2,1)S(1)} %get-tuple-element.28), channel_id=1, source_target_pairs={{0,8},{8,0},{1,9},{9,1},{2,10},{10,2},{3,11},{11,3},{4,12},{12,4},... | collective-permute-start | bytes 258056 | tf_op jit(solution)/shard_map/ppermute | solution.py:306
  2.4 0.9 %collective-permute-done = bf16[24,1792]{1,0:T(8,128)(2,1)S(1)} collective-permute-done((bf16[24,1792]{1,0:T(8,128)(2,1)S(1)}, bf16[24,1792]{1,0:T(8,128)(2,1)S(1)}, u32[]{:S(2)}, u32[]{:S(2)}) %collective-permute-start) | collective-permute-done | bytes 86048 | tf_op jit(solution)/shard_map/ppermute | solution.py:306
  3.4 5.0 %collective-permute-start.1 = (bf16[48,1792]{1,0:T(8,128)(2,1)S(1)}, bf16[48,1792]{1,0:T(8,128)(2,1)S(1)}, u32[]{:S(2)}, u32[]{:S(2)}) collective-permute-start(bf16[48,1792]{1,0:T(8,128)(2,1)S(1)} %constant_dynamic-update-slice_fusion.refs_0_), channel_id=1, source_target_pairs={{0,6},{1,7},{2,4},{3,5},{4,2},{5,3},{6,0},{7,1},{8,14},{9,15},{10,... | collective-permute-start | bytes 516104 | tf_op jit(solution)/shard_map/ppermute | solution.py:302
  8.4 0.0 collective-permute-start.3
  8.4 1.5 %collective-permute-start.2 = (bf16[48,1792]{1,0:T(8,128)(2,1)S(1)}, bf16[48,1792]{1,0:T(8,128)(2,1)S(1)}, u32[]{:S(2)}, u32[]{:S(2)}) collective-permute-start(bf16[48,1792]{1,0:T(8,128)(2,1)S(1)} %constant_dynamic-update-slice_fusion.refs_0_), channel_id=1, source_target_pairs={{0,1},{1,0},{2,3},{3,2},{4,5},{5,4},{6,7},{7,6},{8,9},{9,8},{10,11... | collective-permute-start | bytes 516104 | tf_op jit(solution)/shard_map/ppermute | solution.py:302
  9.9 2.6 %load_weights.1 = (bf16[7168,256]{1,0:T(8,128)(2,1)S(1)}, bf16[512,1792]{1,0:T(8,128)(2,1)S(1)}) custom-call(bf16[7168,128]{1,0:T(8,128)(2,1)} %gate_hbm.1, bf16[7168,128]{1,0:T(8,128)(2,1)} %up_hbm.1, bf16[128,7168]{1,0:T(8,128)(2,1)} %down_hbm.1), custom_call_target="tpu_custom_call" | custom-call | tf_op jit(solution)/shard_map/load_weights/pallas_call | solution.py:113
  12.5 1.1 %collective-permute-done.1.refs_0_ = bf16[48,1792]{1,0:T(8,128)(2,1)S(1)} collective-permute-done((bf16[48,1792]{1,0:T(8,128)(2,1)S(1)}, bf16[48,1792]{1,0:T(8,128)(2,1)S(1)}, u32[]{:S(2)}, u32[]{:S(2)}) %collective-permute-start.1) | collective-permute-done | bytes 172064 | tf_op jit(solution)/shard_map/ppermute | solution.py:302
  13.6 3.2 %collective-permute-done.3.refs_2_ = bf16[48,1792]{1,0:T(8,128)(2,1)S(1)} collective-permute-done((bf16[48,1792]{1,0:T(8,128)(2,1)S(1)}, bf16[48,1792]{1,0:T(8,128)(2,1)S(1)}, u32[]{:S(2)}, u32[]{:S(2)}) %collective-permute-start.3) | collective-permute-done | bytes 172064 | tf_op jit(solution)/shard_map/ppermute | solution.py:302
  16.8 0.0 collective-permute-done.2.refs_1_
  16.8 1.7 %collective-permute-start.5 = (bf16[48,1792]{1,0:T(8,128)(2,1)S(1)}, bf16[48,1792]{1,0:T(8,128)(2,1)S(1)}, u32[]{:S(2)}, u32[]{:S(2)}) collective-permute-start(bf16[48,1792]{1,0:T(8,128)(2,1)S(1)} %get-tuple-element.36.refs_1_), channel_id=1, source_target_pairs={{0,2},{1,3},{2,0},{3,1},{4,6},{5,7},{6,4},{7,5},{8,10},{9,11},{10,... | collective-permute-start | bytes 516104 | tf_op jit(solution)/shard_map/ppermute | solution.py:302
  18.5 1.5 %collective-permute-start.6 = (bf16[48,1792]{1,0:T(8,128)(2,1)S(1)}, bf16[48,1792]{1,0:T(8,128)(2,1)S(1)}, u32[]{:S(2)}, u32[]{:S(2)}) collective-permute-start(bf16[48,1792]{1,0:T(8,128)(2,1)S(1)} %get-tuple-element.36.refs_1_), channel_id=1, source_target_pairs={{0,1},{1,0},{2,3},{3,2},{4,5},{5,4},{6,7},{7,6},{8,9},{9,8},{10,11... | collective-permute-start | bytes 516104 | tf_op jit(solution)/shard_map/ppermute | solution.py:302
  20.0 0.3 collective-permute-start.4
  20.3 3.7 %collective-permute-done.5.refs_0_ = bf16[48,1792]{1,0:T(8,128)(2,1)S(1)} collective-permute-done((bf16[48,1792]{1,0:T(8,128)(2,1)S(1)}, bf16[48,1792]{1,0:T(8,128)(2,1)S(1)}, u32[]{:S(2)}, u32[]{:S(2)}) %collective-permute-start.5) | collective-permute-done | bytes 172064 | tf_op jit(solution)/shard_map/ppermute | solution.py:302
  24.0 0.0 collective-permute-done.6.refs_1_
  24.0 1.5 %collective-permute-start.7 = (bf16[48,1792]{1,0:T(8,128)(2,1)S(1)}, bf16[48,1792]{1,0:T(8,128)(2,1)S(1)}, u32[]{:S(2)}, u32[]{:S(2)}) collective-permute-start(bf16[48,1792]{1,0:T(8,128)(2,1)S(1)} %get-tuple-element.37.refs_2_), channel_id=1, source_target_pairs={{0,1},{1,0},{2,3},{3,2},{4,5},{5,4},{6,7},{7,6},{8,9},{9,8},{10,11... | collective-permute-start | bytes 516104 | tf_op jit(solution)/shard_map/ppermute | solution.py:302
  25.5 1.3 %experts.5 = (bf16[48,1792]{1,0:T(8,128)(2,1)S(1)}, bf16[48,1792]{1,0:T(8,128)(2,1)S(1)}, bf16[48,1792]{1,0:T(8,128)(2,1)S(1)}) custom-call(bf16[48,1792]{1,0:T(8,128)(2,1)S(1)} %get-tuple-element.38.refs_0_, bf16[48,1792]{1,0:T(8,128)(2,1)S(1)} %get-tuple-element.36.refs_1_, bf16[48,1792]{1,0:T(8,128)(2,1)S(1)} %get-tuple-element.37.refs_2_, ...), custom_call_target="tpu_custom_call" | custom-call | flops 792723456 | bytes 5505024 | tf_op jit(solution)/shard_map/experts/pallas_call | solution.py:240
  26.9 1.8 %collective-permute-start.8 = (bf16[48,1792]{1,0:T(8,128)(2,1)S(1)}, bf16[48,1792]{1,0:T(8,128)(2,1)S(1)}, u32[]{:S(2)}, u32[]{:S(2)}) collective-permute-start(bf16[48,1792]{1,0:T(8,128)(2,1)S(1)} %get-tuple-element.39), channel_id=1, source_target_pairs={{0,2},{1,3},{2,0},{3,1},{4,6},{5,7},{6,4},{7,5},{8,10},{9,11},{10,... | collective-permute-start | bytes 516104 | tf_op jit(solution)/shard_map/ppermute | solution.py:302
  28.7 0.0 collective-permute-done.4.refs_0_
  28.7 1.7 %experts.3 = (bf16[48,1792]{1,0:T(8,128)(2,1)S(1)}, bf16[48,1792]{1,0:T(8,128)(2,1)S(1)}, bf16[48,1792]{1,0:T(8,128)(2,1)S(1)}, bf16[48,1792]{1,0:T(8,128)(2,1)S(1)}) custom-call(bf16[48,1792]{1,0:T(8,128)(2,1)S(1)} %constant_dynamic-update-slice_fusion.refs_0_, bf16[48,1792]{1,0:T(8,128)(2,1)S(1)} %get-tuple-element.31.refs_1_, ...), custom_call_target="tpu_custom_call" | custom-call | flops 1056964608 | bytes 5505024 | tf_op jit(solution)/shard_map/experts/pallas_call | solution.py:240
  30.4 0.4 collective-permute-start.11
  30.8 0.4 collective-permute-start.13
  31.2 0.0 collective-permute-done.7.refs_0_
  31.2 1.4 %experts.4 = bf16[48,1792]{1,0:T(8,128)(2,1)S(1)} custom-call(bf16[48,1792]{1,0:T(8,128)(2,1)S(1)} %collective-permute-done.7.refs_0_, bf16[7168,256]{1,0:T(8,128)(2,1)S(1)} %get-tuple-element.33.refs_4_.refs_1_.refs_3_, bf16[512,1792]{1,0:T(8,128)(2,1)S(1)} %get-tuple-element.34.refs_5_.refs_2_.refs_4_), custom_call_target="tpu_custom_call" | custom-call | flops 264241152 | bytes 5505024 | tf_op jit(solution)/shard_map/experts/pallas_call | solution.py:240
  32.6 0.6 %collective-permute-done.8 = bf16[48,1792]{1,0:T(8,128)(2,1)S(1)} collective-permute-done((bf16[48,1792]{1,0:T(8,128)(2,1)S(1)}, bf16[48,1792]{1,0:T(8,128)(2,1)S(1)}, u32[]{:S(2)}, u32[]{:S(2)}) %collective-permute-start.8) | collective-permute-done | bytes 172064 | tf_op jit(solution)/shard_map/ppermute | solution.py:302
  33.3 1.0 %collective-permute-start.9 = (bf16[48,1792]{1,0:T(8,128)(2,1)S(1)}, bf16[48,1792]{1,0:T(8,128)(2,1)S(1)}, u32[]{:S(2)}, u32[]{:S(2)}) collective-permute-start(bf16[48,1792]{1,0:T(8,128)(2,1)S(1)} %add_convert_fusion.2), channel_id=1, source_target_pairs={{0,1},{1,0},{2,3},{3,2},{4,5},{5,4},{6,7},{7,6},{8,9},{9,8},{10,11... | collective-permute-start | bytes 516104 | tf_op jit(solution)/shard_map/ppermute | solution.py:302
  34.2 2.4 %collective-permute-done.11 = bf16[48,1792]{1,0:T(8,128)(2,1)S(1)} collective-permute-done((bf16[48,1792]{1,0:T(8,128)(2,1)S(1)}, bf16[48,1792]{1,0:T(8,128)(2,1)S(1)}, u32[]{:S(2)}, u32[]{:S(2)}) %collective-permute-start.11) | collective-permute-done | bytes 172064 | tf_op jit(solution)/shard_map/ppermute | solution.py:302
  36.7 0.0 collective-permute-done.13.refs_0_
  36.8 2.0 %collective-permute-done.9.refs_0_ = bf16[48,1792]{1,0:T(8,128)(2,1)S(1)} collective-permute-done((bf16[48,1792]{1,0:T(8,128)(2,1)S(1)}, bf16[48,1792]{1,0:T(8,128)(2,1)S(1)}, u32[]{:S(2)}, u32[]{:S(2)}) %collective-permute-start.9) | collective-permute-done | bytes 172064 | tf_op jit(solution)/shard_map/ppermute | solution.py:302
  38.7 0.1 add_convert_fusion
  38.8 1.2 %collective-permute-start.14 = (bf16[48,1792]{1,0:T(8,128)(2,1)S(1)}, bf16[48,1792]{1,0:T(8,128)(2,1)S(1)}, u32[]{:S(2)}, u32[]{:S(2)}) collective-permute-start(bf16[48,1792]{1,0:T(8,128)(2,1)S(1)} %add_convert_fusion), channel_id=1, source_target_pairs={{0,4},{1,5},{2,6},{3,7},{4,0},{5,1},{6,2},{7,3},{8,12},{9,13},{10,... | collective-permute-start | bytes 516104 | tf_op jit(solution)/shard_map/ppermute | solution.py:302
  40.0 1.5 %collective-permute-start.12 = (bf16[48,1792]{1,0:T(8,128)(2,1)S(1)}, bf16[48,1792]{1,0:T(8,128)(2,1)S(1)}, u32[]{:S(2)}, u32[]{:S(2)}) collective-permute-start(bf16[48,1792]{1,0:T(8,128)(2,1)S(1)} %add_convert_fusion.1), channel_id=1, source_target_pairs={{0,2},{1,3},{2,0},{3,1},{4,6},{5,7},{6,4},{7,5},{8,10},{9,11},{10,... | collective-permute-start | bytes 516104 | tf_op jit(solution)/shard_map/ppermute | solution.py:302
  41.5 0.8 %collective-permute-start.10 = (bf16[48,1792]{1,0:T(8,128)(2,1)S(1)}, bf16[48,1792]{1,0:T(8,128)(2,1)S(1)}, u32[]{:S(2)}, u32[]{:S(2)}) collective-permute-start(bf16[48,1792]{1,0:T(8,128)(2,1)S(1)} %get-tuple-element.41), channel_id=1, source_target_pairs={{0,1},{1,0},{2,3},{3,2},{4,5},{5,4},{6,7},{7,6},{8,9},{9,8},{10,11... | collective-permute-start | bytes 516104 | tf_op jit(solution)/shard_map/ppermute | solution.py:302
  42.3 3.0 %collective-permute-done.14.refs_0_ = bf16[48,1792]{1,0:T(8,128)(2,1)S(1)} collective-permute-done((bf16[48,1792]{1,0:T(8,128)(2,1)S(1)}, bf16[48,1792]{1,0:T(8,128)(2,1)S(1)}, u32[]{:S(2)}, u32[]{:S(2)}) %collective-permute-start.14) | collective-permute-done | bytes 172064 | tf_op jit(solution)/shard_map/ppermute | solution.py:302
  45.3 1.7 %collective-permute-done.12.refs_2_ = bf16[48,1792]{1,0:T(8,128)(2,1)S(1)} collective-permute-done((bf16[48,1792]{1,0:T(8,128)(2,1)S(1)}, bf16[48,1792]{1,0:T(8,128)(2,1)S(1)}, u32[]{:S(2)}, u32[]{:S(2)}) %collective-permute-start.12) | collective-permute-done | bytes 172064 | tf_op jit(solution)/shard_map/ppermute | solution.py:302
  47.0 0.0 collective-permute-done.10.refs_1_
  47.0 0.1 add_convert_fusion.3
  47.1 0.1 collective-permute-start.15
  47.2 1.3 %collective-permute-done.15.refs_4_ = bf16[24,1792]{1,0:T(8,128)(2,1)S(1)} collective-permute-done((bf16[24,1792]{1,0:T(8,128)(2,1)S(1)}, bf16[24,1792]{1,0:T(8,128)(2,1)S(1)}, u32[]{:S(2)}, u32[]{:S(2)}) %collective-permute-start.15) | collective-permute-done | bytes 86048 | tf_op jit(solution)/shard_map/ppermute | solution.py:306
  48.4 1.6 %combine.1 = bf16[128,7168]{1,0:T(8,128)(2,1)} custom-call(bf16[48,1792]{1,0:T(8,128)(2,1)S(1)} %get-tuple-element.35.refs_0_, bf16[48,1792]{1,0:T(8,128)(2,1)S(1)} %collective-permute-done.10.refs_1_, bf16[48,1792]{1,0:T(8,128)(2,1)S(1)} %collective-permute-done.12.refs_2_, bf16[48,1792]{1,0:T(8,128)(2,1)S(1)} %join.15.refs_3_, ...), custom_call_target="tpu_custom_call" | custom-call | tf_op jit(solution)/shard_map/combine/pallas_call | solution.py:287
  (12 shorter events, 0.1 us)
Async XLA Ops:
  1.9 1.4 %collective-permute-start = (bf16[24,1792]{1,0:T(8,128)(2,1)S(1)}, bf16[24,1792]{1,0:T(8,128)(2,1)S(1)}, u32[]{:S(2)}, u32[]{:S(2)}) collective-permute-start(bf16[24,1792]{1,0:T(8,128)(2,1)S(1)} %get-tuple-element.28), channel_id=1, source_target_pairs={{0,8},{8,0},{1,9},{9,1},{2,10},{10,2},{3,11},{11,3},{4,12},{12,4},... | collective-permute-start | bytes 258056 | tf_op jit(solution)/shard_map/ppermute | solution.py:306
  3.4 10.2 %collective-permute-start.1 = (bf16[48,1792]{1,0:T(8,128)(2,1)S(1)}, bf16[48,1792]{1,0:T(8,128)(2,1)S(1)}, u32[]{:S(2)}, u32[]{:S(2)}) collective-permute-start(bf16[48,1792]{1,0:T(8,128)(2,1)S(1)} %constant_dynamic-update-slice_fusion.refs_0_), channel_id=1, source_target_pairs={{0,6},{1,7},{2,4},{3,5},{4,2},{5,3},{6,0},{7,1},{8,14},{9,15},{10,... | collective-permute-start | bytes 516104 | tf_op jit(solution)/shard_map/ppermute | solution.py:302
  8.4 8.4 %collective-permute-start.3 = (bf16[48,1792]{1,0:T(8,128)(2,1)S(1)}, bf16[48,1792]{1,0:T(8,128)(2,1)S(1)}, u32[]{:S(2)}, u32[]{:S(2)}) collective-permute-start(bf16[48,1792]{1,0:T(8,128)(2,1)S(1)} %constant_dynamic-update-slice_fusion.refs_0_), channel_id=1, source_target_pairs={{0,2},{1,3},{2,0},{3,1},{4,6},{5,7},{6,4},{7,5},{8,10},{9,11},{10,... | collective-permute-start | bytes 516104 | tf_op jit(solution)/shard_map/ppermute | solution.py:302
  8.4 8.4 %collective-permute-start.2 = (bf16[48,1792]{1,0:T(8,128)(2,1)S(1)}, bf16[48,1792]{1,0:T(8,128)(2,1)S(1)}, u32[]{:S(2)}, u32[]{:S(2)}) collective-permute-start(bf16[48,1792]{1,0:T(8,128)(2,1)S(1)} %constant_dynamic-update-slice_fusion.refs_0_), channel_id=1, source_target_pairs={{0,1},{1,0},{2,3},{3,2},{4,5},{5,4},{6,7},{7,6},{8,9},{9,8},{10,11... | collective-permute-start | bytes 516104 | tf_op jit(solution)/shard_map/ppermute | solution.py:302
  16.8 7.2 %collective-permute-start.5 = (bf16[48,1792]{1,0:T(8,128)(2,1)S(1)}, bf16[48,1792]{1,0:T(8,128)(2,1)S(1)}, u32[]{:S(2)}, u32[]{:S(2)}) collective-permute-start(bf16[48,1792]{1,0:T(8,128)(2,1)S(1)} %get-tuple-element.36.refs_1_), channel_id=1, source_target_pairs={{0,2},{1,3},{2,0},{3,1},{4,6},{5,7},{6,4},{7,5},{8,10},{9,11},{10,... | collective-permute-start | bytes 516104 | tf_op jit(solution)/shard_map/ppermute | solution.py:302
  18.5 5.6 %collective-permute-start.6 = (bf16[48,1792]{1,0:T(8,128)(2,1)S(1)}, bf16[48,1792]{1,0:T(8,128)(2,1)S(1)}, u32[]{:S(2)}, u32[]{:S(2)}) collective-permute-start(bf16[48,1792]{1,0:T(8,128)(2,1)S(1)} %get-tuple-element.36.refs_1_), channel_id=1, source_target_pairs={{0,1},{1,0},{2,3},{3,2},{4,5},{5,4},{6,7},{7,6},{8,9},{9,8},{10,11... | collective-permute-start | bytes 516104 | tf_op jit(solution)/shard_map/ppermute | solution.py:302
  20.0 8.7 %collective-permute-start.4 = (bf16[48,1792]{1,0:T(8,128)(2,1)S(1)}, bf16[48,1792]{1,0:T(8,128)(2,1)S(1)}, u32[]{:S(2)}, u32[]{:S(2)}) collective-permute-start(bf16[48,1792]{1,0:T(8,128)(2,1)S(1)} %get-tuple-element.31.refs_1_), channel_id=1, source_target_pairs={{0,2},{1,3},{2,0},{3,1},{4,6},{5,7},{6,4},{7,5},{8,10},{9,11},{10,... | collective-permute-start | bytes 516104 | tf_op jit(solution)/shard_map/ppermute | solution.py:302
  24.0 7.2 %collective-permute-start.7 = (bf16[48,1792]{1,0:T(8,128)(2,1)S(1)}, bf16[48,1792]{1,0:T(8,128)(2,1)S(1)}, u32[]{:S(2)}, u32[]{:S(2)}) collective-permute-start(bf16[48,1792]{1,0:T(8,128)(2,1)S(1)} %get-tuple-element.37.refs_2_), channel_id=1, source_target_pairs={{0,1},{1,0},{2,3},{3,2},{4,5},{5,4},{6,7},{7,6},{8,9},{9,8},{10,11... | collective-permute-start | bytes 516104 | tf_op jit(solution)/shard_map/ppermute | solution.py:302
  26.9 6.3 %collective-permute-start.8 = (bf16[48,1792]{1,0:T(8,128)(2,1)S(1)}, bf16[48,1792]{1,0:T(8,128)(2,1)S(1)}, u32[]{:S(2)}, u32[]{:S(2)}) collective-permute-start(bf16[48,1792]{1,0:T(8,128)(2,1)S(1)} %get-tuple-element.39), channel_id=1, source_target_pairs={{0,2},{1,3},{2,0},{3,1},{4,6},{5,7},{6,4},{7,5},{8,10},{9,11},{10,... | collective-permute-start | bytes 516104 | tf_op jit(solution)/shard_map/ppermute | solution.py:302
  30.4 6.3 %collective-permute-start.11 = (bf16[48,1792]{1,0:T(8,128)(2,1)S(1)}, bf16[48,1792]{1,0:T(8,128)(2,1)S(1)}, u32[]{:S(2)}, u32[]{:S(2)}) collective-permute-start(bf16[48,1792]{1,0:T(8,128)(2,1)S(1)} %get-tuple-element.43), channel_id=1, source_target_pairs={{0,1},{1,0},{2,3},{3,2},{4,5},{5,4},{6,7},{7,6},{8,9},{9,8},{10,11... | collective-permute-start | bytes 516104 | tf_op jit(solution)/shard_map/ppermute | solution.py:302
  30.8 5.9 %collective-permute-start.13 = (bf16[48,1792]{1,0:T(8,128)(2,1)S(1)}, bf16[48,1792]{1,0:T(8,128)(2,1)S(1)}, u32[]{:S(2)}, u32[]{:S(2)}) collective-permute-start(bf16[48,1792]{1,0:T(8,128)(2,1)S(1)} %get-tuple-element.45), channel_id=1, source_target_pairs={{0,2},{1,3},{2,0},{3,1},{4,6},{5,7},{6,4},{7,5},{8,10},{9,11},{10,... | collective-permute-start | bytes 516104 | tf_op jit(solution)/shard_map/ppermute | solution.py:302
  33.3 5.5 %collective-permute-start.9 = (bf16[48,1792]{1,0:T(8,128)(2,1)S(1)}, bf16[48,1792]{1,0:T(8,128)(2,1)S(1)}, u32[]{:S(2)}, u32[]{:S(2)}) collective-permute-start(bf16[48,1792]{1,0:T(8,128)(2,1)S(1)} %add_convert_fusion.2), channel_id=1, source_target_pairs={{0,1},{1,0},{2,3},{3,2},{4,5},{5,4},{6,7},{7,6},{8,9},{9,8},{10,11... | collective-permute-start | bytes 516104 | tf_op jit(solution)/shard_map/ppermute | solution.py:302
  38.8 6.5 %collective-permute-start.14 = (bf16[48,1792]{1,0:T(8,128)(2,1)S(1)}, bf16[48,1792]{1,0:T(8,128)(2,1)S(1)}, u32[]{:S(2)}, u32[]{:S(2)}) collective-permute-start(bf16[48,1792]{1,0:T(8,128)(2,1)S(1)} %add_convert_fusion), channel_id=1, source_target_pairs={{0,4},{1,5},{2,6},{3,7},{4,0},{5,1},{6,2},{7,3},{8,12},{9,13},{10,... | collective-permute-start | bytes 516104 | tf_op jit(solution)/shard_map/ppermute | solution.py:302
  40.0 7.1 %collective-permute-start.12 = (bf16[48,1792]{1,0:T(8,128)(2,1)S(1)}, bf16[48,1792]{1,0:T(8,128)(2,1)S(1)}, u32[]{:S(2)}, u32[]{:S(2)}) collective-permute-start(bf16[48,1792]{1,0:T(8,128)(2,1)S(1)} %add_convert_fusion.1), channel_id=1, source_target_pairs={{0,2},{1,3},{2,0},{3,1},{4,6},{5,7},{6,4},{7,5},{8,10},{9,11},{10,... | collective-permute-start | bytes 516104 | tf_op jit(solution)/shard_map/ppermute | solution.py:302
  41.5 5.6 %collective-permute-start.10 = (bf16[48,1792]{1,0:T(8,128)(2,1)S(1)}, bf16[48,1792]{1,0:T(8,128)(2,1)S(1)}, u32[]{:S(2)}, u32[]{:S(2)}) collective-permute-start(bf16[48,1792]{1,0:T(8,128)(2,1)S(1)} %get-tuple-element.41), channel_id=1, source_target_pairs={{0,1},{1,0},{2,3},{3,2},{4,5},{5,4},{6,7},{7,6},{8,9},{9,8},{10,11... | collective-permute-start | bytes 516104 | tf_op jit(solution)/shard_map/ppermute | solution.py:302
  47.1 1.3 %collective-permute-start.15 = (bf16[24,1792]{1,0:T(8,128)(2,1)S(1)}, bf16[24,1792]{1,0:T(8,128)(2,1)S(1)}, u32[]{:S(2)}, u32[]{:S(2)}) collective-permute-start(bf16[24,1792]{1,0:T(8,128)(2,1)S(1)} %add_convert_fusion.3), channel_id=1, source_target_pairs={{0,8},{8,0},{1,9},{9,1},{2,10},{10,2},{3,11},{11,3},{4,12},{12,4},... | collective-permute-start | bytes 258056 | tf_op jit(solution)/shard_map/ppermute | solution.py:306

commit v5 on v4

--- a/solution.py
+++ b/solution.py
@@ -316,7 +316,8 @@
     block = jnp.concatenate([own, swap_cores(other)], axis=0)
     loaded = load_weights(gate_weight, up_weight, down_weight)
     (six,) = join(swap(block, 6), cost=1 * LATE)
-    six, one, two, *loaded = join(six, swap(block, 1), swap(block, 2), *loaded)
+    one = swap(block, 1)
+    six, two, *loaded = join(six, swap(block, 2), *loaded)
     (four,) = join(swap(six, 2), cost=1 * LATE)
     four, seven = join(four, swap(six, 1))
     five = swap(four, 1)

time: 50.2 us -> 50 us (level)
  transfers between devices with their start and end apart: 16 -> 16, of which waited for: 10 -> 9; matrix products, arithmetic and copies ran while one was open for 0% -> 0% of each run, Pallas kernels for 14% -> 14%
where the time goes in v5:
time: 50 us; the launch traced here: 49.9 us
  waiting for transfers between devices  19.7 us (39%)
  starting transfers between devices  19.4 us (39%)
  Pallas kernels  10.5 us (21%)
    ppermute x14, starting transfers between devices, swap(): return lax.ppermute(x, 'local', [(i, i ^ mask) for i in range(SPLIT)])  18.8 us
    ppermute x14, waiting for transfers between devices, swap(): return lax.ppermute(x, 'local', [(i, i ^ mask) for i in range(SPLIT)])  17.5 us
    pallas_call x3, Pallas kernels, experts(): pl.pallas_call(kernel, in_specs=[pl.BlockSpec(memory_space=pltpu.VMEM)] *...  4.37 us
    pallas_call x1, Pallas kernels, load_weights(): pl.pallas_call(kernel, in_specs=[pl.BlockSpec(memory_space=pltpu.HBM)] *...  2.59 us
    ppermute x2, waiting for transfers between devices, swap_cores(): return lax.ppermute(x, 'hst', [(0, 1), (1, 0)])  2.19 us
    pallas_call x1, Pallas kernels, select_rows(): pl.pallas_call(kernel, in_specs=[pl.BlockSpec(memory_space=pltpu.SMEM)] +...  1.89 us
    pallas_call x1, Pallas kernels, combine(): pl.pallas_call(kernel, in_specs=[pl.BlockSpec(memory_space=pltpu.VMEM)] *...  1.62 us
  transfers between devices with their start and end apart: 16, of which 9 were waited for; matrix products, arithmetic and copies ran while one was open for 0% of the time, Pallas kernels for 14%

profile of v5, /device:TPU:0, one launch (start us, length us, event | category | flops | bytes accessed | tf_op | source)
XLA Modules:
  0.0 49.9 jit_solution(431127363739693091)
XLA Ops:
  0.0 1.9 %select_rows.1 = (bf16[24,1792]{1,0:T(8,128)(2,1)S(1)}, bf16[24,1792]{1,0:T(8,128)(2,1)S(1)}, f32[2,24,128]{2,1,0:T(8,128)S(1)}, f32[2,24,128]{2,1,0:T(8,128)S(1)}) custom-call(s32[1]{0:T(128)} %bitcast.core_ref, s32[8,128]{1,0:T(8,128)} %bitcast.3, f32[8,128]{1,0:T(8,128)} %bitcast.4, bf16[128,7168]{1,0:T(8,128)(2,1)} %tokens_hbm.1), custom_call_target="tpu_custom_call" | custom-call | tf_op jit(solution)/shard_map/select_rows/pallas_call | solution.py:180
  1.9 0.5 %collective-permute-start = (bf16[24,1792]{1,0:T(8,128)(2,1)S(1)}, bf16[24,1792]{1,0:T(8,128)(2,1)S(1)}, u32[]{:S(2)}, u32[]{:S(2)}) collective-permute-start(bf16[24,1792]{1,0:T(8,128)(2,1)S(1)} %get-tuple-element.27), channel_id=1, source_target_pairs={{0,8},{8,0},{1,9},{9,1},{2,10},{10,2},{3,11},{11,3},{4,12},{12,4},... | collective-permute-start | bytes 258056 | tf_op jit(solution)/shard_map/ppermute | solution.py:306
  2.4 0.9 %collective-permute-done = bf16[24,1792]{1,0:T(8,128)(2,1)S(1)} collective-permute-done((bf16[24,1792]{1,0:T(8,128)(2,1)S(1)}, bf16[24,1792]{1,0:T(8,128)(2,1)S(1)}, u32[]{:S(2)}, u32[]{:S(2)}) %collective-permute-start) | collective-permute-done | bytes 86048 | tf_op jit(solution)/shard_map/ppermute | solution.py:306
  3.4 5.0 %collective-permute-start.2 = (bf16[48,1792]{1,0:T(8,128)(2,1)S(1)}, bf16[48,1792]{1,0:T(8,128)(2,1)S(1)}, u32[]{:S(2)}, u32[]{:S(2)}) collective-permute-start(bf16[48,1792]{1,0:T(8,128)(2,1)S(1)} %constant_dynamic-update-slice_fusion.refs_0_), channel_id=1, source_target_pairs={{0,6},{1,7},{2,4},{3,5},{4,2},{5,3},{6,0},{7,1},{8,14},{9,15},{10,... | collective-permute-start | bytes 516104 | tf_op jit(solution)/shard_map/ppermute | solution.py:302
  8.4 0.0 collective-permute-start.3
  8.4 1.5 %collective-permute-start.1 = (bf16[48,1792]{1,0:T(8,128)(2,1)S(1)}, bf16[48,1792]{1,0:T(8,128)(2,1)S(1)}, u32[]{:S(2)}, u32[]{:S(2)}) collective-permute-start(bf16[48,1792]{1,0:T(8,128)(2,1)S(1)} %constant_dynamic-update-slice_fusion.refs_0_), channel_id=1, source_target_pairs={{0,1},{1,0},{2,3},{3,2},{4,5},{5,4},{6,7},{7,6},{8,9},{9,8},{10,11... | collective-permute-start | bytes 516104 | tf_op jit(solution)/shard_map/ppermute | solution.py:302
  9.9 2.6 %load_weights.1 = (bf16[7168,256]{1,0:T(8,128)(2,1)S(1)}, bf16[512,1792]{1,0:T(8,128)(2,1)S(1)}) custom-call(bf16[7168,128]{1,0:T(8,128)(2,1)} %gate_hbm.1, bf16[7168,128]{1,0:T(8,128)(2,1)} %up_hbm.1, bf16[128,7168]{1,0:T(8,128)(2,1)} %down_hbm.1), custom_call_target="tpu_custom_call" | custom-call | tf_op jit(solution)/shard_map/load_weights/pallas_call | solution.py:113
  12.5 1.1 %collective-permute-done.2.refs_0_ = bf16[48,1792]{1,0:T(8,128)(2,1)S(1)} collective-permute-done((bf16[48,1792]{1,0:T(8,128)(2,1)S(1)}, bf16[48,1792]{1,0:T(8,128)(2,1)S(1)}, u32[]{:S(2)}, u32[]{:S(2)}) %collective-permute-start.2) | collective-permute-done | bytes 172064 | tf_op jit(solution)/shard_map/ppermute | solution.py:302
  13.6 3.2 %collective-permute-done.3.refs_1_ = bf16[48,1792]{1,0:T(8,128)(2,1)S(1)} collective-permute-done((bf16[48,1792]{1,0:T(8,128)(2,1)S(1)}, bf16[48,1792]{1,0:T(8,128)(2,1)S(1)}, u32[]{:S(2)}, u32[]{:S(2)}) %collective-permute-start.3) | collective-permute-done | bytes 172064 | tf_op jit(solution)/shard_map/ppermute | solution.py:302
  16.8 1.7 %collective-permute-start.5 = (bf16[48,1792]{1,0:T(8,128)(2,1)S(1)}, bf16[48,1792]{1,0:T(8,128)(2,1)S(1)}, u32[]{:S(2)}, u32[]{:S(2)}) collective-permute-start(bf16[48,1792]{1,0:T(8,128)(2,1)S(1)} %get-tuple-element.34.refs_1_), channel_id=1, source_target_pairs={{0,2},{1,3},{2,0},{3,1},{4,6},{5,7},{6,4},{7,5},{8,10},{9,11},{10,... | collective-permute-start | bytes 516104 | tf_op jit(solution)/shard_map/ppermute | solution.py:302
  18.5 1.5 %collective-permute-start.6 = (bf16[48,1792]{1,0:T(8,128)(2,1)S(1)}, bf16[48,1792]{1,0:T(8,128)(2,1)S(1)}, u32[]{:S(2)}, u32[]{:S(2)}) collective-permute-start(bf16[48,1792]{1,0:T(8,128)(2,1)S(1)} %get-tuple-element.34.refs_1_), channel_id=1, source_target_pairs={{0,1},{1,0},{2,3},{3,2},{4,5},{5,4},{6,7},{7,6},{8,9},{9,8},{10,11... | collective-permute-start | bytes 516104 | tf_op jit(solution)/shard_map/ppermute | solution.py:302
  20.0 0.0 collective-permute-done.1.refs_1_
  20.0 0.3 collective-permute-start.4
  20.3 3.7 %collective-permute-done.5.refs_0_ = bf16[48,1792]{1,0:T(8,128)(2,1)S(1)} collective-permute-done((bf16[48,1792]{1,0:T(8,128)(2,1)S(1)}, bf16[48,1792]{1,0:T(8,128)(2,1)S(1)}, u32[]{:S(2)}, u32[]{:S(2)}) %collective-permute-start.5) | collective-permute-done | bytes 172064 | tf_op jit(solution)/shard_map/ppermute | solution.py:302
  24.0 0.0 collective-permute-done.6.refs_1_
  24.0 1.5 %collective-permute-start.7 = (bf16[48,1792]{1,0:T(8,128)(2,1)S(1)}, bf16[48,1792]{1,0:T(8,128)(2,1)S(1)}, u32[]{:S(2)}, u32[]{:S(2)}) collective-permute-start(bf16[48,1792]{1,0:T(8,128)(2,1)S(1)} %get-tuple-element.35.refs_2_), channel_id=1, source_target_pairs={{0,1},{1,0},{2,3},{3,2},{4,5},{5,4},{6,7},{7,6},{8,9},{9,8},{10,11... | collective-permute-start | bytes 516104 | tf_op jit(solution)/shard_map/ppermute | solution.py:302
  25.5 1.4 %experts.5 = (bf16[48,1792]{1,0:T(8,128)(2,1)S(1)}, bf16[48,1792]{1,0:T(8,128)(2,1)S(1)}, bf16[48,1792]{1,0:T(8,128)(2,1)S(1)}) custom-call(bf16[48,1792]{1,0:T(8,128)(2,1)S(1)} %get-tuple-element.36.refs_0_, bf16[48,1792]{1,0:T(8,128)(2,1)S(1)} %get-tuple-element.34.refs_1_, bf16[48,1792]{1,0:T(8,128)(2,1)S(1)} %get-tuple-element.35.refs_2_, ...), custom_call_target="tpu_custom_call" | custom-call | flops 792723456 | bytes 5505024 | tf_op jit(solution)/shard_map/experts/pallas_call | solution.py:240
  26.9 1.8 %collective-permute-start.8 = (bf16[48,1792]{1,0:T(8,128)(2,1)S(1)}, bf16[48,1792]{1,0:T(8,128)(2,1)S(1)}, u32[]{:S(2)}, u32[]{:S(2)}) collective-permute-start(bf16[48,1792]{1,0:T(8,128)(2,1)S(1)} %get-tuple-element.37), channel_id=1, source_target_pairs={{0,2},{1,3},{2,0},{3,1},{4,6},{5,7},{6,4},{7,5},{8,10},{9,11},{10,... | collective-permute-start | bytes 516104 | tf_op jit(solution)/shard_map/ppermute | solution.py:302
  28.7 0.3 collective-permute-start.13
  29.0 0.0 collective-permute-done.4.refs_0_
  29.0 1.7 %experts.3 = (bf16[48,1792]{1,0:T(8,128)(2,1)S(1)}, bf16[48,1792]{1,0:T(8,128)(2,1)S(1)}, bf16[48,1792]{1,0:T(8,128)(2,1)S(1)}, bf16[48,1792]{1,0:T(8,128)(2,1)S(1)}) custom-call(bf16[48,1792]{1,0:T(8,128)(2,1)S(1)} %constant_dynamic-update-slice_fusion.refs_0_, bf16[48,1792]{1,0:T(8,128)(2,1)S(1)} %collective-permute-done.1.refs_1_, ...), custom_call_target="tpu_custom_call" | custom-call | flops 1056964608 | bytes 5505024 | tf_op jit(solution)/shard_map/experts/pallas_call | solution.py:240
  30.7 0.6 %collective-permute-start.11 = (bf16[48,1792]{1,0:T(8,128)(2,1)S(1)}, bf16[48,1792]{1,0:T(8,128)(2,1)S(1)}, u32[]{:S(2)}, u32[]{:S(2)}) collective-permute-start(bf16[48,1792]{1,0:T(8,128)(2,1)S(1)} %get-tuple-element.41), channel_id=1, source_target_pairs={{0,1},{1,0},{2,3},{3,2},{4,5},{5,4},{6,7},{7,6},{8,9},{9,8},{10,11... | collective-permute-start | bytes 516104 | tf_op jit(solution)/shard_map/ppermute | solution.py:302
  31.2 0.0 collective-permute-done.7.refs_0_
  31.2 1.4 %experts.4 = bf16[48,1792]{1,0:T(8,128)(2,1)S(1)} custom-call(bf16[48,1792]{1,0:T(8,128)(2,1)S(1)} %collective-permute-done.7.refs_0_, bf16[7168,256]{1,0:T(8,128)(2,1)S(1)} %get-tuple-element.31.refs_4_.refs_1_.refs_3_, bf16[512,1792]{1,0:T(8,128)(2,1)S(1)} %get-tuple-element.32.refs_5_.refs_2_.refs_4_), custom_call_target="tpu_custom_call" | custom-call | flops 264241152 | bytes 5505024 | tf_op jit(solution)/shard_map/experts/pallas_call | solution.py:240
  32.6 0.5 collective-permute-done.8
  33.1 1.2 %collective-permute-start.9 = (bf16[48,1792]{1,0:T(8,128)(2,1)S(1)}, bf16[48,1792]{1,0:T(8,128)(2,1)S(1)}, u32[]{:S(2)}, u32[]{:S(2)}) collective-permute-start(bf16[48,1792]{1,0:T(8,128)(2,1)S(1)} %add_convert_fusion.2), channel_id=1, source_target_pairs={{0,1},{1,0},{2,3},{3,2},{4,5},{5,4},{6,7},{7,6},{8,9},{9,8},{10,11... | collective-permute-start | bytes 516104 | tf_op jit(solution)/shard_map/ppermute | solution.py:302
  34.3 2.4 %collective-permute-done.11 = bf16[48,1792]{1,0:T(8,128)(2,1)S(1)} collective-permute-done((bf16[48,1792]{1,0:T(8,128)(2,1)S(1)}, bf16[48,1792]{1,0:T(8,128)(2,1)S(1)}, u32[]{:S(2)}, u32[]{:S(2)}) %collective-permute-start.11) | collective-permute-done | bytes 172064 | tf_op jit(solution)/shard_map/ppermute | solution.py:302
  36.7 0.0 collective-permute-done.13.refs_0_
  36.7 1.8 %collective-permute-done.9.refs_0_ = bf16[48,1792]{1,0:T(8,128)(2,1)S(1)} collective-permute-done((bf16[48,1792]{1,0:T(8,128)(2,1)S(1)}, bf16[48,1792]{1,0:T(8,128)(2,1)S(1)}, u32[]{:S(2)}, u32[]{:S(2)}) %collective-permute-start.9) | collective-permute-done | bytes 172064 | tf_op jit(solution)/shard_map/ppermute | solution.py:302
  38.6 0.1 add_convert_fusion
  38.6 0.2 collective-permute-start.14
  38.9 1.8 %collective-permute-start.12 = (bf16[48,1792]{1,0:T(8,128)(2,1)S(1)}, bf16[48,1792]{1,0:T(8,128)(2,1)S(1)}, u32[]{:S(2)}, u32[]{:S(2)}) collective-permute-start(bf16[48,1792]{1,0:T(8,128)(2,1)S(1)} %add_convert_fusion.1), channel_id=1, source_target_pairs={{0,2},{1,3},{2,0},{3,1},{4,6},{5,7},{6,4},{7,5},{8,10},{9,11},{10,... | collective-permute-start | bytes 516104 | tf_op jit(solution)/shard_map/ppermute | solution.py:302
  40.6 1.4 %collective-permute-start.10 = (bf16[48,1792]{1,0:T(8,128)(2,1)S(1)}, bf16[48,1792]{1,0:T(8,128)(2,1)S(1)}, u32[]{:S(2)}, u32[]{:S(2)}) collective-permute-start(bf16[48,1792]{1,0:T(8,128)(2,1)S(1)} %get-tuple-element.39), channel_id=1, source_target_pairs={{0,1},{1,0},{2,3},{3,2},{4,5},{5,4},{6,7},{7,6},{8,9},{9,8},{10,11... | collective-permute-start | bytes 516104 | tf_op jit(solution)/shard_map/ppermute | solution.py:302
  42.0 4.8 %collective-permute-done.14.refs_0_ = bf16[48,1792]{1,0:T(8,128)(2,1)S(1)} collective-permute-done((bf16[48,1792]{1,0:T(8,128)(2,1)S(1)}, bf16[48,1792]{1,0:T(8,128)(2,1)S(1)}, u32[]{:S(2)}, u32[]{:S(2)}) %collective-permute-start.14) | collective-permute-done | bytes 172064 | tf_op jit(solution)/shard_map/ppermute | solution.py:302
  46.9 0.0 collective-permute-done.12.refs_2_
  46.9 0.0 collective-permute-done.10.refs_1_
  46.9 0.1 collective-permute-start.15
  47.0 1.3 %collective-permute-done.15.refs_4_ = bf16[24,1792]{1,0:T(8,128)(2,1)S(1)} collective-permute-done((bf16[24,1792]{1,0:T(8,128)(2,1)S(1)}, bf16[24,1792]{1,0:T(8,128)(2,1)S(1)}, u32[]{:S(2)}, u32[]{:S(2)}) %collective-permute-start.15) | collective-permute-done | bytes 86048 | tf_op jit(solution)/shard_map/ppermute | solution.py:306
  48.3 1.6 %combine.1 = bf16[128,7168]{1,0:T(8,128)(2,1)} custom-call(bf16[48,1792]{1,0:T(8,128)(2,1)S(1)} %get-tuple-element.33.refs_0_, bf16[48,1792]{1,0:T(8,128)(2,1)S(1)} %collective-permute-done.10.refs_1_, bf16[48,1792]{1,0:T(8,128)(2,1)S(1)} %collective-permute-done.12.refs_2_, bf16[48,1792]{1,0:T(8,128)(2,1)S(1)} %join.15.refs_3_, ...), custom_call_target="tpu_custom_call" | custom-call | tf_op jit(solution)/shard_map/combine/pallas_call | solution.py:287
  (13 shorter events, 0.2 us)
Async XLA Ops:
  1.9 1.4 %collective-permute-start = (bf16[24,1792]{1,0:T(8,128)(2,1)S(1)}, bf16[24,1792]{1,0:T(8,128)(2,1)S(1)}, u32[]{:S(2)}, u32[]{:S(2)}) collective-permute-start(bf16[24,1792]{1,0:T(8,128)(2,1)S(1)} %get-tuple-element.27), channel_id=1, source_target_pairs={{0,8},{8,0},{1,9},{9,1},{2,10},{10,2},{3,11},{11,3},{4,12},{12,4},... | collective-permute-start | bytes 258056 | tf_op jit(solution)/shard_map/ppermute | solution.py:306
  3.4 10.2 %collective-permute-start.2 = (bf16[48,1792]{1,0:T(8,128)(2,1)S(1)}, bf16[48,1792]{1,0:T(8,128)(2,1)S(1)}, u32[]{:S(2)}, u32[]{:S(2)}) collective-permute-start(bf16[48,1792]{1,0:T(8,128)(2,1)S(1)} %constant_dynamic-update-slice_fusion.refs_0_), channel_id=1, source_target_pairs={{0,6},{1,7},{2,4},{3,5},{4,2},{5,3},{6,0},{7,1},{8,14},{9,15},{10,... | collective-permute-start | bytes 516104 | tf_op jit(solution)/shard_map/ppermute | solution.py:302
  8.4 8.4 %collective-permute-start.3 = (bf16[48,1792]{1,0:T(8,128)(2,1)S(1)}, bf16[48,1792]{1,0:T(8,128)(2,1)S(1)}, u32[]{:S(2)}, u32[]{:S(2)}) collective-permute-start(bf16[48,1792]{1,0:T(8,128)(2,1)S(1)} %constant_dynamic-update-slice_fusion.refs_0_), channel_id=1, source_target_pairs={{0,2},{1,3},{2,0},{3,1},{4,6},{5,7},{6,4},{7,5},{8,10},{9,11},{10,... | collective-permute-start | bytes 516104 | tf_op jit(solution)/shard_map/ppermute | solution.py:302
  8.4 11.6 %collective-permute-start.1 = (bf16[48,1792]{1,0:T(8,128)(2,1)S(1)}, bf16[48,1792]{1,0:T(8,128)(2,1)S(1)}, u32[]{:S(2)}, u32[]{:S(2)}) collective-permute-start(bf16[48,1792]{1,0:T(8,128)(2,1)S(1)} %constant_dynamic-update-slice_fusion.refs_0_), channel_id=1, source_target_pairs={{0,1},{1,0},{2,3},{3,2},{4,5},{5,4},{6,7},{7,6},{8,9},{9,8},{10,11... | collective-permute-start | bytes 516104 | tf_op jit(solution)/shard_map/ppermute | solution.py:302
  16.8 7.2 %collective-permute-start.5 = (bf16[48,1792]{1,0:T(8,128)(2,1)S(1)}, bf16[48,1792]{1,0:T(8,128)(2,1)S(1)}, u32[]{:S(2)}, u32[]{:S(2)}) collective-permute-start(bf16[48,1792]{1,0:T(8,128)(2,1)S(1)} %get-tuple-element.34.refs_1_), channel_id=1, source_target_pairs={{0,2},{1,3},{2,0},{3,1},{4,6},{5,7},{6,4},{7,5},{8,10},{9,11},{10,... | collective-permute-start | bytes 516104 | tf_op jit(solution)/shard_map/ppermute | solution.py:302
  18.5 5.6 %collective-permute-start.6 = (bf16[48,1792]{1,0:T(8,128)(2,1)S(1)}, bf16[48,1792]{1,0:T(8,128)(2,1)S(1)}, u32[]{:S(2)}, u32[]{:S(2)}) collective-permute-start(bf16[48,1792]{1,0:T(8,128)(2,1)S(1)} %get-tuple-element.34.refs_1_), channel_id=1, source_target_pairs={{0,1},{1,0},{2,3},{3,2},{4,5},{5,4},{6,7},{7,6},{8,9},{9,8},{10,11... | collective-permute-start | bytes 516104 | tf_op jit(solution)/shard_map/ppermute | solution.py:302
  20.0 9.0 %collective-permute-start.4 = (bf16[48,1792]{1,0:T(8,128)(2,1)S(1)}, bf16[48,1792]{1,0:T(8,128)(2,1)S(1)}, u32[]{:S(2)}, u32[]{:S(2)}) collective-permute-start(bf16[48,1792]{1,0:T(8,128)(2,1)S(1)} %collective-permute-done.1.refs_1_), channel_id=1, source_target_pairs={{0,2},{1,3},{2,0},{3,1},{4,6},{5,7},{6,4},{7,5},{8,10},{9,11},{10,... | collective-permute-start | bytes 516104 | tf_op jit(solution)/shard_map/ppermute | solution.py:302
  24.0 7.2 %collective-permute-start.7 = (bf16[48,1792]{1,0:T(8,128)(2,1)S(1)}, bf16[48,1792]{1,0:T(8,128)(2,1)S(1)}, u32[]{:S(2)}, u32[]{:S(2)}) collective-permute-start(bf16[48,1792]{1,0:T(8,128)(2,1)S(1)} %get-tuple-element.35.refs_2_), channel_id=1, source_target_pairs={{0,1},{1,0},{2,3},{3,2},{4,5},{5,4},{6,7},{7,6},{8,9},{9,8},{10,11... | collective-permute-start | bytes 516104 | tf_op jit(solution)/shard_map/ppermute | solution.py:302
  26.9 6.1 %collective-permute-start.8 = (bf16[48,1792]{1,0:T(8,128)(2,1)S(1)}, bf16[48,1792]{1,0:T(8,128)(2,1)S(1)}, u32[]{:S(2)}, u32[]{:S(2)}) collective-permute-start(bf16[48,1792]{1,0:T(8,128)(2,1)S(1)} %get-tuple-element.37), channel_id=1, source_target_pairs={{0,2},{1,3},{2,0},{3,1},{4,6},{5,7},{6,4},{7,5},{8,10},{9,11},{10,... | collective-permute-start | bytes 516104 | tf_op jit(solution)/shard_map/ppermute | solution.py:302
  28.7 8.0 %collective-permute-start.13 = (bf16[48,1792]{1,0:T(8,128)(2,1)S(1)}, bf16[48,1792]{1,0:T(8,128)(2,1)S(1)}, u32[]{:S(2)}, u32[]{:S(2)}) collective-permute-start(bf16[48,1792]{1,0:T(8,128)(2,1)S(1)} %get-tuple-element.43), channel_id=1, source_target_pairs={{0,2},{1,3},{2,0},{3,1},{4,6},{5,7},{6,4},{7,5},{8,10},{9,11},{10,... | collective-permute-start | bytes 516104 | tf_op jit(solution)/shard_map/ppermute | solution.py:302
  30.7 6.0 %collective-permute-start.11 = (bf16[48,1792]{1,0:T(8,128)(2,1)S(1)}, bf16[48,1792]{1,0:T(8,128)(2,1)S(1)}, u32[]{:S(2)}, u32[]{:S(2)}) collective-permute-start(bf16[48,1792]{1,0:T(8,128)(2,1)S(1)} %get-tuple-element.41), channel_id=1, source_target_pairs={{0,1},{1,0},{2,3},{3,2},{4,5},{5,4},{6,7},{7,6},{8,9},{9,8},{10,11... | collective-permute-start | bytes 516104 | tf_op jit(solution)/shard_map/ppermute | solution.py:302
  33.1 5.5 %collective-permute-start.9 = (bf16[48,1792]{1,0:T(8,128)(2,1)S(1)}, bf16[48,1792]{1,0:T(8,128)(2,1)S(1)}, u32[]{:S(2)}, u32[]{:S(2)}) collective-permute-start(bf16[48,1792]{1,0:T(8,128)(2,1)S(1)} %add_convert_fusion.2), channel_id=1, source_target_pairs={{0,1},{1,0},{2,3},{3,2},{4,5},{5,4},{6,7},{7,6},{8,9},{9,8},{10,11... | collective-permute-start | bytes 516104 | tf_op jit(solution)/shard_map/ppermute | solution.py:302
  38.6 8.2 %collective-permute-start.14 = (bf16[48,1792]{1,0:T(8,128)(2,1)S(1)}, bf16[48,1792]{1,0:T(8,128)(2,1)S(1)}, u32[]{:S(2)}, u32[]{:S(2)}) collective-permute-start(bf16[48,1792]{1,0:T(8,128)(2,1)S(1)} %add_convert_fusion), channel_id=1, source_target_pairs={{0,4},{1,5},{2,6},{3,7},{4,0},{5,1},{6,2},{7,3},{8,12},{9,13},{10,... | collective-permute-start | bytes 516104 | tf_op jit(solution)/shard_map/ppermute | solution.py:302
  38.9 8.0 %collective-permute-start.12 = (bf16[48,1792]{1,0:T(8,128)(2,1)S(1)}, bf16[48,1792]{1,0:T(8,128)(2,1)S(1)}, u32[]{:S(2)}, u32[]{:S(2)}) collective-permute-start(bf16[48,1792]{1,0:T(8,128)(2,1)S(1)} %add_convert_fusion.1), channel_id=1, source_target_pairs={{0,2},{1,3},{2,0},{3,1},{4,6},{5,7},{6,4},{7,5},{8,10},{9,11},{10,... | collective-permute-start | bytes 516104 | tf_op jit(solution)/shard_map/ppermute | solution.py:302
  40.6 6.2 %collective-permute-start.10 = (bf16[48,1792]{1,0:T(8,128)(2,1)S(1)}, bf16[48,1792]{1,0:T(8,128)(2,1)S(1)}, u32[]{:S(2)}, u32[]{:S(2)}) collective-permute-start(bf16[48,1792]{1,0:T(8,128)(2,1)S(1)} %get-tuple-element.39), channel_id=1, source_target_pairs={{0,1},{1,0},{2,3},{3,2},{4,5},{5,4},{6,7},{7,6},{8,9},{9,8},{10,11... | collective-permute-start | bytes 516104 | tf_op jit(solution)/shard_map/ppermute | solution.py:302
  46.9 1.3 %collective-permute-start.15 = (bf16[24,1792]{1,0:T(8,128)(2,1)S(1)}, bf16[24,1792]{1,0:T(8,128)(2,1)S(1)}, u32[]{:S(2)}, u32[]{:S(2)}) collective-permute-start(bf16[24,1792]{1,0:T(8,128)(2,1)S(1)} %add_convert_fusion.3), channel_id=1, source_target_pairs={{0,8},{8,0},{1,9},{9,1},{2,10},{10,2},{3,11},{11,3},{4,12},{12,4},... | collective-permute-start | bytes 258056 | tf_op jit(solution)/shard_map/ppermute | solution.py:306

commit v6 on v5

--- a/solution.py
+++ b/solution.py
@@ -319,11 +319,12 @@
     one = swap(block, 1)
     six, two, *loaded = join(six, swap(block, 2), *loaded)
     (four,) = join(swap(six, 2), cost=1 * LATE)
-    four, seven = join(four, swap(six, 1))
+    part0, part1, part2 = experts([block, one, two], *loaded)
+    four, seven, part0 = join(four, swap(six, 1), part0)
     five = swap(four, 1)
     (three,) = join(swap(one, 2), cost=3 * LATE)
     part7, part6, part4 = experts([seven, six, four], *loaded)
-    part0, part1, part2, part3 = experts([block, one, two, three], *loaded)
+    (part3,) = experts([three], *loaded)
     (part5,) = experts([five], *loaded)
     half = swap(add(part5, swap(part7, 2)), 1)
     half, part1 = join(half, part1)

time: 50 us -> 50.1 us (level)
  Pallas kernels: 10.5 us -> 11.5 us
  starting transfers between devices: 19.4 us -> 18.8 us
    pallas_call x3 -> x4, Pallas kernels: 4.37 us -> 5.4 us  [experts(): pl.pallas_call(kernel, in_specs=[pl.BlockSpec(memory_space=pltpu.VMEM)] *...]
    ppermute x14, starting transfers between devices: 18.8 us -> 18.2 us  [swap(): return lax.ppermute(x, 'local', [(i, i ^ mask) for i in range(SPLIT)])]
  transfers between devices with their start and end apart: 16 -> 16, of which waited for: 9 -> 9; matrix products, arithmetic and copies ran while one was open for 0% -> 0% of each run, Pallas kernels for 14% -> 16%
where the time goes in v6:
time: 50.1 us; the launch traced here: 49.9 us
  waiting for transfers between devices  19.3 us (39%)
  starting transfers between devices  18.8 us (38%)
  Pallas kernels  11.5 us (23%)
    ppermute x14, starting transfers between devices, swap(): return lax.ppermute(x, 'local', [(i, i ^ mask) for i in range(SPLIT)])  18.2 us
    ppermute x14, waiting for transfers between devices, swap(): return lax.ppermute(x, 'local', [(i, i ^ mask) for i in range(SPLIT)])  17.1 us
    pallas_call x4, Pallas kernels, experts(): pl.pallas_call(kernel, in_specs=[pl.BlockSpec(memory_space=pltpu.VMEM)] *...  5.4 us
    pallas_call x1, Pallas kernels, load_weights(): pl.pallas_call(kernel, in_specs=[pl.BlockSpec(memory_space=pltpu.HBM)] *...  2.59 us
    ppermute x2, waiting for transfers between devices, swap_cores(): return lax.ppermute(x, 'hst', [(0, 1), (1, 0)])  2.19 us
    pallas_call x1, Pallas kernels, select_rows(): pl.pallas_call(kernel, in_specs=[pl.BlockSpec(memory_space=pltpu.SMEM)] +...  1.89 us
    pallas_call x1, Pallas kernels, combine(): pl.pallas_call(kernel, in_specs=[pl.BlockSpec(memory_space=pltpu.VMEM)] *...  1.62 us
  transfers between devices with their start and end apart: 16, of which 9 were waited for; matrix products, arithmetic and copies ran while one was open for 0% of the time, Pallas kernels for 16%

profile of v6, /device:TPU:0, one launch (start us, length us, event | category | flops | bytes accessed | tf_op | source)
XLA Modules:
  0.0 49.9 jit_solution(15911104229547197900)
XLA Ops:
  0.0 1.9 %select_rows.1 = (bf16[24,1792]{1,0:T(8,128)(2,1)S(1)}, bf16[24,1792]{1,0:T(8,128)(2,1)S(1)}, f32[2,24,128]{2,1,0:T(8,128)S(1)}, f32[2,24,128]{2,1,0:T(8,128)S(1)}) custom-call(s32[1]{0:T(128)} %bitcast.core_ref, s32[8,128]{1,0:T(8,128)} %bitcast.3, f32[8,128]{1,0:T(8,128)} %bitcast.4, bf16[128,7168]{1,0:T(8,128)(2,1)} %tokens_hbm.1), custom_call_target="tpu_custom_call" | custom-call | tf_op jit(solution)/shard_map/select_rows/pallas_call | solution.py:180
  1.9 0.5 %collective-permute-start = (bf16[24,1792]{1,0:T(8,128)(2,1)S(1)}, bf16[24,1792]{1,0:T(8,128)(2,1)S(1)}, u32[]{:S(2)}, u32[]{:S(2)}) collective-permute-start(bf16[24,1792]{1,0:T(8,128)(2,1)S(1)} %get-tuple-element.27), channel_id=1, source_target_pairs={{0,8},{8,0},{1,9},{9,1},{2,10},{10,2},{3,11},{11,3},{4,12},{12,4},... | collective-permute-start | bytes 258056 | tf_op jit(solution)/shard_map/ppermute | solution.py:306
  2.4 0.9 %collective-permute-done = bf16[24,1792]{1,0:T(8,128)(2,1)S(1)} collective-permute-done((bf16[24,1792]{1,0:T(8,128)(2,1)S(1)}, bf16[24,1792]{1,0:T(8,128)(2,1)S(1)}, u32[]{:S(2)}, u32[]{:S(2)}) %collective-permute-start) | collective-permute-done | bytes 86048 | tf_op jit(solution)/shard_map/ppermute | solution.py:306
  3.4 5.0 %collective-permute-start.1 = (bf16[48,1792]{1,0:T(8,128)(2,1)S(1)}, bf16[48,1792]{1,0:T(8,128)(2,1)S(1)}, u32[]{:S(2)}, u32[]{:S(2)}) collective-permute-start(bf16[48,1792]{1,0:T(8,128)(2,1)S(1)} %constant_dynamic-update-slice_fusion.refs_0_), channel_id=1, source_target_pairs={{0,6},{1,7},{2,4},{3,5},{4,2},{5,3},{6,0},{7,1},{8,14},{9,15},{10,... | collective-permute-start | bytes 516104 | tf_op jit(solution)/shard_map/ppermute | solution.py:302
  8.4 0.0 collective-permute-start.2
  8.4 1.5 %collective-permute-start.5 = (bf16[48,1792]{1,0:T(8,128)(2,1)S(1)}, bf16[48,1792]{1,0:T(8,128)(2,1)S(1)}, u32[]{:S(2)}, u32[]{:S(2)}) collective-permute-start(bf16[48,1792]{1,0:T(8,128)(2,1)S(1)} %constant_dynamic-update-slice_fusion.refs_0_), channel_id=1, source_target_pairs={{0,1},{1,0},{2,3},{3,2},{4,5},{5,4},{6,7},{7,6},{8,9},{9,8},{10,11... | collective-permute-start | bytes 516104 | tf_op jit(solution)/shard_map/ppermute | solution.py:302
  9.9 2.6 %load_weights.1 = (bf16[7168,256]{1,0:T(8,128)(2,1)S(1)}, bf16[512,1792]{1,0:T(8,128)(2,1)S(1)}) custom-call(bf16[7168,128]{1,0:T(8,128)(2,1)} %gate_hbm.1, bf16[7168,128]{1,0:T(8,128)(2,1)} %up_hbm.1, bf16[128,7168]{1,0:T(8,128)(2,1)} %down_hbm.1), custom_call_target="tpu_custom_call" | custom-call | tf_op jit(solution)/shard_map/load_weights/pallas_call | solution.py:113
  12.5 1.1 %collective-permute-done.1.refs_0_ = bf16[48,1792]{1,0:T(8,128)(2,1)S(1)} collective-permute-done((bf16[48,1792]{1,0:T(8,128)(2,1)S(1)}, bf16[48,1792]{1,0:T(8,128)(2,1)S(1)}, u32[]{:S(2)}, u32[]{:S(2)}) %collective-permute-start.1) | collective-permute-done | bytes 172064 | tf_op jit(solution)/shard_map/ppermute | solution.py:302
  13.6 3.2 %collective-permute-done.2.refs_1_ = bf16[48,1792]{1,0:T(8,128)(2,1)S(1)} collective-permute-done((bf16[48,1792]{1,0:T(8,128)(2,1)S(1)}, bf16[48,1792]{1,0:T(8,128)(2,1)S(1)}, u32[]{:S(2)}, u32[]{:S(2)}) %collective-permute-start.2) | collective-permute-done | bytes 172064 | tf_op jit(solution)/shard_map/ppermute | solution.py:302
  16.8 1.7 %collective-permute-start.3 = (bf16[48,1792]{1,0:T(8,128)(2,1)S(1)}, bf16[48,1792]{1,0:T(8,128)(2,1)S(1)}, u32[]{:S(2)}, u32[]{:S(2)}) collective-permute-start(bf16[48,1792]{1,0:T(8,128)(2,1)S(1)} %get-tuple-element.30.refs_1_), channel_id=1, source_target_pairs={{0,2},{1,3},{2,0},{3,1},{4,6},{5,7},{6,4},{7,5},{8,10},{9,11},{10,... | collective-permute-start | bytes 516104 | tf_op jit(solution)/shard_map/ppermute | solution.py:302
  18.5 1.5 %collective-permute-start.4 = (bf16[48,1792]{1,0:T(8,128)(2,1)S(1)}, bf16[48,1792]{1,0:T(8,128)(2,1)S(1)}, u32[]{:S(2)}, u32[]{:S(2)}) collective-permute-start(bf16[48,1792]{1,0:T(8,128)(2,1)S(1)} %get-tuple-element.30.refs_1_), channel_id=1, source_target_pairs={{0,1},{1,0},{2,3},{3,2},{4,5},{5,4},{6,7},{7,6},{8,9},{9,8},{10,11... | collective-permute-start | bytes 516104 | tf_op jit(solution)/shard_map/ppermute | solution.py:302
  20.0 0.0 collective-permute-done.5.refs_1_
  20.0 0.3 collective-permute-start.10
  20.3 1.4 %experts.4 = (bf16[48,1792]{1,0:T(8,128)(2,1)S(1)}, bf16[48,1792]{1,0:T(8,128)(2,1)S(1)}, bf16[48,1792]{1,0:T(8,128)(2,1)S(1)}) custom-call(bf16[48,1792]{1,0:T(8,128)(2,1)S(1)} %constant_dynamic-update-slice_fusion.refs_0_, bf16[48,1792]{1,0:T(8,128)(2,1)S(1)} %collective-permute-done.5.refs_1_, bf16[48,1792]{1,0:T(8,128)(2,1)S(1)} %get-tuple-element.31.refs_2_, ...), custom_call_target="tpu_custom_call" | custom-call | flops 792723456 | bytes 5505024 | tf_op jit(solution)/shard_map/experts/pallas_call | solution.py:240
  21.7 2.3 %collective-permute-done.3.refs_0_ = bf16[48,1792]{1,0:T(8,128)(2,1)S(1)} collective-permute-done((bf16[48,1792]{1,0:T(8,128)(2,1)S(1)}, bf16[48,1792]{1,0:T(8,128)(2,1)S(1)}, u32[]{:S(2)}, u32[]{:S(2)}) %collective-permute-start.3) | collective-permute-done | bytes 172064 | tf_op jit(solution)/shard_map/ppermute | solution.py:302
  24.0 0.0 collective-permute-done.4.refs_1_
  24.0 1.5 %collective-permute-start.6 = (bf16[48,1792]{1,0:T(8,128)(2,1)S(1)}, bf16[48,1792]{1,0:T(8,128)(2,1)S(1)}, u32[]{:S(2)}, u32[]{:S(2)}) collective-permute-start(bf16[48,1792]{1,0:T(8,128)(2,1)S(1)} %get-tuple-element.36.refs_2_), channel_id=1, source_target_pairs={{0,1},{1,0},{2,3},{3,2},{4,5},{5,4},{6,7},{7,6},{8,9},{9,8},{10,11... | collective-permute-start | bytes 516104 | tf_op jit(solution)/shard_map/ppermute | solution.py:302
  25.5 1.3 %experts.6 = (bf16[48,1792]{1,0:T(8,128)(2,1)S(1)}, bf16[48,1792]{1,0:T(8,128)(2,1)S(1)}, bf16[48,1792]{1,0:T(8,128)(2,1)S(1)}) custom-call(bf16[48,1792]{1,0:T(8,128)(2,1)S(1)} %get-tuple-element.37.refs_0_, bf16[48,1792]{1,0:T(8,128)(2,1)S(1)} %get-tuple-element.30.refs_1_, bf16[48,1792]{1,0:T(8,128)(2,1)S(1)} %get-tuple-element.36.refs_2_, ...), custom_call_target="tpu_custom_call" | custom-call | flops 792723456 | bytes 5505024 | tf_op jit(solution)/shard_map/experts/pallas_call | solution.py:240
  26.9 1.8 %collective-permute-start.7 = (bf16[48,1792]{1,0:T(8,128)(2,1)S(1)}, bf16[48,1792]{1,0:T(8,128)(2,1)S(1)}, u32[]{:S(2)}, u32[]{:S(2)}) collective-permute-start(bf16[48,1792]{1,0:T(8,128)(2,1)S(1)} %get-tuple-element.38), channel_id=1, source_target_pairs={{0,2},{1,3},{2,0},{3,1},{4,6},{5,7},{6,4},{7,5},{8,10},{9,11},{10,... | collective-permute-start | bytes 516104 | tf_op jit(solution)/shard_map/ppermute | solution.py:302
  28.7 0.3 collective-permute-start.13
  29.0 0.0 collective-permute-done.10.refs_0_
  29.0 1.4 %experts.7 = bf16[48,1792]{1,0:T(8,128)(2,1)S(1)} custom-call(bf16[48,1792]{1,0:T(8,128)(2,1)S(1)} %join.13.refs_0_, bf16[7168,256]{1,0:T(8,128)(2,1)S(1)} %get-tuple-element.32.refs_3_.refs_1_, bf16[512,1792]{1,0:T(8,128)(2,1)S(1)} %get-tuple-element.33.refs_4_.refs_2_), custom_call_target="tpu_custom_call" | custom-call | flops 264241152 | bytes 5505024 | tf_op jit(solution)/shard_map/experts/pallas_call | solution.py:240
  30.3 0.6 %collective-permute-start.11 = (bf16[48,1792]{1,0:T(8,128)(2,1)S(1)}, bf16[48,1792]{1,0:T(8,128)(2,1)S(1)}, u32[]{:S(2)}, u32[]{:S(2)}) collective-permute-start(bf16[48,1792]{1,0:T(8,128)(2,1)S(1)} %experts.7), channel_id=1, source_target_pairs={{0,1},{1,0},{2,3},{3,2},{4,5},{5,4},{6,7},{7,6},{8,9},{9,8},{10,11... | collective-permute-start | bytes 516104 | tf_op jit(solution)/shard_map/ppermute | solution.py:302
  30.9 0.0 collective-permute-done.6.refs_0_
  30.9 1.4 %experts.5 = bf16[48,1792]{1,0:T(8,128)(2,1)S(1)} custom-call(bf16[48,1792]{1,0:T(8,128)(2,1)S(1)} %collective-permute-done.6.refs_0_, bf16[7168,256]{1,0:T(8,128)(2,1)S(1)} %get-tuple-element.32.refs_3_.refs_1_, bf16[512,1792]{1,0:T(8,128)(2,1)S(1)} %get-tuple-element.33.refs_4_.refs_2_), custom_call_target="tpu_custom_call" | custom-call | flops 264241152 | bytes 5505024 | tf_op jit(solution)/shard_map/experts/pallas_call | solution.py:240
  32.3 0.8 %collective-permute-done.7 = bf16[48,1792]{1,0:T(8,128)(2,1)S(1)} collective-permute-done((bf16[48,1792]{1,0:T(8,128)(2,1)S(1)}, bf16[48,1792]{1,0:T(8,128)(2,1)S(1)}, u32[]{:S(2)}, u32[]{:S(2)}) %collective-permute-start.7) | collective-permute-done | bytes 172064 | tf_op jit(solution)/shard_map/ppermute | solution.py:302
  33.1 0.8 %collective-permute-start.8 = (bf16[48,1792]{1,0:T(8,128)(2,1)S(1)}, bf16[48,1792]{1,0:T(8,128)(2,1)S(1)}, u32[]{:S(2)}, u32[]{:S(2)}) collective-permute-start(bf16[48,1792]{1,0:T(8,128)(2,1)S(1)} %add_convert_fusion.2), channel_id=1, source_target_pairs={{0,1},{1,0},{2,3},{3,2},{4,5},{5,4},{6,7},{7,6},{8,9},{9,8},{10,11... | collective-permute-start | bytes 516104 | tf_op jit(solution)/shard_map/ppermute | solution.py:302
  33.9 2.4 %collective-permute-done.11 = bf16[48,1792]{1,0:T(8,128)(2,1)S(1)} collective-permute-done((bf16[48,1792]{1,0:T(8,128)(2,1)S(1)}, bf16[48,1792]{1,0:T(8,128)(2,1)S(1)}, u32[]{:S(2)}, u32[]{:S(2)}) %collective-permute-start.11) | collective-permute-done | bytes 172064 | tf_op jit(solution)/shard_map/ppermute | solution.py:302
  36.4 0.0 collective-permute-done.13.refs_0_
  36.4 2.1 %collective-permute-done.8.refs_0_ = bf16[48,1792]{1,0:T(8,128)(2,1)S(1)} collective-permute-done((bf16[48,1792]{1,0:T(8,128)(2,1)S(1)}, bf16[48,1792]{1,0:T(8,128)(2,1)S(1)}, u32[]{:S(2)}, u32[]{:S(2)}) %collective-permute-start.8) | collective-permute-done | bytes 172064 | tf_op jit(solution)/shard_map/ppermute | solution.py:302
  38.6 0.1 add_convert_fusion
  38.6 0.2 collective-permute-start.14
  38.9 1.5 %collective-permute-start.12 = (bf16[48,1792]{1,0:T(8,128)(2,1)S(1)}, bf16[48,1792]{1,0:T(8,128)(2,1)S(1)}, u32[]{:S(2)}, u32[]{:S(2)}) collective-permute-start(bf16[48,1792]{1,0:T(8,128)(2,1)S(1)} %add_convert_fusion.1), channel_id=1, source_target_pairs={{0,2},{1,3},{2,0},{3,1},{4,6},{5,7},{6,4},{7,5},{8,10},{9,11},{10,... | collective-permute-start | bytes 516104 | tf_op jit(solution)/shard_map/ppermute | solution.py:302
  40.4 1.3 %collective-permute-start.9 = (bf16[48,1792]{1,0:T(8,128)(2,1)S(1)}, bf16[48,1792]{1,0:T(8,128)(2,1)S(1)}, u32[]{:S(2)}, u32[]{:S(2)}) collective-permute-start(bf16[48,1792]{1,0:T(8,128)(2,1)S(1)} %get-tuple-element.40), channel_id=1, source_target_pairs={{0,1},{1,0},{2,3},{3,2},{4,5},{5,4},{6,7},{7,6},{8,9},{9,8},{10,11... | collective-permute-start | bytes 516104 | tf_op jit(solution)/shard_map/ppermute | solution.py:302
  41.7 5.2 %collective-permute-done.14.refs_0_ = bf16[48,1792]{1,0:T(8,128)(2,1)S(1)} collective-permute-done((bf16[48,1792]{1,0:T(8,128)(2,1)S(1)}, bf16[48,1792]{1,0:T(8,128)(2,1)S(1)}, u32[]{:S(2)}, u32[]{:S(2)}) %collective-permute-start.14) | collective-permute-done | bytes 172064 | tf_op jit(solution)/shard_map/ppermute | solution.py:302
  46.9 0.0 collective-permute-done.12.refs_2_
  46.9 0.0 collective-permute-done.9.refs_1_
  46.9 0.1 collective-permute-start.15
  47.0 1.3 %collective-permute-done.15.refs_4_ = bf16[24,1792]{1,0:T(8,128)(2,1)S(1)} collective-permute-done((bf16[24,1792]{1,0:T(8,128)(2,1)S(1)}, bf16[24,1792]{1,0:T(8,128)(2,1)S(1)}, u32[]{:S(2)}, u32[]{:S(2)}) %collective-permute-start.15) | collective-permute-done | bytes 86048 | tf_op jit(solution)/shard_map/ppermute | solution.py:306
  48.3 1.6 %combine.1 = bf16[128,7168]{1,0:T(8,128)(2,1)} custom-call(bf16[48,1792]{1,0:T(8,128)(2,1)S(1)} %get-tuple-element.35.refs_0_, bf16[48,1792]{1,0:T(8,128)(2,1)S(1)} %collective-permute-done.9.refs_1_, bf16[48,1792]{1,0:T(8,128)(2,1)S(1)} %collective-permute-done.12.refs_2_, bf16[48,1792]{1,0:T(8,128)(2,1)S(1)} %join.15.refs_3_, ...), custom_call_target="tpu_custom_call" | custom-call | tf_op jit(solution)/shard_map/combine/pallas_call | solution.py:287
  (13 shorter events, 0.2 us)
Async XLA Ops:
  1.9 1.4 %collective-permute-start = (bf16[24,1792]{1,0:T(8,128)(2,1)S(1)}, bf16[24,1792]{1,0:T(8,128)(2,1)S(1)}, u32[]{:S(2)}, u32[]{:S(2)}) collective-permute-start(bf16[24,1792]{1,0:T(8,128)(2,1)S(1)} %get-tuple-element.27), channel_id=1, source_target_pairs={{0,8},{8,0},{1,9},{9,1},{2,10},{10,2},{3,11},{11,3},{4,12},{12,4},... | collective-permute-start | bytes 258056 | tf_op jit(solution)/shard_map/ppermute | solution.py:306
  3.4 10.2 %collective-permute-start.1 = (bf16[48,1792]{1,0:T(8,128)(2,1)S(1)}, bf16[48,1792]{1,0:T(8,128)(2,1)S(1)}, u32[]{:S(2)}, u32[]{:S(2)}) collective-permute-start(bf16[48,1792]{1,0:T(8,128)(2,1)S(1)} %constant_dynamic-update-slice_fusion.refs_0_), channel_id=1, source_target_pairs={{0,6},{1,7},{2,4},{3,5},{4,2},{5,3},{6,0},{7,1},{8,14},{9,15},{10,... | collective-permute-start | bytes 516104 | tf_op jit(solution)/shard_map/ppermute | solution.py:302
  8.4 8.4 %collective-permute-start.2 = (bf16[48,1792]{1,0:T(8,128)(2,1)S(1)}, bf16[48,1792]{1,0:T(8,128)(2,1)S(1)}, u32[]{:S(2)}, u32[]{:S(2)}) collective-permute-start(bf16[48,1792]{1,0:T(8,128)(2,1)S(1)} %constant_dynamic-update-slice_fusion.refs_0_), channel_id=1, source_target_pairs={{0,2},{1,3},{2,0},{3,1},{4,6},{5,7},{6,4},{7,5},{8,10},{9,11},{10,... | collective-permute-start | bytes 516104 | tf_op jit(solution)/shard_map/ppermute | solution.py:302
  8.4 11.6 %collective-permute-start.5 = (bf16[48,1792]{1,0:T(8,128)(2,1)S(1)}, bf16[48,1792]{1,0:T(8,128)(2,1)S(1)}, u32[]{:S(2)}, u32[]{:S(2)}) collective-permute-start(bf16[48,1792]{1,0:T(8,128)(2,1)S(1)} %constant_dynamic-update-slice_fusion.refs_0_), channel_id=1, source_target_pairs={{0,1},{1,0},{2,3},{3,2},{4,5},{5,4},{6,7},{7,6},{8,9},{9,8},{10,11... | collective-permute-start | bytes 516104 | tf_op jit(solution)/shard_map/ppermute | solution.py:302
  16.8 7.2 %collective-permute-start.3 = (bf16[48,1792]{1,0:T(8,128)(2,1)S(1)}, bf16[48,1792]{1,0:T(8,128)(2,1)S(1)}, u32[]{:S(2)}, u32[]{:S(2)}) collective-permute-start(bf16[48,1792]{1,0:T(8,128)(2,1)S(1)} %get-tuple-element.30.refs_1_), channel_id=1, source_target_pairs={{0,2},{1,3},{2,0},{3,1},{4,6},{5,7},{6,4},{7,5},{8,10},{9,11},{10,... | collective-permute-start | bytes 516104 | tf_op jit(solution)/shard_map/ppermute | solution.py:302
  18.5 5.6 %collective-permute-start.4 = (bf16[48,1792]{1,0:T(8,128)(2,1)S(1)}, bf16[48,1792]{1,0:T(8,128)(2,1)S(1)}, u32[]{:S(2)}, u32[]{:S(2)}) collective-permute-start(bf16[48,1792]{1,0:T(8,128)(2,1)S(1)} %get-tuple-element.30.refs_1_), channel_id=1, source_target_pairs={{0,1},{1,0},{2,3},{3,2},{4,5},{5,4},{6,7},{7,6},{8,9},{9,8},{10,11... | collective-permute-start | bytes 516104 | tf_op jit(solution)/shard_map/ppermute | solution.py:302
  20.0 9.0 %collective-permute-start.10 = (bf16[48,1792]{1,0:T(8,128)(2,1)S(1)}, bf16[48,1792]{1,0:T(8,128)(2,1)S(1)}, u32[]{:S(2)}, u32[]{:S(2)}) collective-permute-start(bf16[48,1792]{1,0:T(8,128)(2,1)S(1)} %collective-permute-done.5.refs_1_), channel_id=1, source_target_pairs={{0,2},{1,3},{2,0},{3,1},{4,6},{5,7},{6,4},{7,5},{8,10},{9,11},{10,... | collective-permute-start | bytes 516104 | tf_op jit(solution)/shard_map/ppermute | solution.py:302
  24.0 6.9 %collective-permute-start.6 = (bf16[48,1792]{1,0:T(8,128)(2,1)S(1)}, bf16[48,1792]{1,0:T(8,128)(2,1)S(1)}, u32[]{:S(2)}, u32[]{:S(2)}) collective-permute-start(bf16[48,1792]{1,0:T(8,128)(2,1)S(1)} %get-tuple-element.36.refs_2_), channel_id=1, source_target_pairs={{0,1},{1,0},{2,3},{3,2},{4,5},{5,4},{6,7},{7,6},{8,9},{9,8},{10,11... | collective-permute-start | bytes 516104 | tf_op jit(solution)/shard_map/ppermute | solution.py:302
  26.9 6.1 %collective-permute-start.7 = (bf16[48,1792]{1,0:T(8,128)(2,1)S(1)}, bf16[48,1792]{1,0:T(8,128)(2,1)S(1)}, u32[]{:S(2)}, u32[]{:S(2)}) collective-permute-start(bf16[48,1792]{1,0:T(8,128)(2,1)S(1)} %get-tuple-element.38), channel_id=1, source_target_pairs={{0,2},{1,3},{2,0},{3,1},{4,6},{5,7},{6,4},{7,5},{8,10},{9,11},{10,... | collective-permute-start | bytes 516104 | tf_op jit(solution)/shard_map/ppermute | solution.py:302
  28.7 7.7 %collective-permute-start.13 = (bf16[48,1792]{1,0:T(8,128)(2,1)S(1)}, bf16[48,1792]{1,0:T(8,128)(2,1)S(1)}, u32[]{:S(2)}, u32[]{:S(2)}) collective-permute-start(bf16[48,1792]{1,0:T(8,128)(2,1)S(1)} %get-tuple-element.43), channel_id=1, source_target_pairs={{0,2},{1,3},{2,0},{3,1},{4,6},{5,7},{6,4},{7,5},{8,10},{9,11},{10,... | collective-permute-start | bytes 516104 | tf_op jit(solution)/shard_map/ppermute | solution.py:302
  30.3 6.0 %collective-permute-start.11 = (bf16[48,1792]{1,0:T(8,128)(2,1)S(1)}, bf16[48,1792]{1,0:T(8,128)(2,1)S(1)}, u32[]{:S(2)}, u32[]{:S(2)}) collective-permute-start(bf16[48,1792]{1,0:T(8,128)(2,1)S(1)} %experts.7), channel_id=1, source_target_pairs={{0,1},{1,0},{2,3},{3,2},{4,5},{5,4},{6,7},{7,6},{8,9},{9,8},{10,11... | collective-permute-start | bytes 516104 | tf_op jit(solution)/shard_map/ppermute | solution.py:302
  33.1 5.5 %collective-permute-start.8 = (bf16[48,1792]{1,0:T(8,128)(2,1)S(1)}, bf16[48,1792]{1,0:T(8,128)(2,1)S(1)}, u32[]{:S(2)}, u32[]{:S(2)}) collective-permute-start(bf16[48,1792]{1,0:T(8,128)(2,1)S(1)} %add_convert_fusion.2), channel_id=1, source_target_pairs={{0,1},{1,0},{2,3},{3,2},{4,5},{5,4},{6,7},{7,6},{8,9},{9,8},{10,11... | collective-permute-start | bytes 516104 | tf_op jit(solution)/shard_map/ppermute | solution.py:302
  38.6 8.3 %collective-permute-start.14 = (bf16[48,1792]{1,0:T(8,128)(2,1)S(1)}, bf16[48,1792]{1,0:T(8,128)(2,1)S(1)}, u32[]{:S(2)}, u32[]{:S(2)}) collective-permute-start(bf16[48,1792]{1,0:T(8,128)(2,1)S(1)} %add_convert_fusion), channel_id=1, source_target_pairs={{0,4},{1,5},{2,6},{3,7},{4,0},{5,1},{6,2},{7,3},{8,12},{9,13},{10,... | collective-permute-start | bytes 516104 | tf_op jit(solution)/shard_map/ppermute | solution.py:302
  38.9 8.0 %collective-permute-start.12 = (bf16[48,1792]{1,0:T(8,128)(2,1)S(1)}, bf16[48,1792]{1,0:T(8,128)(2,1)S(1)}, u32[]{:S(2)}, u32[]{:S(2)}) collective-permute-start(bf16[48,1792]{1,0:T(8,128)(2,1)S(1)} %add_convert_fusion.1), channel_id=1, source_target_pairs={{0,2},{1,3},{2,0},{3,1},{4,6},{5,7},{6,4},{7,5},{8,10},{9,11},{10,... | collective-permute-start | bytes 516104 | tf_op jit(solution)/shard_map/ppermute | solution.py:302
  40.4 6.5 %collective-permute-start.9 = (bf16[48,1792]{1,0:T(8,128)(2,1)S(1)}, bf16[48,1792]{1,0:T(8,128)(2,1)S(1)}, u32[]{:S(2)}, u32[]{:S(2)}) collective-permute-start(bf16[48,1792]{1,0:T(8,128)(2,1)S(1)} %get-tuple-element.40), channel_id=1, source_target_pairs={{0,1},{1,0},{2,3},{3,2},{4,5},{5,4},{6,7},{7,6},{8,9},{9,8},{10,11... | collective-permute-start | bytes 516104 | tf_op jit(solution)/shard_map/ppermute | solution.py:302
  46.9 1.3 %collective-permute-start.15 = (bf16[24,1792]{1,0:T(8,128)(2,1)S(1)}, bf16[24,1792]{1,0:T(8,128)(2,1)S(1)}, u32[]{:S(2)}, u32[]{:S(2)}) collective-permute-start(bf16[24,1792]{1,0:T(8,128)(2,1)S(1)} %add_convert_fusion.3), channel_id=1, source_target_pairs={{0,8},{8,0},{1,9},{9,1},{2,10},{10,2},{3,11},{11,3},{4,12},{12,4},... | collective-permute-start | bytes 258056 | tf_op jit(solution)/shard_map/ppermute | solution.py:306
